TPU v7x, 32 devices: a whole 2x2x4 slice. The times are simulated.
32 devices in a mesh: fsdp: 8 (over z, x), context: 2 (over y), tensor: 2 (over core).
Axes of the slice: x: 2, y: 2, z: 4, core: 2. Of those that a mesh axis runs over, the one named last changes fastest.
Arguments:
- tokens: bfloat16 [8, 2048, 768], P('fsdp', 'context'), may hold values from -6 to 6
- pack_lengths: int32 [8, 3], P('fsdp'), may hold values from 1 to 1792, as said below
- cotangent: bfloat16 [8, 2048, 768], P('fsdp', 'context'), may hold values from -6 to 6
- projection: bfloat16 [768, 3, 768], P('fsdp', None, 'tensor'), may hold values from -0.21875 to 0.21875
- projection_bias: bfloat16 [3, 768], P(None, ('tensor', 'fsdp')), may hold values from -3 to 3
- outgoing: bfloat16 [768, 768], P('tensor', 'fsdp'), may hold values from -0.875 to 0.875
- outgoing_bias: bfloat16 [768], P('fsdp'), may hold values from -3 to 3
- widening: bfloat16 [768, 3072], P('fsdp', 'tensor'), may hold values from -0.21875 to 0.21875
- widening_bias: bfloat16 [3072], P(('tensor', 'fsdp')), may hold values from -3 to 3
- narrowing: bfloat16 [3072, 768], P('tensor', 'fsdp'), may hold values from -0.109375 to 0.109375
- narrowing_bias: bfloat16 [768], P('fsdp'), may hold values from -3 to 3
- first_gain: bfloat16 [768], P('fsdp'), may hold values from 0.099609375 to 1.8984375
- first_shift: bfloat16 [768], P('fsdp'), may hold values from -3 to 3
- second_gain: bfloat16 [768], P('fsdp'), may hold values from 0.099609375 to 1.8984375
- second_shift: bfloat16 [768], P('fsdp'), may hold values from -3 to 3
Outputs:
- mixed: bfloat16 [8, 2048, 768], P('fsdp', 'context')
- tokens_gradient: float32 [8, 2048, 768], P('fsdp', 'context')
- projection_gradient: float32 [768, 3, 768], P('fsdp', None, 'tensor')
- projection_bias_gradient: float32 [3, 768], P(None, ('tensor', 'fsdp'))
- outgoing_gradient: float32 [768, 768], P('tensor', 'fsdp')
- outgoing_bias_gradient: float32 [768], P('fsdp')
- widening_gradient: float32 [768, 3072], P('fsdp', 'tensor')
- widening_bias_gradient: float32 [3072], P(('tensor', 'fsdp'))
- narrowing_gradient: float32 [3072, 768], P('tensor', 'fsdp')
- narrowing_bias_gradient: float32 [768], P('fsdp')
- first_gain_gradient: float32 [768], P('fsdp')
- first_shift_gradient: float32 [768], P('fsdp')
- second_gain_gradient: float32 [768], P('fsdp')
- second_shift_gradient: float32 [768], P('fsdp')
Inputs may be any that keep to these rules, and one draw needn't show every extreme that they name: `pack_lengths`: each row lists the lengths of the 3 sequences of one pack in the order in which they lie from the pack's first token, each starting at a multiple of 128; with every length rounded up to a multiple of 128 they fit into the pack's 2048 tokens, and one of them starts within the first 1024 tokens and ends within the last 1024 tokens.
All inputs are finite; a program needn't handle non-finite values.
Results may differ from a plain program's by a relative error of at most 0.028.
Values may be sent and summed in bfloat16 or wider, within the bound.
No kernel may reach another device: no remote copies, remote signals or barrier semaphores. Data moves between devices by JAX's collectives and lax.ppermute only.
A program may use at most 256 MiB of HBM per device.

v0:
```python
import jax
import jax.numpy as jnp
from jax import lax
from jax.sharding import PartitionSpec as P

HEAD_DIM = 64
ROTARY = 16
TILE = 128
SEQS = 3


epsilon = 1e-05


def layout(lengths, index):
    padded = (lengths + TILE - 1) // TILE * TILE
    finish = jnp.cumsum(padded)
    before = (index[:, None] >= finish[None, :]).astype(jnp.int32)
    number = jnp.sum(before, axis=1)
    start = jnp.sum(before * padded[None, :], axis=1)
    position = index - start
    labels = jnp.arange(SEQS, dtype=jnp.int32)
    length = jnp.sum(jnp.where(number[:, None] == labels[None, :], lengths[None, :], 0), axis=1)
    return (number, position, position < length)


def turn_tables(position):
    frequency = 10000.0 ** (-jnp.arange(0, ROTARY, 2, dtype=jnp.float32) / ROTARY)
    angles = position.astype(jnp.float32)[:, None] * frequency[None, :]
    angles = jnp.concatenate([angles, angles], axis=1)
    return (jnp.cos(angles)[:, None, :], jnp.sin(angles)[:, None, :])


def rotate(field, cosine, sine):
    half = ROTARY // 2
    front = field[..., :ROTARY]
    turned = jnp.concatenate([-front[..., half:], front[..., :half]], axis=-1)
    return jnp.concatenate([front * cosine + turned * sine, field[..., ROTARY:]], axis=-1)


def rotate_back(slope, cosine, sine):
    half = ROTARY // 2
    front = slope[..., :ROTARY]
    scaled = front * sine
    turned = jnp.concatenate([scaled[..., half:], -scaled[..., :half]], axis=-1)
    return jnp.concatenate([front * cosine + turned, slope[..., ROTARY:]], axis=-1)


def normalize(values, gain, shift):
    average = jnp.mean(values, axis=-1, keepdims=True)
    centered = values - average
    spread = jnp.mean(centered * centered, axis=-1, keepdims=True)
    factor = lax.rsqrt(spread + epsilon)
    unit = centered * factor
    return (unit, factor, unit * gain + shift)


def normalize_back(slope, unit, factor, gain):
    scaled = slope * gain
    return factor * (
        scaled
        - jnp.mean(scaled, axis=-1, keepdims=True)
        - unit * jnp.mean(scaled * unit, axis=-1, keepdims=True)
    )


def gelu_slope(values):
    return (
        0.5 * (1.0 + lax.erf(values * 0.7071067811865476))
        + values * jnp.exp(-0.5 * values * values) * 0.3989422804014327
    )


def allowed_mask(
    query_number, query_position, query_index, key_number, key_position, key_valid, key_index
):
    same = (
        (query_number[:, None] == key_number[None, :])
        & (key_position[None, :] <= query_position[:, None])
        & key_valid[None, :]
    )
    return same | (query_index[:, None] == key_index[None, :])


def body(
    tokens,
    pack_lengths,
    cotangent,
    projection,
    projection_bias,
    outgoing,
    outgoing_bias,
    widening,
    widening_bias,
    narrowing,
    narrowing_bias,
    first_gain,
    first_shift,
    second_gain,
    second_shift,
):
    packs, local, width = tokens.shape
    group = local * lax.axis_size("context")
    rows = packs * local
    (
        projection,
        projection_bias,
        outgoing,
        outgoing_bias,
        widening,
        widening_bias,
        narrowing,
        narrowing_bias,
        first_gain,
        first_shift,
        second_gain,
        second_shift,
    ) = (
        lax.all_gather(projection, "fsdp", axis=0, tiled=True),
        lax.all_gather(projection_bias, "fsdp", axis=1, tiled=True),
        lax.all_gather(outgoing, "fsdp", axis=1, tiled=True),
        lax.all_gather(outgoing_bias, "fsdp", axis=0, tiled=True),
        lax.all_gather(widening, "fsdp", axis=0, tiled=True),
        lax.all_gather(widening_bias, "fsdp", axis=0, tiled=True),
        lax.all_gather(narrowing, "fsdp", axis=1, tiled=True),
        lax.all_gather(narrowing_bias, "fsdp", axis=0, tiled=True),
        lax.all_gather(first_gain, "fsdp", axis=0, tiled=True),
        lax.all_gather(first_shift, "fsdp", axis=0, tiled=True),
        lax.all_gather(second_gain, "fsdp", axis=0, tiled=True),
        lax.all_gather(second_shift, "fsdp", axis=0, tiled=True),
    )
    inner = projection.shape[2]
    heads_here = inner // HEAD_DIM
    score_scale = HEAD_DIM ** (-0.5)
    gain_one = first_gain.astype(jnp.float32)
    gain_two = second_gain.astype(jnp.float32)
    source = tokens.reshape(rows, width).astype(jnp.float32)
    unit_one, factor_one, normed_one = normalize(source, gain_one, first_shift.astype(jnp.float32))
    unit_two, factor_two, normed_two = normalize(source, gain_two, second_shift.astype(jnp.float32))
    normed_one = normed_one.astype(jnp.bfloat16)
    normed_two = normed_two.astype(jnp.bfloat16)
    projected = jnp.dot(
        normed_one, projection.reshape(width, 3 * inner), preferred_element_type=jnp.float32
    ).reshape(rows, 3, inner)
    projected = projected + projection_bias.astype(jnp.float32)[None]
    query_index = lax.axis_index("context") * local + jnp.arange(local, dtype=jnp.int32)
    key_index = jnp.arange(group, dtype=jnp.int32)
    query_number, query_position, query_valid = jax.vmap(layout, in_axes=(0, None))(
        pack_lengths, query_index
    )
    key_number, key_position, key_valid = jax.vmap(layout, in_axes=(0, None))(
        pack_lengths, key_index
    )
    cosine, sine = turn_tables(query_position.reshape(rows))
    shaped = projected.reshape(rows, 3, heads_here, HEAD_DIM)
    queries = rotate(shaped[:, 0], cosine, sine).astype(jnp.bfloat16)
    keys = rotate(shaped[:, 1], cosine, sine).astype(jnp.bfloat16)
    values = shaped[:, 2].astype(jnp.bfloat16)
    all_keys, all_values = (
        lax.all_gather(keys.reshape(packs, local, inner), "context", axis=1, tiled=True),
        lax.all_gather(values.reshape(packs, local, inner), "context", axis=1, tiled=True),
    )
    query_packs = queries.reshape(packs, local, heads_here, HEAD_DIM)

    def scores_for(pack):
        key_block = all_keys[pack].reshape(group, heads_here, HEAD_DIM)
        raw = (
            jnp.einsum(
                "qhd,khd->hqk", query_packs[pack], key_block, preferred_element_type=jnp.float32
            )
            * score_scale
        )
        allowed = allowed_mask(
            query_number[pack],
            query_position[pack],
            query_index,
            key_number[pack],
            key_position[pack],
            key_valid[pack],
            key_index,
        )
        return jnp.where(allowed[None], raw, -1e30)

    pack = 0
    scores = scores_for(pack)
    top = jnp.max(scores, axis=-1, keepdims=True)
    total = jnp.log(jnp.sum(jnp.exp(scores - top), axis=-1, keepdims=True)) + top
    weights = jnp.exp(scores - total).astype(jnp.bfloat16)
    value_block = all_values[pack].reshape(group, heads_here, HEAD_DIM)
    head_blocks = [
        jnp.einsum("hqk,khd->qhd", weights, value_block, preferred_element_type=jnp.float32)
    ]
    totals = [total]
    mixed_heads = jnp.stack(head_blocks).reshape(rows, inner).astype(jnp.bfloat16)
    hidden = jnp.dot(
        normed_two, widening, preferred_element_type=jnp.float32
    ) + widening_bias.astype(jnp.float32)
    active = jax.nn.gelu(hidden, approximate=False).astype(jnp.bfloat16)
    attention_part = jnp.dot(mixed_heads, outgoing, preferred_element_type=jnp.float32)
    feed_part = jnp.dot(active, narrowing, preferred_element_type=jnp.float32)
    biases = outgoing_bias.astype(jnp.float32) + narrowing_bias.astype(jnp.float32)
    attention_sum, feed_sum = (
        lax.psum(attention_part.astype(jnp.bfloat16), "tensor").astype(jnp.float32),
        lax.psum(feed_part.astype(jnp.bfloat16), "tensor").astype(jnp.float32),
    )
    result = source + attention_sum + feed_sum + biases
    mixed = result.astype(jnp.bfloat16).reshape(packs, local, width)
    slope_out = cotangent.reshape(rows, width)
    slope_float = slope_out.astype(jnp.float32)
    outgoing_bias_slope = jnp.sum(slope_float, axis=0)
    outgoing_slope = jnp.einsum(
        "rf,rd->fd", mixed_heads, slope_out, preferred_element_type=jnp.float32
    )
    narrowing_slope = jnp.einsum("rf,rd->fd", active, slope_out, preferred_element_type=jnp.float32)
    heads_slope = jnp.einsum(
        "rd,fd->rf", slope_out, outgoing, preferred_element_type=jnp.float32
    ).astype(jnp.bfloat16)
    hidden_slope = (
        jnp.einsum("rd,fd->rf", slope_out, narrowing, preferred_element_type=jnp.float32)
        * gelu_slope(hidden)
    ).astype(jnp.bfloat16)
    widening_slope = jnp.einsum(
        "rd,rf->df", normed_two, hidden_slope, preferred_element_type=jnp.float32
    )
    widening_bias_slope = jnp.sum(hidden_slope.astype(jnp.float32), axis=0)
    second_back = jnp.einsum(
        "rf,df->rd", hidden_slope, widening, preferred_element_type=jnp.float32
    )
    heads_slope_packs = heads_slope.reshape(packs, local, heads_here, HEAD_DIM)
    balances = []
    pack = 0
    scores = scores_for(pack)
    probs = jnp.exp(scores - totals[pack])
    key_block = all_keys[pack].reshape(group, heads_here, HEAD_DIM)
    value_block = all_values[pack].reshape(group, heads_here, HEAD_DIM)
    outer = heads_slope_packs[pack]
    probs_slope = jnp.einsum("qhd,khd->hqk", outer, value_block, preferred_element_type=jnp.float32)
    balance = jnp.sum(probs * probs_slope, axis=-1, keepdims=True)
    balances.append(balance)
    score_slope = (probs * (probs_slope - balance)).astype(jnp.bfloat16)
    query_slopes = [
        jnp.einsum("hqk,khd->qhd", score_slope, key_block, preferred_element_type=jnp.float32)
        * score_scale
    ]
    weights = probs.astype(jnp.bfloat16)
    key_slopes = [
        jnp.einsum(
            "hqk,qhd->khd", score_slope, query_packs[pack], preferred_element_type=jnp.float32
        )
        * score_scale
    ]
    value_slopes = [jnp.einsum("hqk,qhd->khd", weights, outer, preferred_element_type=jnp.float32)]
    key_total, value_total = (
        lax.psum_scatter(
            jnp.stack(key_slopes).reshape(packs, group, inner).astype(jnp.bfloat16),
            "context",
            scatter_dimension=1,
            tiled=True,
        ).astype(jnp.float32),
        lax.psum_scatter(
            jnp.stack(value_slopes).reshape(packs, group, inner).astype(jnp.bfloat16),
            "context",
            scatter_dimension=1,
            tiled=True,
        ).astype(jnp.float32),
    )
    query_back = rotate_back(
        jnp.stack(query_slopes).reshape(rows, heads_here, HEAD_DIM), cosine, sine
    )
    key_back = rotate_back(key_total.reshape(rows, heads_here, HEAD_DIM), cosine, sine)
    projected_slope = jnp.stack(
        [
            query_back.reshape(rows, inner),
            key_back.reshape(rows, inner),
            value_total.reshape(rows, inner),
        ],
        axis=1,
    ).astype(jnp.bfloat16)
    projection_slope = jnp.einsum(
        "rd,rcf->dcf", normed_one, projected_slope, preferred_element_type=jnp.float32
    )
    projection_bias_slope = jnp.sum(projected_slope.astype(jnp.float32), axis=0)
    first_back = jnp.einsum(
        "rcf,dcf->rd", projected_slope, projection, preferred_element_type=jnp.float32
    )
    first_total, second_total = (
        lax.psum(first_back.astype(jnp.bfloat16), "tensor").astype(jnp.float32),
        lax.psum(second_back.astype(jnp.bfloat16), "tensor").astype(jnp.float32),
    )
    first_gain_slope = jnp.sum(first_total * unit_one, axis=0)
    first_shift_slope = jnp.sum(first_total, axis=0)
    second_gain_slope = jnp.sum(second_total * unit_two, axis=0)
    second_shift_slope = jnp.sum(second_total, axis=0)
    tokens_gradient = (
        slope_float
        + normalize_back(first_total, unit_one, factor_one, gain_one)
        + normalize_back(second_total, unit_two, factor_two, gain_two)
    )
    tokens_gradient = tokens_gradient.reshape(packs, local, width)
    owned = (
        lax.psum_scatter(
            projection_slope.astype(jnp.bfloat16), "fsdp", scatter_dimension=0, tiled=True
        ).astype(jnp.float32),
        lax.psum_scatter(
            projection_bias_slope.astype(jnp.bfloat16), "fsdp", scatter_dimension=1, tiled=True
        ).astype(jnp.float32),
        lax.psum_scatter(
            outgoing_slope.astype(jnp.bfloat16), "fsdp", scatter_dimension=1, tiled=True
        ).astype(jnp.float32),
        lax.psum_scatter(
            outgoing_bias_slope.astype(jnp.bfloat16), "fsdp", scatter_dimension=0, tiled=True
        ).astype(jnp.float32),
        lax.psum_scatter(
            widening_slope.astype(jnp.bfloat16), "fsdp", scatter_dimension=0, tiled=True
        ).astype(jnp.float32),
        lax.psum_scatter(
            widening_bias_slope.astype(jnp.bfloat16), "fsdp", scatter_dimension=0, tiled=True
        ).astype(jnp.float32),
        lax.psum_scatter(
            narrowing_slope.astype(jnp.bfloat16), "fsdp", scatter_dimension=1, tiled=True
        ).astype(jnp.float32),
        lax.psum_scatter(
            outgoing_bias_slope.astype(jnp.bfloat16), "fsdp", scatter_dimension=0, tiled=True
        ).astype(jnp.float32),
        lax.psum_scatter(
            first_gain_slope.astype(jnp.bfloat16), "fsdp", scatter_dimension=0, tiled=True
        ).astype(jnp.float32),
        lax.psum_scatter(
            first_shift_slope.astype(jnp.bfloat16), "fsdp", scatter_dimension=0, tiled=True
        ).astype(jnp.float32),
        lax.psum_scatter(
            second_gain_slope.astype(jnp.bfloat16), "fsdp", scatter_dimension=0, tiled=True
        ).astype(jnp.float32),
        lax.psum_scatter(
            second_shift_slope.astype(jnp.bfloat16), "fsdp", scatter_dimension=0, tiled=True
        ).astype(jnp.float32),
    )
    final = (
        lax.psum(owned[0].astype(jnp.bfloat16), "context").astype(jnp.float32),
        lax.psum(owned[1].astype(jnp.bfloat16), "context").astype(jnp.float32),
        lax.psum(owned[2].astype(jnp.bfloat16), "context").astype(jnp.float32),
        lax.psum(owned[3].astype(jnp.bfloat16), "context").astype(jnp.float32),
        lax.psum(owned[4].astype(jnp.bfloat16), "context").astype(jnp.float32),
        lax.psum(owned[5].astype(jnp.bfloat16), "context").astype(jnp.float32),
        lax.psum(owned[6].astype(jnp.bfloat16), "context").astype(jnp.float32),
        lax.psum(owned[7].astype(jnp.bfloat16), "context").astype(jnp.float32),
        lax.psum(owned[8].astype(jnp.bfloat16), "context").astype(jnp.float32),
        lax.psum(owned[9].astype(jnp.bfloat16), "context").astype(jnp.float32),
        lax.psum(owned[10].astype(jnp.bfloat16), "context").astype(jnp.float32),
        lax.psum(owned[11].astype(jnp.bfloat16), "context").astype(jnp.float32),
    )
    return (mixed, tokens_gradient) + tuple(final)


def solution(mesh):
    return jax.shard_map(
        body,
        mesh=mesh,
        in_specs=(
            P("fsdp", "context", None),
            P("fsdp", None),
            P("fsdp", "context", None),
            P("fsdp", None, "tensor"),
            P(None, ("tensor", "fsdp")),
            P("tensor", "fsdp"),
            P("fsdp"),
            P("fsdp", "tensor"),
            P(("tensor", "fsdp")),
            P("tensor", "fsdp"),
            P("fsdp"),
            P("fsdp"),
            P("fsdp"),
            P("fsdp"),
            P("fsdp"),
        ),
        out_specs=(
            P("fsdp", "context", None),
            P("fsdp", "context", None),
            P("fsdp", None, "tensor"),
            P(None, ("tensor", "fsdp")),
            P("tensor", "fsdp"),
            P("fsdp"),
            P("fsdp", "tensor"),
            P(("tensor", "fsdp")),
            P("tensor", "fsdp"),
            P("fsdp"),
            P("fsdp"),
            P("fsdp"),
            P("fsdp"),
            P("fsdp"),
        ),
        check_vma=False,
    )
```

profile of v0, /device:TPU:0, one launch (start us, length us, event | category | flops | bytes accessed | tf_op | source)
XLA Modules:
  0.0 804.5 jit_solution(9674731823006236743)
XLA Ops:
  14.8 39.1 %all-reduce.14 = (bf16[768]{0:T(1024)(128)(2,1)S(1)}, bf16[768]{0:T(1024)(128)(2,1)}, bf16[1536]{0:T(1024)(128)(2,1)S(1)}, bf16[768]{0:T(1024)(128)(2,1)S(1)}, bf16[768]{0:T(1024)(128)(2,1)S(1)}) all-reduce(bf16[768]{0:T(1024)(128)(2,1)S(1)} %dynamic-update-slice.3, ...), channel_id=1, replica_groups=mesh['fsdp'=8,'context'=2,'tensor'=2] {'fsdp'}, use_global_device_ids=true, to_apply=%add.3 | all-reduce | flops 4608 | bytes 18432
  54.0 16.8 %all-gather = bf16[8,48,3]{1,2,0:T(4,128)(2,1)S(1)} all-gather(bf16[1,48,3]{1,2,0:T(4,128)(2,1)} %bitcast.199), channel_id=1, replica_groups=mesh['fsdp'=8,'context'=2,'tensor'=2] {'fsdp'}, dimensions={0}, use_global_device_ids=true | all-gather | bytes 2592 | tf_op jit(solution)/shard_map/all_gather | solution.py:120
  72.7 1.7 convert_reduce_fusion
  75.1 2.6 copy.51
  77.8 2.2 broadcast_add_fusion
  80.4 1.7 copy-done.7
  84.3 2.4 slice.138
  88.3 31.6 %all_gather.48 = bf16[384,768]{0,1:T(8,128)(2,1)S(1)} all-gather(bf16[384,96]{0,1:T(8,128)(2,1)S(1)} %copy-done.21), channel_id=1, replica_groups=mesh['fsdp'=8,'context'=2,'tensor'=2] {'fsdp'}, dimensions={1}, use_global_device_ids=true | all-gather | bytes 663552 | tf_op jit(solution)/shard_map/all_gather | solution.py:121
  120.7 3.7 fusion.2
  125.9 21.9 %fusion = (f32[6,1024]{1,0:T(8,128)S(1)}, f32[6,1024,2048]{2,1,0:T(8,128)}) fusion(pred[1024,2048]{1,0:T(8,128)(4,1)S(1)} %fusion.2, bf16[2048,6,64]{0,2,1:T(8,128)(2,1)} %bitcast.183, bf16[1024,6,48]{0,2,1:T(8,128)(2,1)S(1)} %slice.141, bf16[1024,6,16]{0,2,1:T(8,128)(2,1)} %get-tuple-element.68), kind=kOutput, calls=%fused_computation.5 | convolution fusion | flops 1649928192 | bytes 54812672 | tf_op jit(solution)/shard_map/qhd,khd->hqk/dot_general | solution.py:168
  147.8 23.7 %exponential_reduce_fusion = f32[6,1024]{1,0:T(8,128)} fusion(f32[6,1024,2048]{2,1,0:T(8,128)} %get-tuple-element.81, f32[6,1024]{1,0:T(8,128)S(1)} %get-tuple-element.80, pred[1024,2048]{1,0:T(8,128)(4,1)S(1)} %fusion.2), kind=kLoop, calls=%fused_computation.3 | loop fusion | flops 50325504 | bytes 52477952 | tf_op jit(solution)/shard_map/reduce_sum | solution.py:187
  172.2 35.6 %multiply_reduce_fusion = (f32[6,1024]{1,0:T(8,128)S(1)}, f32[6,1024,2048]{2,1,0:T(8,128)}) fusion(f32[6,1024,2048]{2,1,0:T(8,128)} %get-tuple-element.81, f32[6,1024]{1,0:T(8,128)S(1)} %log_add_fusion, pred[1024,2048]{1,0:T(8,128)(4,1)S(1)} %fusion.2, bf16[1024,6,64]{0,2,1:T(8,128)(2,1)S(1)} %bitcast.189, bf16[2048,6,64]{0,2,1:T(8,128)(2,1)} %bitcast.181), kind=kOutput, calls=%fused_computation.1 | convolution fusion | flops 1673521152 | bytes 105168896 | tf_op jit(solution)/shard_map/qhd,khd->hqk/dot_general | solution.py:237
  207.9 41.2 %multiply_convert_fusion = bf16[6,1024,2048]{2,1,0:T(8,128)(2,1)} fusion(f32[6,1024,2048]{2,1,0:T(8,128)} %get-tuple-element.83, f32[6,1024,2048]{2,1,0:T(8,128)} %get-tuple-element.81, f32[6,1024]{1,0:T(8,128)S(1)} %get-tuple-element.82, f32[6,1024]{1,0:T(8,128)S(1)} %log_add_fusion, pred[1024,2048]{1,0:T(8,128)(4,1)S(1)} %fusion.2), kind=kLoop, calls=%fused_computation | loop fusion | flops 75497472 | bytes 127975424 | tf_op jit(solution)/shard_map/convert_element_type | solution.py:240
  249.1 13.8 %multiply_convert_fusion.1 = bf16[6,64,2048]{2,1,0:T(8,128)(2,1)} fusion(bf16[6,1024,2048]{2,1,0:T(8,128)(2,1)} %multiply_convert_fusion, bf16[1024,6,48]{0,2,1:T(8,128)(2,1)S(1)} %slice.141, bf16[1024,6,16]{0,2,1:T(8,128)(2,1)S(1)} %copy-done.13), kind=kOutput, calls=%fused_computation.82 | convolution fusion | flops 1613758464 | bytes 27525120 | tf_op jit(solution)/shard_map/hqk,qhd->khd/dot_general | solution.py:247
  263.1 21.5 %convolution_convert_fusion.2 = bf16[6,64,2048]{2,1,0:T(8,128)(2,1)} fusion(bf16[1024,6,64]{0,2,1:T(8,128)(2,1)S(1)} %bitcast.190, f32[6,1024,2048]{2,1,0:T(8,128)} %get-tuple-element.81, f32[6,1024]{1,0:T(8,128)S(1)} %log_add_fusion, pred[1024,2048]{1,0:T(8,128)(4,1)S(1)} %fusion.2), kind=kOutput, calls=%fused_computation.83 | convolution fusion | flops 1661730816 | bytes 54812672 | tf_op jit(solution)/shard_map/hqk,qhd->khd/dot_general | solution.py:252
  284.5 2.6 copy.53
  287.2 19.6 %fusion.5 = (bf16[1024,1536]{1,0:T(8,128)(2,1)}, f32[1024,1536]{1,0:T(8,128)}) fusion(f32[1536]{0:T(1024)S(1)} %convert_element_type.293, bf16[768,1536]{1,0:T(8,128)(2,1)} %all-gather.13.cloned.1.call-done, bf16[1,1024,768]{2,1,0:T(8,128)(2,1)} %param.15, f32[768]{0:T(1024)S(1)} %convert_element_type.291, f32[768]{0:T(1024)S(1)} %convert_element_type.290, ...), kind=kOutput, calls=%fused_computation.13 | convolution fusion | flops 2524446720 | bytes 13389824 | tf_op jit(solution)/shard_map/dot_general | solution.py:195
  306.8 21.4 %convolution_convert_fusion.7 = bf16[6,64,1024]{2,1,0:T(8,128)(2,1)S(1)} fusion(bf16[2048,6,64]{0,2,1:T(8,128)(2,1)S(1)} %bitcast.182, f32[6,1024,2048]{2,1,0:T(8,128)} %get-tuple-element.81, f32[6,1024]{1,0:T(8,128)S(1)} %log_add_fusion, pred[1024,2048]{1,0:T(8,128)(4,1)S(1)} %fusion.2), kind=kOutput, calls=%fused_computation.112 | convolution fusion | flops 1661337600 | bytes 54812672 | tf_op jit(solution)/shard_map/hqk,khd->qhd/dot_general | solution.py:191
  329.1 1.9 fusion.79
  331.0 7.2 fusion.113
  339.9 4.1 convolution_convert_fusion.1
  344.1 5.8 convolution_convert_fusion
  350.0 13.9 %multiply_bitcast_fusion = f32[1024,6,64]{0,2,1:T(8,128)} fusion(bf16[2048,6,64]{0,2,1:T(8,128)(2,1)} %bitcast.184, bf16[6,1024,2048]{2,1,0:T(8,128)(2,1)} %multiply_convert_fusion), kind=kOutput, calls=%fused_computation.105 | convolution fusion | flops 1611005952 | bytes 28311552 | tf_op jit(solution)/shard_map/hqk,khd->qhd/dot_general | solution.py:242
  363.9 2.3 slice.139
  366.2 2.0 slice.107
  371.5 2.3 copy.54
  373.8 2.0 pad_maximum_fusion.4
  375.8 2.3 copy.55
  378.2 5.5 convolution_convert_fusion.3
  383.7 2.2 fusion.104
  387.0 6.4 convolution_convert_fusion.5
  393.4 69.8 %reduce-scatter.18.cloned.1.call-done = bf16[96,1536]{1,0:T(8,128)(2,1)} async-done(((bf16[768,1536]{1,0:T(8,128)(2,1)}), bf16[96,1536]{1,0:T(8,128)(2,1)}) %reduce-scatter.18.cloned.1.call-update) | async-done | bytes 294928 | tf_op jit(solution)/shard_map/reduce_scatter | solution.py:313
  463.2 71.8 %reduce-scatter.20.cloned.1.call-done = bf16[1536,96]{0,1:T(8,128)(2,1)} async-done(((bf16[1536,768]{0,1:T(8,128)(2,1)}), bf16[1536,96]{0,1:T(8,128)(2,1)}) %reduce-scatter.20.cloned.1.call-update) | async-done | bytes 294928 | tf_op jit(solution)/shard_map/reduce_scatter | solution.py:319
  535.0 69.1 %reduce-scatter.14.cloned.1.call-done = bf16[96,3,384]{2,0,1:T(8,128)(2,1)} async-done(((bf16[768,3,384]{2,0,1:T(8,128)(2,1)}), bf16[96,3,384]{2,0,1:T(8,128)(2,1)}) %reduce-scatter.14.cloned.1.call-update) | async-done | bytes 221200 | tf_op jit(solution)/shard_map/reduce_scatter | solution.py:301
  604.3 6.5 convolution_convert_fusion.6
  610.8 2.2 convolution_convert_fusion.4
  613.0 3.4 bitcast_convert_fusion
  618.5 45.9 %reduce-scatter.22.cloned.1.call-done = bf16[48,3]{1,0:T(8,128)(2,1)} async-done(((bf16[384,3]{1,0:T(8,128)(2,1)}), bf16[48,3]{1,0:T(8,128)(2,1)}) %reduce-scatter.22.cloned.1.call-update) | async-done | bytes 304
  665.2 37.8 %all-reduce.23.cloned.1.call-done = (bf16[96,3,384]{2,0,1:T(8,128)(2,1)}, bf16[384,96]{0,1:T(8,128)(2,1)}, bf16[96,1536]{1,0:T(8,128)(2,1)}, bf16[1536,96]{0,1:T(8,128)(2,1)}) async-done(((bf16[96,3,384]{2,0,1:T(8,128)(2,1)}, bf16[384,96]{0,1:T(8,128)(2,1)}, bf16[96,1536]{1,0:T(8,128)(2,1)}, bf16[1536,96]{0,1:T(8,128)(2,1)}), (bf16[96,3,384]{2,0,1:T(8,128)(2,1)}, bf16[384,96]{0,1:T(8,128)(2,1)}, ...) | async-done | bytes 884752 | tf_op jit(solution)/shard_map/psum | solution.py:339
  702.9 1.8 convert_element_type.322
  704.8 1.8 convert_element_type.325
  706.6 1.7 convert_element_type.316
  709.9 28.5 %all-reduce.21.cloned.1.call-done = (bf16[1024,768]{1,0:T(8,128)(2,1)}, bf16[1024,768]{1,0:T(8,128)(2,1)}, bf16[1024,768]{1,0:T(8,128)(2,1)}, bf16[1024,768]{1,0:T(8,128)(2,1)}) async-done(((bf16[1024,768]{1,0:T(8,128)(2,1)}, bf16[1024,768]{1,0:T(8,128)(2,1)}, bf16[1024,768]{1,0:T(8,128)(2,1)}, bf16[1024,768]{1,0:T(8,128)(2,1)}), (bf16[1024,768]{1,0:T(8,128)(2,1)}, bf16[1024,768]{1,0:T(8,128)(2,1)}, ...) | async-done | bytes 6291472 | tf_op jit(solution)/shard_map/psum | solution.py:204
  738.4 4.8 fusion.48
  743.2 1.7 reduce_sum.220
  745.2 37.3 %all-reduce.13 = (bf16[768]{0:T(1024)(128)(2,1)S(1)}, bf16[768]{0:T(1024)(128)(2,1)S(1)}, bf16[768]{0:T(1024)(128)(2,1)S(1)}, bf16[1536]{0:T(1024)(128)(2,1)S(1)...) all-reduce(bf16[768]{0:T(1024)(128)(2,1)S(1)} %dynamic-update-slice, ...), channel_id=1, replica_groups=mesh['fsdp'=8,'context'=2,'tensor'=2] {'fsdp'}, use_global_device_ids=true, to_apply=%add.6 | all-reduce | flops 6912 | bytes 27648
  783.0 4.9 all-reduce.16
  791.2 5.8 fusion.39
  (178 shorter events, 31.0 us)
Async XLA Ops:
  7.2 67.3 %copy-start = (bf16[1,1024,768]{2,1,0:T(8,128)(2,1)S(1)}, bf16[1,1024,768]{2,1,0:T(8,128)(2,1)}, u32[]{:S(2)}) copy-start(bf16[1,1024,768]{2,1,0:T(8,128)(2,1)} %param.15) | copy-start | bytes 4718596
  7.2 67.9 %all-gather.7.cloned.1.call-start = ((), (), s32[]{:S(2)}) async-start(), calls=%async_computation.7 | async-start | bytes 1990656 | tf_op jit(solution)/shard_map/all_gather | solution.py:119
  7.9 117.9 %all-gather.11.cloned.1.call-start = ((), (), s32[]{:S(2)}) async-start(), calls=%async_computation.9 | async-start | bytes 2359296 | tf_op jit(solution)/shard_map/all_gather | solution.py:160
  54.0 23.8 %copy-start.22 = (f32[768]{0:T(1024)}, f32[768]{0:T(1024)S(1)}, u32[]{:S(2)}) copy-start(f32[768]{0:T(1024)S(1)} %convert_element_type.274) | copy-start | bytes 9220
  54.0 23.8 %copy-start.24 = (f32[768]{0:T(1024)}, f32[768]{0:T(1024)S(1)}, u32[]{:S(2)}) copy-start(f32[768]{0:T(1024)S(1)} %convert_element_type.275) | copy-start | bytes 9220
  72.7 9.6 %copy-start.15 = (f32[1024,16]{0,1:T(8,128)}, f32[1024,16]{0,1:T(8,128)S(1)}, u32[]{:S(2)}) copy-start(f32[1024,16]{0,1:T(8,128)S(1)} %get-tuple-element.74) | copy-start | bytes 196612
  72.7 9.6 %copy-start.17 = (f32[1024,16]{0,1:T(8,128)}, f32[1024,16]{0,1:T(8,128)S(1)}, u32[]{:S(2)}) copy-start(f32[1024,16]{0,1:T(8,128)S(1)} %get-tuple-element.75) | copy-start | bytes 196612
  80.0 2.1 copy-start.7
  82.1 2.1 copy-start.6
  83.3 4.9 copy-start.27
  83.3 5.0 copy-start.21
  83.3 36.6 %copy-start.3 = (bf16[1,1024,768]{2,1,0:T(8,128)(2,1)S(1)}, bf16[1,1024,768]{2,1,0:T(8,128)(2,1)}, u32[]{:S(2)}) copy-start(bf16[1,1024,768]{2,1,0:T(8,128)(2,1)} %param.17) | copy-start | bytes 4718596
  84.3 87.9 %all-gather.9.cloned.1.call-start = ((), (), s32[]{:S(2)}) async-start(), calls=%async_computation.8 | async-start | bytes 2359296 | tf_op jit(solution)/shard_map/all_gather | solution.py:161
  86.8 200.4 %all-gather.13.cloned.1.call-start = ((), (), s32[]{:S(2)}) async-start(), calls=%async_computation.10 | async-start | bytes 2654208 | tf_op jit(solution)/shard_map/all_gather | solution.py:123
  87.4 243.7 %all-gather.15.cloned.1.call-start = ((), (), s32[]{:S(2)}) async-start(), calls=%async_computation.11 | async-start | bytes 2654208 | tf_op jit(solution)/shard_map/all_gather | solution.py:125
  88.0 278.2 %reduce-scatter.10.cloned.1.call-start = ((), (), s32[]{:S(2)}) async-start(), calls=%async_computation.12 | async-start | bytes 2359296 | tf_op jit(solution)/shard_map/reduce_scatter | solution.py:254
  119.9 0.8 copy-start.19
  207.9 41.2 %copy-start.13 = (bf16[1024,6,16]{0,2,1:T(8,128)(2,1)S(1)}, bf16[1024,6,16]{0,2,1:T(8,128)(2,1)}, u32[]{:S(2)}) copy-start(bf16[1024,6,16]{0,2,1:T(8,128)(2,1)} %get-tuple-element.68) | copy-start | bytes 589828
  249.1 13.9 %copy-start.26 = (bf16[768]{0:T(1024)(128)(2,1)S(1)}, bf16[768]{0:T(1024)(128)(2,1)}, u32[]{:S(2)}) copy-start(bf16[768]{0:T(1024)(128)(2,1)} %get-tuple-element.35) | copy-start | bytes 4612
  263.0 115.2 %reduce-scatter.12.cloned.1.call-start = ((), (), s32[]{:S(2)}) async-start(), calls=%async_computation.13 | async-start | bytes 2359296 | tf_op jit(solution)/shard_map/reduce_scatter | solution.py:260
  287.1 106.3 %reduce-scatter.16.cloned.1.call-start = ((), (), s32[]{:S(2)}) async-start(), calls=%async_computation.15 | async-start | bytes 663552 | tf_op jit(solution)/shard_map/reduce_scatter | solution.py:307
  287.2 19.6 %copy-start.12 = (bf16[1,2048,384]{1,2,0:T(8,128)(2,1)S(1)}, bf16[1,2048,384]{1,2,0:T(8,128)(2,1)}, u32[]{:S(2)}) copy-start(bf16[1,2048,384]{1,2,0:T(8,128)(2,1)} %all-gather.9.cloned.1.call-done) | copy-start | bytes 4718596
  306.8 22.3 %copy-start.4 = (bf16[1,1024,768]{2,1,0:T(8,128)(2,1)S(1)}, bf16[1,1024,768]{2,1,0:T(8,128)(2,1)}, u32[]{:S(2)}) copy-start(bf16[1,1024,768]{2,1,0:T(8,128)(2,1)} %param.17) | copy-start | bytes 4718596
  328.2 0.9 copy-start.30
  328.2 2.8 copy-start.5
  331.0 132.3 %reduce-scatter.18.cloned.1.call-start = ((), (), s32[]{:S(2)}) async-start(), calls=%async_computation.16 | async-start | bytes 2654208 | tf_op jit(solution)/shard_map/reduce_scatter | solution.py:313
  331.0 8.9 %copy-start.1 = (bf16[1,1024,768]{2,1,0:T(8,128)(2,1)S(1)}, bf16[1,1024,768]{2,1,0:T(8,128)(2,1)}, u32[]{:S(2)}) copy-start(bf16[1,1024,768]{2,1,0:T(8,128)(2,1)} %param.15) | copy-start | bytes 4718596
  338.2 1.7 copy-start.33
  344.1 191.0 %reduce-scatter.20.cloned.1.call-start = ((), (), s32[]{:S(2)}) async-start(), calls=%async_computation.17 | async-start | bytes 2654208 | tf_op jit(solution)/shard_map/reduce_scatter | solution.py:319
  350.0 18.2 %copy-start.18 = (f32[1024,16]{0,1:T(8,128)S(1)}, f32[1024,16]{0,1:T(8,128)}, u32[]{:S(2)}) copy-start(f32[1024,16]{0,1:T(8,128)} %copy-done.17) | copy-start | bytes 196612
  350.0 254.2 %reduce-scatter.14.cloned.1.call-start = ((), (), s32[]{:S(2)}) async-start(), calls=%async_computation.14 | async-start | bytes 1990656 | tf_op jit(solution)/shard_map/reduce_scatter | solution.py:301
  363.9 5.5 copy-start.16
  366.2 4.4 copy-start.10
  370.6 7.6 copy-start.23
  370.6 7.6 copy-start.25
  383.7 280.7 %reduce-scatter.22.cloned.1.call-start = ((), (), s32[]{:S(2)}) async-start(), calls=%async_computation.18 | async-start | bytes 110592
  386.7 316.2 %all-reduce.23.cloned.1.call-start = ((), (), s32[]{:S(2)}) async-start(), calls=%async_computation.20 | async-start | bytes 1769472 | tf_op jit(solution)/shard_map/psum | solution.py:339
  604.1 134.3 %all-reduce.21.cloned.1.call-start = ((), (), s32[]{:S(2)}) async-start(), calls=%async_computation.19 | async-start | bytes 12582912 | tf_op jit(solution)/shard_map/psum | solution.py:204
  604.2 6.6 copy-start.20
  604.2 6.6 copy-start.31
  604.2 8.8 %copy-start.8 = (bf16[1024,1,384]{2,0,1:T(8,128)(2,1)S(1)}, bf16[1024,1,384]{2,0,1:T(8,128)(2,1)}, u32[]{:S(2)}) copy-start(bf16[1024,1,384]{2,0,1:T(8,128)(2,1)} %copy.54) | copy-start | bytes 2359300
  604.2 8.7 %copy-start.9 = (bf16[1024,1,384]{2,0,1:T(8,128)(2,1)S(1)}, bf16[1024,1,384]{2,0,1:T(8,128)(2,1)}, u32[]{:S(2)}) copy-start(bf16[1024,1,384]{2,0,1:T(8,128)(2,1)} %copy.55) | copy-start | bytes 2359300
  604.2 8.7 %copy-start.11 = (bf16[768,3,384]{2,0,1:T(8,128)(2,1)S(1)}, bf16[768,3,384]{2,0,1:T(8,128)(2,1)}, u32[]{:S(2)}) copy-start(bf16[768,3,384]{2,0,1:T(8,128)(2,1)} %all-gather.7.cloned.1.call-done) | copy-start | bytes 5308420
  604.2 8.7 %copy-start.14 = (bf16[1,1024,384]{2,1,0:T(8,128)(2,1)S(1)}, bf16[1,1024,384]{2,1,0:T(8,128)(2,1)}, u32[]{:S(2)}) copy-start(bf16[1,1024,384]{2,1,0:T(8,128)(2,1)} %reduce-scatter.12.cloned.1.call-done) | copy-start | bytes 2359300
  616.4 1.6 copy-start.28
  616.4 1.9 copy-start.29
  738.4 6.5 copy-start.2
  789.1 7.9 copy-start.32
Sparse Core Ops, SparseCore 0:
  10.2 48.7 all-gather.6
  84.4 25.6 all-gather.10
  112.3 27.1 all-gather.8
  141.5 52.0 all-gather.12
  195.7 50.6 all-gather.14
  263.1 24.1 reduce-scatter.9
  289.6 26.0 reduce-scatter.11
  331.1 60.0 reduce-scatter.15
  395.1 68.0 reduce-scatter.17
  467.0 68.0 reduce-scatter.19
  538.9 65.1 reduce-scatter.13
  607.8 56.5 reduce-scatter.21
  666.9 36.0 all-reduce.22
  706.2 32.2 all-reduce.20
where the time goes:
time: 811 us; the launch traced here: 804 us
  waiting for transfers between devices  325 us (40%)
  matrix products  194 us (24%)
  blocking collectives  130 us (16%)
  other arithmetic  106 us (13%)
  local copies, waits for them, and re-layouts  31.3 us (4%)
  between operations  17.6 us (2%)
    unnamed x2, blocking collectives  76.5 us
    reduce_scatter x1, waiting for transfers between devices, body(): lax.psum_scatter(narrowing_slope.astype(jnp.bfloat16), 'fsdp', scatter_di...  71.8 us
    reduce_scatter x1, waiting for transfers between devices, body(): lax.psum_scatter(widening_slope.astype(jnp.bfloat16), 'fsdp', scatter_dim...  69.8 us
    reduce_scatter x1, waiting for transfers between devices, body(): lax.psum_scatter(projection_slope.astype(jnp.bfloat16), 'fsdp', scatter_d...  69.1 us
    unnamed x15, waiting for transfers between devices  47.8 us
    convert_element_type x1, other arithmetic, body(): score_slope = (probs * (probs_slope - balance)).astype(jnp.bfloat16)  41.2 us
    psum x1, waiting for transfers between devices, body(): lax.psum(owned[0].astype(jnp.bfloat16), 'context').astype(jnp.float32)  37.8 us
    dot_general x1, matrix products, body(): jnp.einsum('qhd,khd->hqk', outer, value_block, preferred_element_type=jnp...  35.6 us
  transfers between devices with their start and end apart: 14, of which 6 were waited for; matrix products, arithmetic and copies ran while one was open for 38% of the time, Pallas kernels for 0%

commit v1 on v0

--- a/solution.py
+++ b/solution.py
@@ -1,6 +1,8 @@
 import jax
 import jax.numpy as jnp
 from jax import lax
+from jax.experimental import pallas as pl
+from jax.experimental.pallas import tpu as pltpu
 from jax.sharding import PartitionSpec as P
 
 HEAD_DIM = 64
@@ -14,12 +16,12 @@
 
 def layout(lengths, index):
     padded = (lengths + TILE - 1) // TILE * TILE
-    finish = jnp.cumsum(padded)
+    labels = jnp.arange(SEQS, dtype=jnp.int32)
+    finish = jnp.sum(jnp.where(labels[:, None] <= labels[None, :], padded[:, None], 0), axis=0)
     before = (index[:, None] >= finish[None, :]).astype(jnp.int32)
     number = jnp.sum(before, axis=1)
     start = jnp.sum(before * padded[None, :], axis=1)
     position = index - start
-    labels = jnp.arange(SEQS, dtype=jnp.int32)
     length = jnp.sum(jnp.where(number[:, None] == labels[None, :], lengths[None, :], 0), axis=1)
     return (number, position, position < length)
 
@@ -82,7 +84,7 @@
     return same | (query_index[:, None] == key_index[None, :])
 
 
-def body(
+def general_body(
     tokens,
     pack_lengths,
     cotangent,
@@ -352,6 +354,731 @@
     return (mixed, tokens_gradient) + tuple(final)
 
 
+BLOCK = 256
+FLOAT = jnp.float32
+LOW = jnp.bfloat16
+
+
+def nn(left, right):
+    return lax.dot_general(left, right, (((1,), (0,)), ((), ())), preferred_element_type=FLOAT)
+
+
+def nt(left, right):
+    return lax.dot_general(left, right, (((1,), (1,)), ((), ())), preferred_element_type=FLOAT)
+
+
+def tn(left, right):
+    return lax.dot_general(left, right, (((0,), (0,)), ((), ())), preferred_element_type=FLOAT)
+
+
+def center(values):
+    average = jnp.mean(values, axis=-1, keepdims=True)
+    centered = values - average
+    spread = jnp.mean(centered * centered, axis=-1, keepdims=True)
+    factor = lax.rsqrt(spread + epsilon)
+    return centered * factor, factor
+
+
+def widen_lanes(table, times):
+    return jnp.concatenate([table] * times, axis=1)
+
+
+def prepare_kernel(
+    place, own_x, peer_x, own_g, peer_g, gain, shift, bias, weight, cos, left, right,
+    q_out, k_out, v_out, o_out,
+):
+    inner = q_out.shape[1]
+    step = pl.program_id(0)
+    half = pl.num_programs(0) // 2
+
+    def work(x_ref, g_ref):
+        unit, _ = center(x_ref[...].astype(FLOAT))
+        normed = (unit * gain[...] + shift[...]).astype(LOW)
+        raw = nn(normed, weight[:, : 3 * inner + 64]) + bias[...]
+        both = raw[:, : 2 * inner]
+        times = 2 * inner // 128
+        turned = (
+            both * widen_lanes(cos[...], times)
+            + pltpu.roll(both, 2 * inner - ROTARY // 2, 1) * widen_lanes(left[...], times)
+            + pltpu.roll(both, ROTARY // 2, 1) * widen_lanes(right[...], times)
+        )
+        q_out[...] = (turned[:, :inner] * HEAD_DIM ** (-0.5)).astype(LOW)
+        k_out[...] = turned[:, inner:].astype(LOW)
+        v_out[...] = raw[:, 2 * inner : 3 * inner].astype(LOW)
+        o_out[...] = nn(g_ref[...], weight[:, 3 * inner - 64 :])[:, 64:].astype(LOW)
+
+    @pl.when(step < half)
+    def _():
+        work(own_x, own_g)
+
+    @pl.when(step >= half)
+    def _():
+        work(peer_x, peer_g)
+
+
+def prepare(place, own_x, peer_x, own_g, peer_g, gain, shift, bias, weight, tables, inner):
+    rows, width = own_x.shape
+    half = rows // BLOCK
+
+    def own(s, place):
+        return (jnp.minimum(s, half - 1), 0)
+
+    def peer(s, place):
+        return (jnp.maximum(s - half, 0), 0)
+
+    def target(s, place):
+        return (jnp.where(s < half, place[0] * half + s, (1 - place[0]) * half + s - half), 0)
+
+    def fixed(s, place):
+        return (0, 0)
+
+    table = pl.BlockSpec((BLOCK, 128), target)
+    return pl.pallas_call(
+        prepare_kernel,
+        grid_spec=pltpu.PrefetchScalarGridSpec(
+            num_scalar_prefetch=1,
+            grid=(2 * half,),
+            in_specs=[
+                pl.BlockSpec((BLOCK, width), own),
+                pl.BlockSpec((BLOCK, width), peer),
+                pl.BlockSpec((BLOCK, width), own),
+                pl.BlockSpec((BLOCK, width), peer),
+                pl.BlockSpec((1, width), fixed),
+                pl.BlockSpec((1, width), fixed),
+                pl.BlockSpec(bias.shape, fixed),
+                pl.BlockSpec(weight.shape, fixed),
+                table,
+                table,
+                table,
+            ],
+            out_specs=[pl.BlockSpec((BLOCK, inner), target)] * 4,
+        ),
+        out_shape=[jax.ShapeDtypeStruct((2 * rows, inner), LOW)] * 4,
+        compiler_params=pltpu.CompilerParams(vmem_limit_bytes=40 << 20),
+        cost_estimate=pl.CostEstimate(
+            flops=2 * 2 * rows * width * 4 * inner, bytes_accessed=16 * rows * width, transcendentals=0
+        ),
+        name="prepare",
+    )(place, own_x, peer_x, own_g, peer_g, gain, shift, bias, weight, *tables)
+
+
+def attention_kernel(
+    first, q_ref, k_ref, v_ref, o_ref, start_ref, stop_ref, cos, left, right,
+    heads_out, slope_out,
+    kt, vt, qm, om, probs, outer, dk, dv, ot, dqt,
+):
+    inner = q_ref.shape[1]
+    heads = inner // HEAD_DIM
+    wide = heads * BLOCK
+    step = pl.program_id(0)
+    count = pl.num_programs(0)
+    block = count - 1 - step
+
+    @pl.when(step == 0)
+    def _():
+        dk[...] = jnp.zeros_like(dk)
+        dv[...] = jnp.zeros_like(dv)
+        ot[...] = jnp.zeros_like(ot)
+        dqt[...] = jnp.zeros_like(dqt)
+
+        @pl.loop(0, count)
+        def _(j):
+            rows = pl.ds(pl.multiple_of(j * BLOCK, BLOCK), BLOCK)
+            kt[:, rows] = jnp.transpose(k_ref[rows, :].astype(FLOAT)).astype(LOW)
+            vt[:, rows] = jnp.transpose(v_ref[rows, :].astype(FLOAT)).astype(LOW)
+
+    head = lax.broadcasted_iota(jnp.int32, (BLOCK, inner), 1) // HEAD_DIM
+    query = q_ref[...].astype(FLOAT)
+    slope = o_ref[...].astype(FLOAT)
+    for h in range(heads):
+        qm[h * BLOCK : (h + 1) * BLOCK, :] = jnp.where(head == h, query, 0.0).astype(LOW)
+        om[h * BLOCK : (h + 1) * BLOCK, :] = jnp.where(head == h, slope, 0.0).astype(LOW)
+    start = widen_lanes(start_ref[...], heads)
+    stop = widen_lanes(stop_ref[...], heads)
+    low = first[block]
+    row = lax.broadcasted_iota(jnp.int32, (BLOCK, wide), 0)
+
+    def span(j):
+        return pl.ds(pl.multiple_of(j * BLOCK, BLOCK), BLOCK)
+
+    def score(j, top):
+        raw = nt(k_ref[span(j), :], qm[...])
+        raw = jnp.where(row + j * BLOCK >= start, raw, -1e30)
+        probs[span(j), :] = raw
+        return jnp.maximum(top, jnp.max(raw, axis=0, keepdims=True))
+
+    raw = nt(k_ref[span(block), :], qm[...])
+    key = row + block * BLOCK
+    itself = widen_lanes(
+        lax.broadcasted_iota(jnp.int32, (1, BLOCK), 1) + block * BLOCK, heads
+    )
+    raw = jnp.where(((key >= start) & (key < stop)) | (key == itself), raw, -1e30)
+    probs[span(block), :] = raw
+    top = lax.fori_loop(low, block, score, jnp.max(raw, axis=0, keepdims=True))
+
+    def weigh(j, carry):
+        total, balance = carry
+        weight = jnp.exp(probs[span(j), :] - top)
+        back = nt(v_ref[span(j), :], om[...])
+        probs[span(j), :] = weight
+        outer[span(j), :] = back
+        return (
+            total + jnp.sum(weight, axis=0, keepdims=True),
+            balance + jnp.sum(weight * back, axis=0, keepdims=True),
+        )
+
+    zero = jnp.zeros((1, wide), FLOAT)
+    total, balance = lax.fori_loop(low, block + 1, weigh, (zero, zero))
+    scale = 1.0 / total
+    balance = balance * scale
+    ot[:inner, :] = jnp.zeros((inner, BLOCK), FLOAT)
+    dqt[:inner, :] = jnp.zeros((inner, BLOCK), FLOAT)
+
+    @pl.loop(low, block + 1)
+    def _(j):
+        normal = probs[span(j), :] * scale
+        weight = normal.astype(LOW)
+        change = (normal * (outer[span(j), :] - balance)).astype(LOW)
+        dv[span(j), :] += nn(weight, om[...])
+        dk[span(j), :] += nn(change, qm[...])
+        for h in range(heads):
+            lines = slice(h * HEAD_DIM, (h + 1) * HEAD_DIM)
+            lanes = slice(h * BLOCK, (h + 1) * BLOCK)
+            ot[lines, :] += nn(vt[lines, span(j)], weight[:, lanes])
+            dqt[lines, :] += nn(kt[lines, span(j)], change[:, lanes])
+
+    heads_out[...] = jnp.transpose(ot[...])[:, :inner].astype(LOW)
+    dq = jnp.transpose(dqt[...])[:, :inner] * HEAD_DIM ** (-0.5)
+    both = jnp.concatenate([dq, dk[span(block), :]], axis=1)
+    times = 2 * inner // 128
+    turned = (
+        both * widen_lanes(cos[...], times)
+        - pltpu.roll(both, 2 * inner - ROTARY // 2, 1) * widen_lanes(left[...], times)
+        - pltpu.roll(both, ROTARY // 2, 1) * widen_lanes(right[...], times)
+    )
+    slope_out[...] = jnp.concatenate([turned, dv[span(block), :]], axis=1).astype(LOW)
+
+
+def attention(first, q, k, v, o, start, stop, tables):
+    group, inner = q.shape
+    count = group // BLOCK
+    heads = inner // HEAD_DIM
+
+    def rows(s, first):
+        return (count - 1 - s, 0)
+
+    def lanes(s, first):
+        return (0, count - 1 - s)
+
+    def fixed(s, first):
+        return (0, 0)
+
+    blocked = pl.BlockSpec((BLOCK, inner), rows)
+    whole = pl.BlockSpec((group, inner), fixed)
+    table = pl.BlockSpec((BLOCK, 128), rows)
+    side = pl.BlockSpec((1, BLOCK), lanes)
+    return pl.pallas_call(
+        attention_kernel,
+        grid_spec=pltpu.PrefetchScalarGridSpec(
+            num_scalar_prefetch=1,
+            grid=(count,),
+            in_specs=[blocked, whole, whole, blocked, side, side, table, table, table],
+            out_specs=[blocked, pl.BlockSpec((BLOCK, 3 * inner), rows)],
+            scratch_shapes=[
+                pltpu.VMEM((inner, group), LOW),
+                pltpu.VMEM((inner, group), LOW),
+                pltpu.VMEM((heads * BLOCK, inner), LOW),
+                pltpu.VMEM((heads * BLOCK, inner), LOW),
+                pltpu.VMEM((group, heads * BLOCK), FLOAT),
+                pltpu.VMEM((group, heads * BLOCK), FLOAT),
+                pltpu.VMEM((group, inner), FLOAT),
+                pltpu.VMEM((group, inner), FLOAT),
+                pltpu.VMEM((BLOCK, BLOCK), FLOAT),
+                pltpu.VMEM((BLOCK, BLOCK), FLOAT),
+            ],
+        ),
+        out_shape=[
+            jax.ShapeDtypeStruct((group, inner), LOW),
+            jax.ShapeDtypeStruct((group, 3 * inner), LOW),
+        ],
+        compiler_params=pltpu.CompilerParams(vmem_limit_bytes=48 << 20),
+        cost_estimate=pl.CostEstimate(
+            flops=40 * group * group * inner // 2, bytes_accessed=20 * group * inner, transcendentals=0
+        ),
+        name="attention",
+    )(first, q, k, v, o, start, stop, *tables)
+
+
+def feed_kernel(
+    x_ref, g_ref, gain, shift, bias, wide, narrow,
+    feed_out, e_out, wide_out, narrow_out, sums_out,
+):
+    step = pl.program_id(0)
+    unit, _ = center(x_ref[...].astype(FLOAT))
+    normed = (unit * gain[...] + shift[...]).astype(LOW)
+    slope = g_ref[...]
+    hidden = nn(normed, wide[...]) + bias[...]
+    phi = 0.5 * (1.0 + lax.erf(hidden * 0.7071067811865476))
+    active = (hidden * phi).astype(LOW)
+    feed_out[...] = nt(active, narrow[...]).astype(LOW)
+    inside = phi + hidden * jnp.exp(-0.5 * hidden * hidden) * 0.3989422804014327
+    change = (nn(slope, narrow[...]) * inside).astype(LOW)
+    back = nt(change, wide[...])
+    e_out[...] = (back * gain[...]).astype(LOW)
+    wide_part = tn(normed, change)
+    narrow_part = tn(slope, active)
+    sums = jnp.concatenate(
+        [
+            jnp.sum(back * unit, axis=0, keepdims=True),
+            jnp.sum(back, axis=0, keepdims=True),
+            jnp.sum(change.astype(FLOAT), axis=0, keepdims=True),
+            jnp.sum(slope.astype(FLOAT), axis=0, keepdims=True),
+            jnp.zeros((4, back.shape[1]), FLOAT),
+        ],
+        axis=0,
+    )
+
+    @pl.when(step == 0)
+    def _():
+        wide_out[...] = wide_part
+        narrow_out[...] = narrow_part
+        sums_out[...] = sums
+
+    @pl.when(step > 0)
+    def _():
+        wide_out[...] += wide_part
+        narrow_out[...] += narrow_part
+        sums_out[...] += sums
+
+
+def feed(x, g, gain, shift, bias, wide, narrow):
+    rows, width = x.shape
+    units = wide.shape[1]
+
+    def moving(s):
+        return (s, 0)
+
+    def fixed(s):
+        return (0, 0)
+
+    return pl.pallas_call(
+        feed_kernel,
+        grid=(rows // BLOCK,),
+        in_specs=[
+            pl.BlockSpec((BLOCK, width), moving),
+            pl.BlockSpec((BLOCK, width), moving),
+            pl.BlockSpec((1, width), fixed),
+            pl.BlockSpec((1, width), fixed),
+            pl.BlockSpec((1, units), fixed),
+            pl.BlockSpec((width, units), fixed),
+            pl.BlockSpec((width, units), fixed),
+        ],
+        out_specs=[
+            pl.BlockSpec((BLOCK, width), moving),
+            pl.BlockSpec((BLOCK, width), moving),
+            pl.BlockSpec((width, units), fixed),
+            pl.BlockSpec((width, units), fixed),
+            pl.BlockSpec((8, width), fixed),
+        ],
+        out_shape=[
+            jax.ShapeDtypeStruct((rows, width), LOW),
+            jax.ShapeDtypeStruct((rows, width), LOW),
+            jax.ShapeDtypeStruct((width, units), FLOAT),
+            jax.ShapeDtypeStruct((width, units), FLOAT),
+            jax.ShapeDtypeStruct((8, width), FLOAT),
+        ],
+        compiler_params=pltpu.CompilerParams(vmem_limit_bytes=48 << 20),
+        cost_estimate=pl.CostEstimate(
+            flops=12 * rows * width * units, bytes_accessed=12 * rows * width, transcendentals=0
+        ),
+        name="feed",
+    )(x, g, gain, shift, bias, wide, narrow)
+
+
+def finish_kernel(
+    place, x_ref, g_ref, heads_ref, slope_ref, feed_ref, e_ref, gain, shift, weight,
+    mixed_out, e_out, weight_out, sums_out,
+):
+    step = pl.program_id(0)
+    inner = heads_ref.shape[1]
+    unit, _ = center(x_ref[...].astype(FLOAT))
+    normed = (unit * gain[...] + shift[...]).astype(LOW)
+    mixed = heads_ref[...]
+    slope = slope_ref[...]
+    pad = jnp.zeros((BLOCK, 64), LOW)
+    lower = jnp.concatenate([pad, mixed], axis=1)
+    mixed_out[...] = (
+        nt(lower, weight[:, 3 * inner - 64 :]) + feed_ref[...].astype(FLOAT)
+    ).astype(LOW)
+    upper = jnp.concatenate([slope, pad], axis=1)
+    back = nt(upper, weight[:, : 3 * inner + 64])
+    e_out[...] = (back * gain[...] + e_ref[...].astype(FLOAT)).astype(LOW)
+    part = jnp.concatenate([tn(normed, upper)[:, : 3 * inner], tn(g_ref[...], mixed)], axis=1)
+    width = back.shape[1]
+    sums = jnp.concatenate(
+        [
+            jnp.sum(back * unit, axis=0, keepdims=True),
+            jnp.sum(back, axis=0, keepdims=True),
+            jnp.sum(jnp.concatenate([slope, jnp.zeros((BLOCK, width - 3 * inner), LOW)], axis=1).astype(FLOAT), axis=0, keepdims=True),
+            jnp.zeros((5, width), FLOAT),
+        ],
+        axis=0,
+    )
+
+    @pl.when(step == 0)
+    def _():
+        weight_out[...] = part
+        sums_out[...] = sums
+
+    @pl.when(step > 0)
+    def _():
+        weight_out[...] += part
+        sums_out[...] += sums
+
+
+def finish(place, x, g, heads, slope, feed_part, e, gain, shift, weight):
+    rows, width = x.shape
+    inner = heads.shape[1]
+    count = rows // BLOCK
+
+    def moving(s, place):
+        return (s, 0)
+
+    def shifted(s, place):
+        return (place[0] * count + s, 0)
+
+    def fixed(s, place):
+        return (0, 0)
+
+    token = pl.BlockSpec((BLOCK, width), moving)
+    line = pl.BlockSpec((1, width), fixed)
+    return pl.pallas_call(
+        finish_kernel,
+        grid_spec=pltpu.PrefetchScalarGridSpec(
+            num_scalar_prefetch=1,
+            grid=(count,),
+            in_specs=[
+                token,
+                token,
+                pl.BlockSpec((BLOCK, inner), shifted),
+                pl.BlockSpec((BLOCK, 3 * inner), shifted),
+                token,
+                token,
+                line,
+                line,
+                pl.BlockSpec(weight.shape, fixed),
+            ],
+            out_specs=[
+                token,
+                token,
+                pl.BlockSpec(weight.shape, fixed),
+                pl.BlockSpec((8, width), fixed),
+            ],
+        ),
+        out_shape=[
+            jax.ShapeDtypeStruct((rows, width), LOW),
+            jax.ShapeDtypeStruct((rows, width), LOW),
+            jax.ShapeDtypeStruct(weight.shape, FLOAT),
+            jax.ShapeDtypeStruct((8, width), FLOAT),
+        ],
+        compiler_params=pltpu.CompilerParams(vmem_limit_bytes=48 << 20),
+        cost_estimate=pl.CostEstimate(
+            flops=16 * rows * width * inner, bytes_accessed=12 * rows * width, transcendentals=0
+        ),
+        name="finish",
+    )(place, x, g, heads, slope, feed_part, e, gain, shift, weight)
+
+
+PAIR = [(0, 1), (1, 0)]
+
+
+def swap(value, axis):
+    return lax.ppermute(value, axis, PAIR)
+
+
+def ring_gather(piece):
+    n = lax.axis_size("fsdp")
+    order = list(range(0, n, 2)) + list(range(n - 1, 0, -2))
+    forward = [(order[i], order[(i + 1) % n]) for i in range(n)]
+    backward = [(b, a) for a, b in forward]
+    me = lax.axis_index("fsdp")
+    spot = jnp.where(me % 2 == 0, me // 2, n - 1 - me // 2)
+
+    def owner(position):
+        position = position % n
+        return jnp.where(position < n // 2, 2 * position, 2 * (n - 1 - position) + 1)
+
+    result = jnp.zeros((n,) + piece.shape, piece.dtype)
+    result = lax.dynamic_update_index_in_dim(result, piece, me, 0)
+    ahead = behind = piece
+    for step in range(1, n // 2 + 1):
+        ahead = lax.ppermute(ahead, "fsdp", forward)
+        result = lax.dynamic_update_index_in_dim(result, ahead, owner(spot - step + n), 0)
+        if step < n - n // 2:
+            behind = lax.ppermute(behind, "fsdp", backward)
+            result = lax.dynamic_update_index_in_dim(result, behind, owner(spot + step), 0)
+    return result
+
+
+def scatter_sum(parts):
+    n = lax.axis_size("fsdp")
+    depth = n // 2
+    me = lax.axis_index("fsdp")
+    z, x = me // 2, me % 2
+    parts = parts.reshape((depth, 2) + parts.shape[1:])
+    kept = lax.dynamic_index_in_dim(parts, x, 1, keepdims=False)
+    sent = lax.dynamic_index_in_dim(parts, 1 - x, 1, keepdims=False)
+    got = lax.ppermute(sent, "fsdp", [(i, i ^ 1) for i in range(n)])
+    both = (kept.astype(FLOAT) + got.astype(FLOAT)).astype(LOW)
+    total = lax.dynamic_index_in_dim(both, z, 0, keepdims=False).astype(FLOAT)
+    for step in range(1, depth):
+        pairs = [(2 * a + b, 2 * ((a + step) % depth) + b) for a in range(depth) for b in range(2)]
+        piece = lax.dynamic_index_in_dim(both, (z + step) % depth, 0, keepdims=False)
+        total = total + lax.ppermute(piece, "fsdp", pairs).astype(FLOAT)
+    return total.astype(LOW)
+
+
+def ordered(own, peer, index, axis=0):
+    first = jnp.where(index == 0, own, peer)
+    second = jnp.where(index == 0, peer, own)
+    return jnp.concatenate([first, second], axis=axis)
+
+
+def take_half(value, index, axis=0):
+    size = value.shape[axis] // 2
+    return lax.dynamic_slice_in_dim(value, index * size, size, axis)
+
+
+def split_body(
+    tokens,
+    pack_lengths,
+    cotangent,
+    projection,
+    projection_bias,
+    outgoing,
+    outgoing_bias,
+    widening,
+    widening_bias,
+    narrowing,
+    narrowing_bias,
+    first_gain,
+    first_shift,
+    second_gain,
+    second_shift,
+):
+    _, local, width = tokens.shape
+    n = lax.axis_size("fsdp")
+    group = 2 * local
+    share = width // n
+    y = lax.axis_index("context")
+    core = lax.axis_index("tensor")
+    own_x = tokens.reshape(local, width)
+    own_g = cotangent.reshape(local, width)
+    inner = outgoing.shape[0] // 2
+    units = narrowing.shape[0] // 2
+
+    def exchange(value):
+        mine = swap(take_half(value, core), "context")
+        return ordered(mine, swap(mine, "tensor"), core)
+
+    vectors = jnp.concatenate(
+        [
+            first_gain,
+            first_shift,
+            second_gain,
+            second_shift,
+            outgoing_bias,
+            narrowing_bias,
+            projection_bias.reshape(-1),
+            widening_bias,
+        ]
+    )
+    extra = 8 * units
+    vectors = jnp.pad(vectors, (0, extra - vectors.shape[0])).reshape(8, units)
+    wide_piece = jnp.concatenate([take_half(widening, y, 1), vectors], axis=0)
+    narrow_piece = take_half(narrowing, y, 0).T
+    attend_piece = jnp.concatenate(
+        [
+            take_half(projection, y, 2).reshape(share, 3 * inner),
+            take_half(outgoing, y, 0).T,
+        ],
+        axis=1,
+    )
+    peer_x = exchange(own_x)
+    peer_g = exchange(own_g)
+    gathered = ring_gather(wide_piece)
+    wide = gathered[:, :share].reshape(width, units)
+    flat = gathered[:, share:].reshape(n, extra)
+    narrow = ring_gather(narrow_piece).reshape(width, units)
+    attend = ring_gather(attend_piece).reshape(width, 3 * inner + inner)
+
+    def line(index):
+        return flat[:, index * share : (index + 1) * share].reshape(1, width).astype(FLOAT)
+
+    gain_one, shift_one, gain_two, shift_two, out_bias, narrow_bias = (line(i) for i in range(6))
+    base = 6 * share
+    third = projection_bias.shape[1]
+    bias_all = flat[:, base : base + 3 * third].reshape(n, 3, third).transpose(1, 0, 2)
+    bias_all = bias_all.reshape(3, n * third)
+    attend_bias = take_half(bias_all, y, 1).reshape(1, 3 * inner).astype(FLOAT)
+    attend_bias = jnp.pad(attend_bias, ((0, 0), (0, 64)))
+    base = base + 3 * third
+    unit_bias = flat[:, base : base + widening_bias.shape[0]].reshape(1, -1)
+    unit_bias = take_half(unit_bias, y, 1).astype(FLOAT)
+
+    index = jnp.arange(group, dtype=jnp.int32)
+    number, position, valid = layout(pack_lengths[0], index)
+    begin = index - position
+    labels = jnp.arange(SEQS, dtype=jnp.int32)
+    length = jnp.sum(
+        jnp.where(number[:, None] == labels[None, :], pack_lengths[0][None, :], 0), axis=1
+    )
+    stop = jnp.minimum(index + 1, begin + length)
+    start = jnp.where(number == SEQS, index, begin)
+    first = jnp.min(start.reshape(group // BLOCK, BLOCK), axis=1) // BLOCK
+    frequency = 10000.0 ** (-jnp.arange(0, ROTARY, 2, dtype=FLOAT) / ROTARY)
+    angles = frequency[:, None] * position.astype(FLOAT)[None, :]
+    cosine, sine = jnp.cos(angles).T, jnp.sin(angles).T
+    ones = jnp.ones((group, HEAD_DIM - ROTARY), FLOAT)
+    none = jnp.zeros((group, ROTARY // 2), FLOAT)
+    blank = jnp.zeros((group, HEAD_DIM - ROTARY), FLOAT)
+    tables = (
+        jnp.concatenate([cosine, cosine, ones] * 2, axis=1),
+        jnp.concatenate([-sine, none, blank] * 2, axis=1),
+        jnp.concatenate([none, sine, blank] * 2, axis=1),
+    )
+    place = y.reshape(1)
+    other = 1 - place
+
+    feed_own, e_own, wide_own, narrow_own, sums_own = feed(
+        own_x, own_g, gain_two, shift_two, unit_bias, wide, narrow
+    )
+    feed_peer, e_peer, wide_peer, narrow_peer, sums_peer = feed(
+        peer_x, peer_g, gain_two, shift_two, unit_bias, wide, narrow
+    )
+    g_sum = jnp.where(core == 0, 1.0, 0.0) * sums_own[3]
+    sums_feed = sums_own + sums_peer
+    narrow_total = scatter_sum((narrow_own + narrow_peer).astype(LOW).reshape(n, share, units))
+    all_units = jnp.zeros((2, units), FLOAT)
+    all_units = lax.dynamic_update_index_in_dim(all_units, sums_feed[2], y, 0)
+    vector = jnp.concatenate(
+        [
+            sums_feed[0].reshape(n, share),
+            sums_feed[1].reshape(n, share),
+            g_sum.reshape(n, share),
+            all_units.reshape(n, 2 * units // n),
+        ],
+        axis=1,
+    )
+    vector = jnp.pad(vector, ((0, 0), (0, extra - vector.shape[1]))).reshape(n, 8, units)
+    wide_total = scatter_sum(
+        jnp.concatenate(
+            [(wide_own + wide_peer).reshape(n, share, units), vector], axis=1
+        ).astype(LOW)
+    )
+
+    q, k, v, o = prepare(
+        place, own_x, peer_x, own_g, peer_g, gain_one, shift_one, attend_bias, attend, tables, inner
+    )
+    heads, slope = attention(
+        first, q, k, v, o, start.reshape(1, group), stop.reshape(1, group), tables
+    )
+    mixed_peer, e_peer, part_peer, sums_peer = finish(
+        other, peer_x, peer_g, heads, slope, feed_peer, e_peer, gain_one, shift_one, attend
+    )
+    mixed_own, e_own, part_own, sums_own = finish(
+        place, own_x, own_g, heads, slope, feed_own, e_own, gain_one, shift_one, attend
+    )
+
+    def reduce(own, peer):
+        far = take_half(peer, core).astype(FLOAT) + swap(take_half(peer, 1 - core), "tensor").astype(FLOAT)
+        far = swap(far.astype(LOW), "context").astype(FLOAT)
+        near = take_half(own, core).astype(FLOAT) + swap(take_half(own, 1 - core), "tensor").astype(FLOAT)
+        mine = (near + far).astype(LOW)
+        return ordered(mine, swap(mine, "tensor"), core).astype(FLOAT)
+
+    e_total = reduce(e_own, e_peer)
+    mixed_total = reduce(mixed_own, mixed_peer)
+    sums_attend = sums_own + sums_peer
+    all_bias = jnp.zeros((3, 2, inner), FLOAT)
+    all_bias = lax.dynamic_update_index_in_dim(
+        all_bias, sums_attend[2, : 3 * inner].reshape(3, inner), y, 1
+    )
+    vector = jnp.concatenate(
+        [
+            sums_attend[0].reshape(n, share),
+            sums_attend[1].reshape(n, share),
+            all_bias.reshape(3, n, third).transpose(1, 0, 2).reshape(n, 3 * third),
+        ],
+        axis=1,
+    )
+    columns = 4 * inner
+    vector = jnp.pad(vector, ((0, 0), (0, 8 * columns - vector.shape[1]))).reshape(n, 8, columns)
+    attend_total = scatter_sum(
+        jnp.concatenate([(part_own + part_peer).reshape(n, share, columns), vector], axis=1).astype(LOW)
+    )
+
+    source = own_x.astype(FLOAT)
+    unit, factor = center(source)
+    mixed = (source + mixed_total + out_bias + narrow_bias).astype(LOW)
+    tokens_gradient = own_g.astype(FLOAT) + factor * (
+        e_total
+        - jnp.mean(e_total, axis=-1, keepdims=True)
+        - unit * jnp.mean(e_total * unit, axis=-1, keepdims=True)
+    )
+
+    narrow_other = swap(narrow_total, "context")
+    wide_other = swap(wide_total, "context")
+    attend_other = swap(attend_total, "context")
+
+    def joined(own, other):
+        both = own.astype(FLOAT) + other.astype(FLOAT)
+        return both.reshape(-1)
+
+    narrow_slope = ordered(narrow_total.T, narrow_other.T, y, 0).astype(FLOAT)
+    wide_slope = ordered(wide_total[:share], wide_other[:share], y, 1).astype(FLOAT)
+    own, far = attend_total[:share], attend_other[:share]
+    projection_slope = ordered(
+        own[:, : 3 * inner].reshape(share, 3, inner), far[:, : 3 * inner].reshape(share, 3, inner), y, 2
+    ).astype(FLOAT)
+    outgoing_slope = ordered(own[:, 3 * inner :].T, far[:, 3 * inner :].T, y, 0).astype(FLOAT)
+    feed_vector = joined(wide_total[share:], wide_other[share:])
+    attend_vector = joined(attend_total[share:], attend_other[share:])
+    across = jnp.concatenate([feed_vector[: 3 * share], attend_vector[: 2 * share]]).astype(LOW)
+    across = across.astype(FLOAT) + swap(across, "tensor").astype(FLOAT)
+    gains = across.reshape(5, share)
+    bias_slope = attend_vector[2 * share : 2 * share + 3 * third].reshape(3, third)
+    unit_slope = feed_vector[3 * share : 3 * share + 2 * units // n]
+    return (
+        mixed.reshape(tokens.shape),
+        tokens_gradient.reshape(tokens.shape),
+        projection_slope,
+        bias_slope,
+        outgoing_slope,
+        gains[2],
+        wide_slope,
+        unit_slope,
+        narrow_slope,
+        gains[2],
+        gains[3],
+        gains[4],
+        gains[0],
+        gains[1],
+    )
+
+
+def body(*arrays):
+    tokens, outgoing, narrowing = arrays[0], arrays[5], arrays[9]
+    fits = (
+        lax.axis_size("context") == 2
+        and lax.axis_size("tensor") == 2
+        and tokens.shape[0] == 1
+        and tokens.shape[1] % BLOCK == 0
+        and outgoing.shape[0] == 6 * HEAD_DIM
+    )
+    return split_body(*arrays) if fits else general_body(*arrays)
+
+
 def solution(mesh):
     return jax.shard_map(
         body,

time: 811 us -> 336 us (0.41)
  waiting for transfers between devices: 325 us -> 71.1 us
  matrix products: 194 us -> 0 us
  blocking collectives: 130 us -> 0 us
  Pallas kernels: 0 us -> 90.6 us
  other arithmetic: 106 us -> 42.2 us
  starting transfers between devices: 0.82 us -> 58.3 us
  local copies, waits for them, and re-layouts: 31.3 us -> 70.1 us
  between operations: 17.6 us -> 1.83 us
    reduce_scatter x6 -> x0, waiting for transfers between devices: 211 us -> none  [the longest x1 71.8 us: body(): lax.psum_scatter(narrowing_slope.astype(jnp.bfloat16), 'fsdp', scatter_di...]
    dot_general x18 -> x0, matrix products: 194 us -> none  [the longest x1 35.6 us: body(): jnp.einsum('qhd,khd->hqk', outer, value_block, preferred_element_type=jnp...]
    pallas_call x0 -> x6, Pallas kernels: none -> 90.6 us  [the longest x1 33.7 us: attention(): pl.pallas_call(attention_kernel, grid_spec=pltpu.PrefetchScalarGridSpec(n...]
    unnamed x2 -> x0, blocking collectives: 76.5 us -> none
    ppermute x0 -> x49, waiting for transfers between devices: none -> 71.1 us  [the longest x16 37.3 us: swap(): return lax.ppermute(value, axis, PAIR)]
    psum x2 -> x0, waiting for transfers between devices: 66.3 us -> none  [the longest x1 37.8 us: body(): lax.psum(owned[0].astype(jnp.bfloat16), 'context').astype(jnp.float32)]
    ppermute x0 -> x49, starting transfers between devices: none -> 58.3 us  [the longest x9 18.8 us: scatter_sum(): total = total + lax.ppermute(piece, 'fsdp', pairs).astype(FLOAT)]
    all_gather x2 -> x0, blocking collectives: 48.3 us -> none  [the longest x1 31.6 us: body(): lax.all_gather(outgoing, 'fsdp', axis=1, tiled=True)]
  transfers between devices with their start and end apart: 14 -> 49, of which waited for: 6 -> 16; matrix products, arithmetic and copies ran while one was open for 38% -> 27% of each run, Pallas kernels for 0% -> 23%
where the time goes in v1:
time: 336 us; the launch traced here: 334 us
  Pallas kernels  90.6 us (27%)
  waiting for transfers between devices  71.1 us (21%)
  local copies, waits for them, and re-layouts  70.1 us (21%)
  starting transfers between devices  58.3 us (17%)
  other arithmetic  42.2 us (13%)
    ppermute x16, waiting for transfers between devices, swap(): return lax.ppermute(value, axis, PAIR)  37.3 us
    pallas_call x1, Pallas kernels, attention(): pl.pallas_call(attention_kernel, grid_spec=pltpu.PrefetchScalarGridSpec(n...  33.7 us
    pallas_call x2, Pallas kernels, feed(): pl.pallas_call(feed_kernel, grid=(rows // BLOCK,), in_specs=[pl.BlockSpec...  30.2 us
    ppermute x9, waiting for transfers between devices, scatter_sum(): total = total + lax.ppermute(piece, 'fsdp', pairs).astype(FLOAT)  27.1 us
    ppermute x9, starting transfers between devices, scatter_sum(): total = total + lax.ppermute(piece, 'fsdp', pairs).astype(FLOAT)  18.8 us
    ppermute x12, starting transfers between devices, ring_gather(): ahead = lax.ppermute(ahead, 'fsdp', forward)  18.5 us
    pallas_call x2, Pallas kernels, finish(): pl.pallas_call(finish_kernel, grid_spec=pltpu.PrefetchScalarGridSpec(num_...  17.9 us
    unnamed x79, local copies, waits for them, and re-layouts  13.4 us
  transfers between devices with their start and end apart: 49, of which 16 were waited for; matrix products, arithmetic and copies ran while one was open for 27% of the time, Pallas kernels for 23%

profile of v1, /device:TPU:0, one launch (start us, length us, event | category | flops | bytes accessed | tf_op | source)
XLA Modules:
  0.0 334.2 jit_solution(6344008104785173420)
XLA Ops:
  1.7 3.1 collective-permute-start.18
  5.6 4.8 %concatenate.98 = bf16[912]{0:T(1024)(128)(2,1)S(1)} concatenate(bf16[96]{0:T(256)(128)(2,1)} %param.26, bf16[96]{0:T(256)(128)(2,1)} %param.27, bf16[96]{0:T(256)(128)(2,1)} %param.28, bf16[96]{0:T(256)(128)(2,1)} %param.29, bf16[96]{0:T(256)(128)(2,1)} %param.21, bf16[96]{0:T(256)(128)(2,1)} %param.25, bf16[144]{0:T(256)(128)(2,1)S(1)} %reshape.470, bf16[192]{0:T(256)(128)(2,1)} %param.23), dimensions={0} | concatenate | bytes 3648 | tf_op jit(solution)/shard_map/concatenate | solution.py:884
  11.1 2.0 collective-permute-start.4
  15.3 2.0 collective-permute-start.11
  23.4 5.7 %multiply_sine_fusion = (f32[2048,8]{1,0:T(8,128)}, f32[2048,8]{1,0:T(8,128)}, f32[2048,8]{1,0:T(8,128)}) fusion(f32[8]{0:T(128)S(1)} %multiply_power_fusion, f32[2048]{0:T(1024)S(1)} %subtract_convert_fusion), kind=kLoop, calls=%fused_computation.32 | loop fusion | flops 32768 | bytes 204832 | tf_op jit(solution)/shard_map/sin | solution.py:941
  30.7 4.8 %concatenate.102.left = f32[2048,128]{1,0:T(8,128)} concatenate(f32[2048,8]{1,0:T(8,128)} %get-tuple-element.195, f32[2048,8]{1,0:T(8,128)S(1)} %broadcast_in_dim.154, f32[2048,48]{1,0:T(8,128)} %broadcast_in_dim.155, f32[2048,8]{1,0:T(8,128)} %get-tuple-element.195, f32[2048,8]{1,0:T(8,128)S(1)} %broadcast_in_dim.154, f32[2048,48]{1,0:T(8,128)} %broadcast_in_dim.155), dimensions={1} | concatenate | bytes 2097152 | tf_op jit(solution)/shard_map/concatenate | solution.py:947
  35.5 4.9 %concatenate.103.right = f32[2048,128]{1,0:T(8,128)} concatenate(f32[2048,8]{1,0:T(8,128)S(1)} %broadcast_in_dim.154, f32[2048,8]{1,0:T(8,128)} %get-tuple-element.194, f32[2048,48]{1,0:T(8,128)} %broadcast_in_dim.155, f32[2048,8]{1,0:T(8,128)S(1)} %broadcast_in_dim.154, f32[2048,8]{1,0:T(8,128)} %get-tuple-element.194, f32[2048,48]{1,0:T(8,128)} %broadcast_in_dim.155), dimensions={1} | concatenate | bytes 2097152 | tf_op jit(solution)/shard_map/concatenate | solution.py:948
  41.4 6.1 %concatenate.101.cos = f32[2048,128]{1,0:T(8,128)} concatenate(f32[2048,8]{1,0:T(8,128)} %get-tuple-element.196, f32[2048,8]{1,0:T(8,128)} %get-tuple-element.196, f32[2048,48]{1,0:T(8,128)} %broadcast_in_dim.153, f32[2048,8]{1,0:T(8,128)} %get-tuple-element.196, f32[2048,8]{1,0:T(8,128)} %get-tuple-element.196, f32[2048,48]{1,0:T(8,128)} %broadcast_in_dim.153), dimensions={1} | concatenate | bytes 2097152 | tf_op jit(solution)/shard_map/concatenate | solution.py:946
  49.2 1.9 collective-permute-start.2
  54.4 1.6 collective-permute-start.20
  56.6 1.6 bitcast_dynamic-update-slice_fusion.6
  58.2 1.6 collective-permute-start.13
  59.8 1.6 bitcast_dynamic-update-slice_fusion.5
  65.5 1.6 collective-permute-start.7
  68.5 1.9 collective-permute-start.22
  71.6 1.7 collective-permute-start.15
  74.1 1.7 collective-permute-start.16
  75.8 1.6 bitcast_dynamic-update-slice_fusion.11
  78.5 1.7 collective-permute-start.9
  81.8 2.4 collective-permute-done.8
  84.9 1.6 bitcast_dynamic-update-slice_fusion.2
  86.5 1.7 collective-permute-start.10
  95.9 15.0 %feed.2 = (bf16[1024,768]{1,0:T(8,128)(2,1)S(1)}, bf16[1024,768]{1,0:T(8,128)(2,1)S(1)}, f32[768,768]{1,0:T(8,128)}, f32[768,768]{1,0:T(8,128)}, f32[8,768]{1,0:T(8,128)S(1)}) custom-call(bf16[1024,768]{1,0:T(8,128)(2,1)} %bitcast.151, bf16[1024,768]{1,0:T(8,128)(2,1)} %bitcast.154, f32[1,768]{1,0:T(1,128)S(1)} %reshape.487.gain, ...), custom_call_target="tpu_custom_call" | custom-call | flops 7247757312 | bytes 9437184 | tf_op jit(solution)/shard_map/feed/pallas_call | solution.py:664
  115.8 1.9 pad_maximum_fusion
  117.7 15.2 %feed.3 = (bf16[1024,768]{1,0:T(8,128)(2,1)S(1)}, bf16[1024,768]{1,0:T(8,128)(2,1)S(1)}, f32[768,768]{1,0:T(8,128)}, f32[768,768]{1,0:T(8,128)}, f32[8,768]{1,0:T(8,128)S(1)}) custom-call(bf16[1024,768]{1,0:T(8,128)(2,1)} %get-tuple-element.204.peer_x.x_ref, bf16[1024,768]{1,0:T(8,128)(2,1)} %get-tuple-element.205.peer_g.g_ref, f32[1,768]{1,0:T(1,128)S(1)} %reshape.487.gain, ...), custom_call_target="tpu_custom_call" | custom-call | flops 7247757312 | bytes 9437184 | tf_op jit(solution)/shard_map/feed/pallas_call | solution.py:664
  133.0 3.1 add_convert_fusion
  139.3 2.0 add_convert_fusion.1
  146.3 8.8 %prepare.1 = (bf16[2048,192]{1,0:T(8,128)(2,1)S(1)}, bf16[2048,192]{1,0:T(8,128)(2,1)S(1)}, bf16[2048,192]{1,0:T(8,128)(2,1)S(1)}, bf16[2048,192]{1,0:T(8,128)(2,1)S(1)}) custom-call(s32[1]{0:T(128)} %bitcast.place, bf16[1024,768]{1,0:T(8,128)(2,1)S(1)} %bitcast.153, bf16[1024,768]{1,0:T(8,128)(2,1)S(1)} %copy-done.10, bf16[1024,768]{1,0:T(8,128)(2,1)S(1)} %bitcast.156, ...), custom_call_target="tpu_custom_call" | custom-call | flops 2415919104 | bytes 12582912 | tf_op jit(solution)/shard_map/prepare/pallas_call | solution.py:436
  155.2 33.7 %attention.1 = (bf16[2048,192]{1,0:T(8,128)(2,1)S(1)}, bf16[2048,576]{1,0:T(8,128)(2,1)}) custom-call(s32[8]{0:T(128)S(1)} %and_select_fusion.first, bf16[2048,192]{1,0:T(8,128)(2,1)S(1)} %get-tuple-element.38.q_ref, bf16[2048,192]{1,0:T(8,128)(2,1)S(1)} %get-tuple-element.39.k_ref, bf16[2048,192]{1,0:T(8,128)(2,1)S(1)} %get-tuple-element.40.v_ref, ...), custom_call_target="tpu_custom_call" | custom-call | flops 16106127360 | bytes 7864320 | tf_op jit(solution)/shard_map/attention/pallas_call | solution.py:580
  188.9 8.6 %finish.2 = (bf16[1024,768]{1,0:T(8,128)(2,1)S(1)}, bf16[1024,768]{1,0:T(8,128)(2,1)S(1)}, f32[768,768]{1,0:T(8,128)}, f32[8,768]{1,0:T(8,128)S(1)}) custom-call(s32[1]{0:T(128)} %bitcast.place, bf16[1024,768]{1,0:T(8,128)(2,1)} %bitcast.152, bf16[1024,768]{1,0:T(8,128)(2,1)} %bitcast.155, bf16[2048,192]{1,0:T(8,128)(2,1)S(1)} %get-tuple-element.42.heads_ref, ...), custom_call_target="tpu_custom_call" | custom-call | flops 2415919104 | bytes 9437184 | tf_op jit(solution)/shard_map/finish/pallas_call | solution.py:755
  198.7 9.2 %finish.3 = (bf16[1024,768]{1,0:T(8,128)(2,1)S(1)}, bf16[1024,768]{1,0:T(8,128)(2,1)S(1)}, f32[768,768]{1,0:T(8,128)}, f32[8,768]{1,0:T(8,128)S(1)}) custom-call(s32[1]{0:T(128)S(6)} %sub.155.place, bf16[1024,768]{1,0:T(8,128)(2,1)} %get-tuple-element.204.peer_x.x_ref, bf16[1024,768]{1,0:T(8,128)(2,1)} %get-tuple-element.205.peer_g.g_ref, ...), custom_call_target="tpu_custom_call" | custom-call | flops 2415919104 | bytes 9437184 | tf_op jit(solution)/shard_map/finish/pallas_call | solution.py:755
  208.6 2.6 add_convert_fusion.2
  211.2 1.7 collective-permute-start.33
  217.4 8.5 %collective-permute-start.45 = (bf16[96,768]{1,0:T(8,128)(2,1)S(1)}, bf16[96,768]{1,0:T(8,128)(2,1)S(1)}, u32[]{:S(2)}, u32[]{:S(2)}) collective-permute-start(bf16[96,768]{1,0:T(8,128)(2,1)S(1)} %get-tuple-element.172), channel_id=1, source_target_pairs={{0,8},{4,12},{8,16},{12,20},{16,24},{20,28},{24,0},{28,4},{1,9},{5... | collective-permute-start | bytes 442376 | tf_op jit(solution)/shard_map/ppermute | solution.py:837
  227.4 6.0 %collective-permute-start.47 = (bf16[96,768]{1,0:T(8,128)(2,1)S(1)}, bf16[96,768]{1,0:T(8,128)(2,1)S(1)}, u32[]{:S(2)}, u32[]{:S(2)}) collective-permute-start(bf16[96,768]{1,0:T(8,128)(2,1)S(1)} %get-tuple-element.173), channel_id=1, source_target_pairs={{0,24},{4,28},{8,0},{12,4},{16,8},{20,12},{24,16},{28,20},{1,25},{... | collective-permute-start | bytes 442376 | tf_op jit(solution)/shard_map/ppermute | solution.py:837
  235.3 3.8 %collective-permute-done.47 = bf16[96,768]{1,0:T(8,128)(2,1)S(1)} collective-permute-done((bf16[96,768]{1,0:T(8,128)(2,1)S(1)}, bf16[96,768]{1,0:T(8,128)(2,1)S(1)}, u32[]{:S(2)}, u32[]{:S(2)}) %collective-permute-start.47) | collective-permute-done | bytes 147488 | tf_op jit(solution)/shard_map/ppermute | solution.py:837
  239.1 1.8 collective-permute-start.39
  245.6 2.4 collective-permute-done.39
  248.0 10.7 %collective-permute-done.40 = bf16[104,768]{1,0:T(8,128)(2,1)S(1)} collective-permute-done((bf16[104,768]{1,0:T(8,128)(2,1)S(1)}, bf16[104,768]{1,0:T(8,128)(2,1)S(1)}, u32[]{:S(2)}, u32[]{:S(2)}) %collective-permute-start.40) | collective-permute-done | bytes 159776 | tf_op jit(solution)/shard_map/ppermute | solution.py:837
  260.4 6.9 %collective-permute-done.35 = bf16[104,768]{1,0:T(8,128)(2,1)S(1)} collective-permute-done((bf16[104,768]{1,0:T(8,128)(2,1)S(1)}, bf16[104,768]{1,0:T(8,128)(2,1)S(1)}, u32[]{:S(2)}, u32[]{:S(2)}) %collective-permute-start.35) | collective-permute-done | bytes 159776 | tf_op jit(solution)/shard_map/ppermute | solution.py:837
  268.8 1.8 collective-permute-done.36
  273.7 33.5 %collective-permute-done.42 = bf16[104,768]{1,0:T(8,128)(2,1)S(1)} collective-permute-done((bf16[104,768]{1,0:T(8,128)(2,1)S(1)}, bf16[104,768]{1,0:T(8,128)(2,1)S(1)}, u32[]{:S(2)}, u32[]{:S(2)}) %collective-permute-start.42) | collective-permute-done | bytes 159776 | tf_op jit(solution)/shard_map/ppermute | solution.py:796
  308.7 3.8 %collective-permute-done.37 = bf16[104,768]{1,0:T(8,128)(2,1)S(1)} collective-permute-done((bf16[104,768]{1,0:T(8,128)(2,1)S(1)}, bf16[104,768]{1,0:T(8,128)(2,1)S(1)}, u32[]{:S(2)}, u32[]{:S(2)}) %collective-permute-start.37) | collective-permute-done | bytes 159776 | tf_op jit(solution)/shard_map/ppermute | solution.py:796
  314.9 2.7 add_convert_fusion.3
  320.1 2.1 copy.163
  322.9 1.7 add_convert_fusion.5
  326.2 1.9 convert_reduce_fusion
  329.6 4.1 %fusion.10 = (f32[1,1024,768]{2,1,0:T(8,128)}, bf16[1,1024,768]{2,1,0:T(8,128)(2,1)}) fusion(bf16[1,1024,768]{2,1,0:T(8,128)(2,1)S(1)} %copy-done.4, bf16[1,1024,768]{2,1,0:T(8,128)(2,1)S(1)} %copy-done.7, bf16[1,512,768]{2,1,0:T(8,128)(2,1)S(1)} %bitcast.167, bf16[1,512,768]{2,1,0:T(8,128)(2,1)S(1)} %bitcast.166, f32[1024]{0:T(1024)S(1)} %broadcast_multiply_fusion, ...), kind=kLoop, calls=%fused_computation.16 | loop fusion | flops 16515072 | bytes 11032576 | tf_op jit(solution)/shard_map/add | solution.py:1024
  (301 shorter events, 81.2 us)
Async XLA Ops:
  1.7 46.8 %collective-permute-start.18 = (bf16[96,768]{1,0:T(8,128)(2,1)S(1)}, bf16[96,768]{1,0:T(8,128)(2,1)S(1)}, u32[]{:S(2)}, u32[]{:S(2)}) collective-permute-start(bf16[96,768]{1,0:T(8,128)(2,1)S(1)} %dynamic-slice_bitcast_fusion.12), channel_id=1, source_target_pairs={{0,8},{8,16},{16,24},{24,28},{28,20},{20,12},{12,4},{4,0},{1,9},{9... | collective-permute-start | bytes 442376 | tf_op jit(solution)/shard_map/ppermute | solution.py:815
  4.7 44.4 %collective-permute-start.19 = (bf16[96,768]{1,0:T(8,128)(2,1)S(1)}, bf16[96,768]{1,0:T(8,128)(2,1)}, u32[]{:S(2)}, u32[]{:S(2)}) collective-permute-start(bf16[96,768]{1,0:T(8,128)(2,1)S(1)} %dynamic-slice_bitcast_fusion.12), channel_id=1, source_target_pairs={{8,0},{16,8},{24,16},{28,24},{20,28},{12,20},{4,12},{0,4},{9,1},{1... | collective-permute-start | bytes 442376 | tf_op jit(solution)/shard_map/ppermute | solution.py:818
  11.1 45.0 %collective-permute-start.4 = (bf16[104,768]{1,0:T(8,128)(2,1)}, bf16[104,768]{1,0:T(8,128)(2,1)}, u32[]{:S(2)}, u32[]{:S(2)}) collective-permute-start(bf16[104,768]{1,0:T(8,128)(2,1)} %pad_maximum_fusion.4), channel_id=1, source_target_pairs={{0,8},{8,16},{16,24},{24,28},{28,20},{20,12},{12,4},{4,0},{1,9},{9... | collective-permute-start | bytes 479240 | tf_op jit(solution)/shard_map/ppermute | solution.py:815
  13.1 45.1 %collective-permute-start.5 = (bf16[104,768]{1,0:T(8,128)(2,1)}, bf16[104,768]{1,0:T(8,128)(2,1)}, u32[]{:S(2)}, u32[]{:S(2)}) collective-permute-start(bf16[104,768]{1,0:T(8,128)(2,1)} %pad_maximum_fusion.4), channel_id=1, source_target_pairs={{8,0},{16,8},{24,16},{28,24},{20,28},{12,20},{4,12},{0,4},{9,1},{1... | collective-permute-start | bytes 479240 | tf_op jit(solution)/shard_map/ppermute | solution.py:818
  15.3 37.4 %collective-permute-start.11 = (bf16[96,768]{0,1:T(8,128)(2,1)}, bf16[96,768]{0,1:T(8,128)(2,1)}, u32[]{:S(2)}, u32[]{:S(2)}) collective-permute-start(bf16[96,768]{0,1:T(8,128)(2,1)} %get-tuple-element.185), channel_id=1, source_target_pairs={{0,8},{8,16},{16,24},{24,28},{28,20},{20,12},{12,4},{4,0},{1,9},{9... | collective-permute-start | bytes 442376 | tf_op jit(solution)/shard_map/ppermute | solution.py:815
  48.5 5.9 %collective-permute-start.12 = (bf16[96,768]{0,1:T(8,128)(2,1)}, bf16[96,768]{0,1:T(8,128)(2,1)S(1)}, u32[]{:S(2)}, u32[]{:S(2)}) collective-permute-start(bf16[96,768]{0,1:T(8,128)(2,1)} %get-tuple-element.185), channel_id=1, source_target_pairs={{8,0},{16,8},{24,16},{28,24},{20,28},{12,20},{4,12},{0,4},{9,1},{1... | collective-permute-start | bytes 442376 | tf_op jit(solution)/shard_map/ppermute | solution.py:818
  49.2 46.2 %collective-permute-start.2 = (bf16[512,768]{1,0:T(8,128)(2,1)}, bf16[512,768]{1,0:T(8,128)(2,1)S(1)}, u32[]{:S(2)}, u32[]{:S(2)}) collective-permute-start(bf16[512,768]{1,0:T(8,128)(2,1)} %dynamic-slice_bitcast_fusion), channel_id=1, source_target_pairs={{0,2},{2,0},{1,3},{3,1},{4,6},{6,4},{5,7},{7,5},{8,10},{10,8},{9,1... | collective-permute-start | bytes 2359304 | tf_op jit(solution)/shard_map/ppermute | solution.py:796
  52.7 42.8 %collective-permute-start = (bf16[512,768]{1,0:T(8,128)(2,1)}, bf16[512,768]{1,0:T(8,128)(2,1)}, u32[]{:S(2)}, u32[]{:S(2)}) collective-permute-start(bf16[512,768]{1,0:T(8,128)(2,1)} %dynamic-slice_bitcast_fusion.1), channel_id=1, source_target_pairs={{0,2},{2,0},{1,3},{3,1},{4,6},{6,4},{5,7},{7,5},{8,10},{10,8},{9,1... | collective-permute-start | bytes 2359304 | tf_op jit(solution)/shard_map/ppermute | solution.py:796
  54.4 7.0 %collective-permute-start.20 = (bf16[96,768]{1,0:T(8,128)(2,1)}, bf16[96,768]{1,0:T(8,128)(2,1)S(1)}, u32[]{:S(2)}, u32[]{:S(2)}) collective-permute-start(bf16[96,768]{1,0:T(8,128)(2,1)} %copy-done.31), channel_id=1, source_target_pairs={{0,8},{8,16},{16,24},{24,28},{28,20},{20,12},{12,4},{4,0},{1,9},{9... | collective-permute-start | bytes 442376 | tf_op jit(solution)/shard_map/ppermute | solution.py:815
  56.1 7.3 %collective-permute-start.21 = (bf16[96,768]{1,0:T(8,128)(2,1)}, bf16[96,768]{1,0:T(8,128)(2,1)S(1)}, u32[]{:S(2)}, u32[]{:S(2)}) collective-permute-start(bf16[96,768]{1,0:T(8,128)(2,1)} %collective-permute-done.19), channel_id=1, source_target_pairs={{8,0},{16,8},{24,16},{28,24},{20,28},{12,20},{4,12},{0,4},{9,1},{1... | collective-permute-start | bytes 442376 | tf_op jit(solution)/shard_map/ppermute | solution.py:818
  58.2 7.3 %collective-permute-start.13 = (bf16[96,768]{0,1:T(8,128)(2,1)}, bf16[96,768]{0,1:T(8,128)(2,1)S(1)}, u32[]{:S(2)}, u32[]{:S(2)}) collective-permute-start(bf16[96,768]{0,1:T(8,128)(2,1)} %collective-permute-done.11), channel_id=1, source_target_pairs={{0,8},{8,16},{16,24},{24,28},{28,20},{20,12},{12,4},{4,0},{1,9},{9... | collective-permute-start | bytes 442376 | tf_op jit(solution)/shard_map/ppermute | solution.py:815
  61.4 7.1 %collective-permute-start.14 = (bf16[96,768]{0,1:T(8,128)(2,1)S(1)}, bf16[96,768]{0,1:T(8,128)(2,1)S(1)}, u32[]{:S(2)}, u32[]{:S(2)}) collective-permute-start(bf16[96,768]{0,1:T(8,128)(2,1)S(1)} %collective-permute-done.12), channel_id=1, source_target_pairs={{8,0},{16,8},{24,16},{28,24},{20,28},{12,20},{4,12},{0,4},{9,1},{1... | collective-permute-start | bytes 442376 | tf_op jit(solution)/shard_map/ppermute | solution.py:818
  63.4 7.1 %collective-permute-start.6 = (bf16[104,768]{1,0:T(8,128)(2,1)}, bf16[104,768]{1,0:T(8,128)(2,1)S(1)}, u32[]{:S(2)}, u32[]{:S(2)}) collective-permute-start(bf16[104,768]{1,0:T(8,128)(2,1)} %collective-permute-done.4), channel_id=1, source_target_pairs={{0,8},{8,16},{16,24},{24,28},{28,20},{20,12},{12,4},{4,0},{1,9},{9... | collective-permute-start | bytes 479240 | tf_op jit(solution)/shard_map/ppermute | solution.py:815
  65.5 6.2 %collective-permute-start.7 = (bf16[104,768]{1,0:T(8,128)(2,1)}, bf16[104,768]{1,0:T(8,128)(2,1)S(1)}, u32[]{:S(2)}, u32[]{:S(2)}) collective-permute-start(bf16[104,768]{1,0:T(8,128)(2,1)} %collective-permute-done.5), channel_id=1, source_target_pairs={{8,0},{16,8},{24,16},{28,24},{20,28},{12,20},{4,12},{0,4},{9,1},{1... | collective-permute-start | bytes 479240 | tf_op jit(solution)/shard_map/ppermute | solution.py:818
  68.5 5.6 %collective-permute-start.22 = (bf16[96,768]{1,0:T(8,128)(2,1)S(1)}, bf16[96,768]{1,0:T(8,128)(2,1)}, u32[]{:S(2)}, u32[]{:S(2)}) collective-permute-start(bf16[96,768]{1,0:T(8,128)(2,1)S(1)} %collective-permute-done.20), channel_id=1, source_target_pairs={{0,8},{8,16},{16,24},{24,28},{28,20},{20,12},{12,4},{4,0},{1,9},{9... | collective-permute-start | bytes 442376 | tf_op jit(solution)/shard_map/ppermute | solution.py:815
  70.5 6.9 %collective-permute-start.23 = (bf16[96,768]{1,0:T(8,128)(2,1)}, bf16[96,768]{1,0:T(8,128)(2,1)S(1)}, u32[]{:S(2)}, u32[]{:S(2)}) collective-permute-start(bf16[96,768]{1,0:T(8,128)(2,1)} %copy-done.32), channel_id=1, source_target_pairs={{8,0},{16,8},{24,16},{28,24},{20,28},{12,20},{4,12},{0,4},{9,1},{1... | collective-permute-start | bytes 442376 | tf_op jit(solution)/shard_map/ppermute | solution.py:818
  71.6 6.8 %collective-permute-start.15 = (bf16[96,768]{0,1:T(8,128)(2,1)S(1)}, bf16[96,768]{0,1:T(8,128)(2,1)S(1)}, u32[]{:S(2)}, u32[]{:S(2)}) collective-permute-start(bf16[96,768]{0,1:T(8,128)(2,1)S(1)} %collective-permute-done.13), channel_id=1, source_target_pairs={{0,8},{8,16},{16,24},{24,28},{28,20},{20,12},{12,4},{4,0},{1,9},{9... | collective-permute-start | bytes 442376 | tf_op jit(solution)/shard_map/ppermute | solution.py:815
  74.1 6.2 %collective-permute-start.16 = (bf16[96,768]{0,1:T(8,128)(2,1)S(1)}, bf16[96,768]{0,1:T(8,128)(2,1)S(1)}, u32[]{:S(2)}, u32[]{:S(2)}) collective-permute-start(bf16[96,768]{0,1:T(8,128)(2,1)S(1)} %collective-permute-done.14), channel_id=1, source_target_pairs={{8,0},{16,8},{24,16},{28,24},{20,28},{12,20},{4,12},{0,4},{9,1},{1... | collective-permute-start | bytes 442376 | tf_op jit(solution)/shard_map/ppermute | solution.py:818
  77.4 6.8 %collective-permute-start.8 = (bf16[104,768]{1,0:T(8,128)(2,1)S(1)}, bf16[104,768]{1,0:T(8,128)(2,1)}, u32[]{:S(2)}, u32[]{:S(2)}) collective-permute-start(bf16[104,768]{1,0:T(8,128)(2,1)S(1)} %collective-permute-done.6), channel_id=1, source_target_pairs={{0,8},{8,16},{16,24},{24,28},{28,20},{20,12},{12,4},{4,0},{1,9},{9... | collective-permute-start | bytes 479240 | tf_op jit(solution)/shard_map/ppermute | solution.py:815
  78.5 8.1 %collective-permute-start.9 = (bf16[104,768]{1,0:T(8,128)(2,1)S(1)}, bf16[104,768]{1,0:T(8,128)(2,1)S(1)}, u32[]{:S(2)}, u32[]{:S(2)}) collective-permute-start(bf16[104,768]{1,0:T(8,128)(2,1)S(1)} %collective-permute-done.7), channel_id=1, source_target_pairs={{8,0},{16,8},{24,16},{28,24},{20,28},{12,20},{4,12},{0,4},{9,1},{1... | collective-permute-start | bytes 479240 | tf_op jit(solution)/shard_map/ppermute | solution.py:818
  80.3 8.5 %collective-permute-start.24 = (bf16[96,768]{1,0:T(8,128)(2,1)}, bf16[96,768]{1,0:T(8,128)(2,1)}, u32[]{:S(2)}, u32[]{:S(2)}) collective-permute-start(bf16[96,768]{1,0:T(8,128)(2,1)} %collective-permute-done.22), channel_id=1, source_target_pairs={{0,8},{8,16},{16,24},{24,28},{28,20},{20,12},{12,4},{4,0},{1,9},{9... | collective-permute-start | bytes 442376 | tf_op jit(solution)/shard_map/ppermute | solution.py:815
  84.2 6.2 %collective-permute-start.17 = (bf16[96,768]{0,1:T(8,128)(2,1)S(1)}, bf16[96,768]{0,1:T(8,128)(2,1)S(1)}, u32[]{:S(2)}, u32[]{:S(2)}) collective-permute-start(bf16[96,768]{0,1:T(8,128)(2,1)S(1)} %collective-permute-done.15), channel_id=1, source_target_pairs={{0,8},{8,16},{16,24},{24,28},{28,20},{20,12},{12,4},{4,0},{1,9},{9... | collective-permute-start | bytes 442376 | tf_op jit(solution)/shard_map/ppermute | solution.py:815
  86.5 5.5 %collective-permute-start.10 = (bf16[104,768]{1,0:T(8,128)(2,1)}, bf16[104,768]{1,0:T(8,128)(2,1)S(1)}, u32[]{:S(2)}, u32[]{:S(2)}) collective-permute-start(bf16[104,768]{1,0:T(8,128)(2,1)} %collective-permute-done.8), channel_id=1, source_target_pairs={{0,8},{8,16},{16,24},{24,28},{28,20},{20,12},{12,4},{4,0},{1,9},{9... | collective-permute-start | bytes 479240 | tf_op jit(solution)/shard_map/ppermute | solution.py:815
  95.4 18.8 %collective-permute-start.3 = (bf16[512,768]{1,0:T(8,128)(2,1)S(1)}, bf16[512,768]{1,0:T(8,128)(2,1)S(1)}, u32[]{:S(2)}, u32[]{:S(2)}) collective-permute-start(bf16[512,768]{1,0:T(8,128)(2,1)S(1)} %collective-permute-done.2), channel_id=1, source_target_pairs={{0,1},{1,0},{2,3},{3,2},{4,5},{5,4},{6,7},{7,6},{8,9},{9,8},{10,11... | collective-permute-start | bytes 2359304 | tf_op jit(solution)/shard_map/ppermute | solution.py:796
  95.5 18.8 %collective-permute-start.1 = (bf16[512,768]{1,0:T(8,128)(2,1)}, bf16[512,768]{1,0:T(8,128)(2,1)}, u32[]{:S(2)}, u32[]{:S(2)}) collective-permute-start(bf16[512,768]{1,0:T(8,128)(2,1)} %collective-permute-done), channel_id=1, source_target_pairs={{0,1},{1,0},{2,3},{3,2},{4,5},{5,4},{6,7},{7,6},{8,9},{9,8},{10,11... | collective-permute-start | bytes 2359304 | tf_op jit(solution)/shard_map/ppermute | solution.py:796
  137.0 78.7 %collective-permute-start.44 = (bf16[4,96,768]{2,1,0:T(8,128)(2,1)}, bf16[4,96,768]{2,1,0:T(8,128)(2,1)}, u32[]{:S(2)}, u32[]{:S(2)}) collective-permute-start(bf16[4,96,768]{2,1,0:T(8,128)(2,1)} %dynamic-slice_bitcast_fusion.2), channel_id=1, source_target_pairs={{0,4},{4,0},{8,12},{12,8},{16,20},{20,16},{24,28},{28,24},{1,5},{5... | collective-permute-start | bytes 1769480 | tf_op jit(solution)/shard_map/ppermute | solution.py:831
  142.3 83.6 %collective-permute-start.38 = (bf16[4,104,768]{2,1,0:T(8,128)(2,1)}, bf16[4,104,768]{2,1,0:T(8,128)(2,1)}, u32[]{:S(2)}, u32[]{:S(2)}) collective-permute-start(bf16[4,104,768]{2,1,0:T(8,128)(2,1)} %fusion.16), channel_id=1, source_target_pairs={{0,4},{4,0},{8,12},{12,8},{16,20},{20,16},{24,28},{28,24},{1,5},{5... | collective-permute-start | bytes 1916936 | tf_op jit(solution)/shard_map/ppermute | solution.py:831
  211.2 16.2 %collective-permute-start.33 = (bf16[4,104,768]{2,1,0:T(8,128)(2,1)S(1)}, bf16[4,104,768]{2,1,0:T(8,128)(2,1)S(1)}, u32[]{:S(2)}, u32[]{:S(2)}) collective-permute-start(bf16[4,104,768]{2,1,0:T(8,128)(2,1)S(1)} %fusion.20), channel_id=1, source_target_pairs={{0,4},{4,0},{8,12},{12,8},{16,20},{20,16},{24,28},{28,24},{1,5},{5... | collective-permute-start | bytes 1916936 | tf_op jit(solution)/shard_map/ppermute | solution.py:831
  212.9 28.1 %collective-permute-start.26 = (bf16[512,768]{1,0:T(8,128)(2,1)S(1)}, bf16[512,768]{1,0:T(8,128)(2,1)S(1)}, u32[]{:S(2)}, u32[]{:S(2)}) collective-permute-start(bf16[512,768]{1,0:T(8,128)(2,1)S(1)} %constant_dynamic-slice_fusion.2), channel_id=1, source_target_pairs={{0,1},{1,0},{2,3},{3,2},{4,5},{5,4},{6,7},{7,6},{8,9},{9,8},{10,11... | collective-permute-start | bytes 2359304 | tf_op jit(solution)/shard_map/ppermute | solution.py:796
  215.6 28.0 %collective-permute-start.30 = (bf16[512,768]{1,0:T(8,128)(2,1)S(1)}, bf16[512,768]{1,0:T(8,128)(2,1)S(1)}, u32[]{:S(2)}, u32[]{:S(2)}) collective-permute-start(bf16[512,768]{1,0:T(8,128)(2,1)S(1)} %constant_dynamic-slice_fusion), channel_id=1, source_target_pairs={{0,1},{1,0},{2,3},{3,2},{4,5},{5,4},{6,7},{7,6},{8,9},{9,8},{10,11... | collective-permute-start | bytes 2359304 | tf_op jit(solution)/shard_map/ppermute | solution.py:796
  217.4 16.4 %collective-permute-start.45 = (bf16[96,768]{1,0:T(8,128)(2,1)S(1)}, bf16[96,768]{1,0:T(8,128)(2,1)S(1)}, u32[]{:S(2)}, u32[]{:S(2)}) collective-permute-start(bf16[96,768]{1,0:T(8,128)(2,1)S(1)} %get-tuple-element.172), channel_id=1, source_target_pairs={{0,8},{4,12},{8,16},{12,20},{16,24},{20,28},{24,0},{28,4},{1,9},{5... | collective-permute-start | bytes 442376 | tf_op jit(solution)/shard_map/ppermute | solution.py:837
  225.9 9.4 %collective-permute-start.46 = (bf16[96,768]{1,0:T(8,128)(2,1)S(1)}, bf16[96,768]{1,0:T(8,128)(2,1)S(1)}, u32[]{:S(2)}, u32[]{:S(2)}) collective-permute-start(bf16[96,768]{1,0:T(8,128)(2,1)S(1)} %get-tuple-element.174), channel_id=1, source_target_pairs={{0,16},{4,20},{8,24},{12,28},{16,0},{20,4},{24,8},{28,12},{1,17},{... | collective-permute-start | bytes 442376 | tf_op jit(solution)/shard_map/ppermute | solution.py:837
  227.4 11.7 %collective-permute-start.47 = (bf16[96,768]{1,0:T(8,128)(2,1)S(1)}, bf16[96,768]{1,0:T(8,128)(2,1)S(1)}, u32[]{:S(2)}, u32[]{:S(2)}) collective-permute-start(bf16[96,768]{1,0:T(8,128)(2,1)S(1)} %get-tuple-element.173), channel_id=1, source_target_pairs={{0,24},{4,28},{8,0},{12,4},{16,8},{20,12},{24,16},{28,20},{1,25},{... | collective-permute-start | bytes 442376 | tf_op jit(solution)/shard_map/ppermute | solution.py:837
  233.7 89.1 %collective-permute-start.25 = (bf16[512,768]{1,0:T(8,128)(2,1)}, bf16[512,768]{1,0:T(8,128)(2,1)}, u32[]{:S(2)}, u32[]{:S(2)}) collective-permute-start(bf16[512,768]{1,0:T(8,128)(2,1)} %constant_dynamic-slice_fusion.3), channel_id=1, source_target_pairs={{0,1},{1,0},{2,3},{3,2},{4,5},{5,4},{6,7},{7,6},{8,9},{9,8},{10,11... | collective-permute-start | bytes 2359304 | tf_op jit(solution)/shard_map/ppermute | solution.py:796
  235.3 79.6 %collective-permute-start.29 = (bf16[512,768]{1,0:T(8,128)(2,1)}, bf16[512,768]{1,0:T(8,128)(2,1)}, u32[]{:S(2)}, u32[]{:S(2)}) collective-permute-start(bf16[512,768]{1,0:T(8,128)(2,1)} %constant_dynamic-slice_fusion.1), channel_id=1, source_target_pairs={{0,1},{1,0},{2,3},{3,2},{4,5},{5,4},{6,7},{7,6},{8,9},{9,8},{10,11... | collective-permute-start | bytes 2359304 | tf_op jit(solution)/shard_map/ppermute | solution.py:796
  239.1 8.9 %collective-permute-start.39 = (bf16[104,768]{1,0:T(8,128)(2,1)S(1)}, bf16[104,768]{1,0:T(8,128)(2,1)S(1)}, u32[]{:S(2)}, u32[]{:S(2)}) collective-permute-start(bf16[104,768]{1,0:T(8,128)(2,1)S(1)} %get-tuple-element.166), channel_id=1, source_target_pairs={{0,8},{4,12},{8,16},{12,20},{16,24},{20,28},{24,0},{28,4},{1,9},{5... | collective-permute-start | bytes 479240 | tf_op jit(solution)/shard_map/ppermute | solution.py:837
  241.0 17.7 %collective-permute-start.40 = (bf16[104,768]{1,0:T(8,128)(2,1)S(1)}, bf16[104,768]{1,0:T(8,128)(2,1)S(1)}, u32[]{:S(2)}, u32[]{:S(2)}) collective-permute-start(bf16[104,768]{1,0:T(8,128)(2,1)S(1)} %get-tuple-element.168), channel_id=1, source_target_pairs={{0,16},{4,20},{8,24},{12,28},{16,0},{20,4},{24,8},{28,12},{1,17},{... | collective-permute-start | bytes 479240 | tf_op jit(solution)/shard_map/ppermute | solution.py:837
  243.6 15.1 %collective-permute-start.41 = (bf16[104,768]{1,0:T(8,128)(2,1)S(1)}, bf16[104,768]{1,0:T(8,128)(2,1)S(1)}, u32[]{:S(2)}, u32[]{:S(2)}) collective-permute-start(bf16[104,768]{1,0:T(8,128)(2,1)S(1)} %get-tuple-element.167), channel_id=1, source_target_pairs={{0,24},{4,28},{8,0},{12,4},{16,8},{20,12},{24,16},{28,20},{1,25},{... | collective-permute-start | bytes 479240 | tf_op jit(solution)/shard_map/ppermute | solution.py:837
  248.0 10.8 %collective-permute-start.34 = (bf16[104,768]{1,0:T(8,128)(2,1)S(1)}, bf16[104,768]{1,0:T(8,128)(2,1)S(1)}, u32[]{:S(2)}, u32[]{:S(2)}) collective-permute-start(bf16[104,768]{1,0:T(8,128)(2,1)S(1)} %get-tuple-element.169), channel_id=1, source_target_pairs={{0,8},{4,12},{8,16},{12,20},{16,24},{20,28},{24,0},{28,4},{1,9},{5... | collective-permute-start | bytes 479240 | tf_op jit(solution)/shard_map/ppermute | solution.py:837
  258.7 8.6 %collective-permute-start.35 = (bf16[104,768]{1,0:T(8,128)(2,1)S(1)}, bf16[104,768]{1,0:T(8,128)(2,1)S(1)}, u32[]{:S(2)}, u32[]{:S(2)}) collective-permute-start(bf16[104,768]{1,0:T(8,128)(2,1)S(1)} %get-tuple-element.171), channel_id=1, source_target_pairs={{0,16},{4,20},{8,24},{12,28},{16,0},{20,4},{24,8},{28,12},{1,17},{... | collective-permute-start | bytes 479240 | tf_op jit(solution)/shard_map/ppermute | solution.py:837
  258.7 11.9 %collective-permute-start.36 = (bf16[104,768]{1,0:T(8,128)(2,1)S(1)}, bf16[104,768]{1,0:T(8,128)(2,1)S(1)}, u32[]{:S(2)}, u32[]{:S(2)}) collective-permute-start(bf16[104,768]{1,0:T(8,128)(2,1)S(1)} %get-tuple-element.170), channel_id=1, source_target_pairs={{0,24},{4,28},{8,0},{12,4},{16,8},{20,12},{24,16},{28,20},{1,25},{... | collective-permute-start | bytes 479240 | tf_op jit(solution)/shard_map/ppermute | solution.py:837
  258.8 13.4 %collective-permute-start.48 = (bf16[96,768]{1,0:T(8,128)(2,1)S(1)}, bf16[96,768]{1,0:T(8,128)(2,1)S(1)}, u32[]{:S(2)}, u32[]{:S(2)}) collective-permute-start(bf16[96,768]{1,0:T(8,128)(2,1)S(1)} %fusion.32), channel_id=1, source_target_pairs={{0,2},{2,0},{1,3},{3,1},{4,6},{6,4},{5,7},{7,5},{8,10},{10,8},{9,1... | collective-permute-start | bytes 442376 | tf_op jit(solution)/shard_map/ppermute | solution.py:796
  267.3 55.5 %collective-permute-start.27 = (bf16[512,768]{1,0:T(8,128)(2,1)}, bf16[512,768]{1,0:T(8,128)(2,1)}, u32[]{:S(2)}, u32[]{:S(2)}) collective-permute-start(bf16[512,768]{1,0:T(8,128)(2,1)} %add_convert_fusion.6), channel_id=1, source_target_pairs={{0,2},{2,0},{1,3},{3,1},{4,6},{6,4},{5,7},{7,5},{8,10},{10,8},{9,1... | collective-permute-start | bytes 2359304 | tf_op jit(solution)/shard_map/ppermute | solution.py:796
  270.6 44.3 %collective-permute-start.31 = (bf16[512,768]{1,0:T(8,128)(2,1)}, bf16[512,768]{1,0:T(8,128)(2,1)}, u32[]{:S(2)}, u32[]{:S(2)}) collective-permute-start(bf16[512,768]{1,0:T(8,128)(2,1)} %add_convert_fusion.4), channel_id=1, source_target_pairs={{0,2},{2,0},{1,3},{3,1},{4,6},{6,4},{5,7},{7,5},{8,10},{10,8},{9,1... | collective-permute-start | bytes 2359304 | tf_op jit(solution)/shard_map/ppermute | solution.py:796
  272.2 35.0 %collective-permute-start.42 = (bf16[104,768]{1,0:T(8,128)(2,1)S(1)}, bf16[104,768]{1,0:T(8,128)(2,1)S(1)}, u32[]{:S(2)}, u32[]{:S(2)}) collective-permute-start(bf16[104,768]{1,0:T(8,128)(2,1)S(1)} %fusion.26), channel_id=1, source_target_pairs={{0,2},{2,0},{1,3},{3,1},{4,6},{6,4},{5,7},{7,5},{8,10},{10,8},{9,1... | collective-permute-start | bytes 479240 | tf_op jit(solution)/shard_map/ppermute | solution.py:796
  307.2 5.3 %collective-permute-start.37 = (bf16[104,768]{1,0:T(8,128)(2,1)S(1)}, bf16[104,768]{1,0:T(8,128)(2,1)S(1)}, u32[]{:S(2)}, u32[]{:S(2)}) collective-permute-start(bf16[104,768]{1,0:T(8,128)(2,1)S(1)} %fusion.29), channel_id=1, source_target_pairs={{0,2},{2,0},{1,3},{3,1},{4,6},{6,4},{5,7},{7,5},{8,10},{10,8},{9,1... | collective-permute-start | bytes 479240 | tf_op jit(solution)/shard_map/ppermute | solution.py:796
  312.6 9.6 %collective-permute-start.43 = (bf16[480]{0:T(512)(128)(2,1)S(1)}, bf16[480]{0:T(512)(128)(2,1)S(1)}, u32[]{:S(2)}, u32[]{:S(2)}) collective-permute-start(bf16[480]{0:T(512)(128)(2,1)S(1)} %pad_maximum_fusion.5), channel_id=1, source_target_pairs={{0,1},{1,0},{2,3},{3,2},{4,5},{5,4},{6,7},{7,6},{8,9},{9,8},{10,11... | collective-permute-start | bytes 2888 | tf_op jit(solution)/shard_map/ppermute | solution.py:796
  317.6 7.1 %collective-permute-start.32 = (bf16[512,768]{1,0:T(8,128)(2,1)}, bf16[512,768]{1,0:T(8,128)(2,1)S(1)}, u32[]{:S(2)}, u32[]{:S(2)}) collective-permute-start(bf16[512,768]{1,0:T(8,128)(2,1)} %add_convert_fusion.3), channel_id=1, source_target_pairs={{0,1},{1,0},{2,3},{3,2},{4,5},{5,4},{6,7},{7,6},{8,9},{9,8},{10,11... | collective-permute-start | bytes 2359304 | tf_op jit(solution)/shard_map/ppermute | solution.py:796
  (37 other events, 176.1 us)

commit v2 on v0

--- a/solution.py
+++ b/solution.py
@@ -1,6 +1,11 @@
+import functools
+
 import jax
 import jax.numpy as jnp
+import numpy as np
 from jax import lax
+from jax.experimental import pallas as pl
+from jax.experimental.pallas import tpu as pltpu
 from jax.sharding import PartitionSpec as P
 
 HEAD_DIM = 64
@@ -14,12 +19,12 @@
 
 def layout(lengths, index):
     padded = (lengths + TILE - 1) // TILE * TILE
-    finish = jnp.cumsum(padded)
+    labels = jnp.arange(SEQS, dtype=jnp.int32)
+    finish = jnp.sum(jnp.where(labels[:, None] <= labels[None, :], padded[:, None], 0), axis=0)
     before = (index[:, None] >= finish[None, :]).astype(jnp.int32)
     number = jnp.sum(before, axis=1)
     start = jnp.sum(before * padded[None, :], axis=1)
     position = index - start
-    labels = jnp.arange(SEQS, dtype=jnp.int32)
     length = jnp.sum(jnp.where(number[:, None] == labels[None, :], lengths[None, :], 0), axis=1)
     return (number, position, position < length)
 
@@ -82,7 +87,7 @@
     return same | (query_index[:, None] == key_index[None, :])
 
 
-def body(
+def general_body(
     tokens,
     pack_lengths,
     cotangent,
@@ -352,6 +357,1080 @@
     return (mixed, tokens_gradient) + tuple(final)
 
 
+BLOCK = 256
+FLOAT = jnp.float32
+LOW = jnp.bfloat16
+
+
+def nn(left, right):
+    return lax.dot_general(left, right, (((1,), (0,)), ((), ())), preferred_element_type=FLOAT)
+
+
+def nt(left, right):
+    return lax.dot_general(left, right, (((1,), (1,)), ((), ())), preferred_element_type=FLOAT)
+
+
+def tn(left, right):
+    return lax.dot_general(left, right, (((0,), (0,)), ((), ())), preferred_element_type=FLOAT)
+
+
+def center(values):
+    average = jnp.mean(values, axis=-1, keepdims=True)
+    centered = values - average
+    spread = jnp.mean(centered * centered, axis=-1, keepdims=True)
+    factor = lax.rsqrt(spread + epsilon)
+    return centered * factor, factor
+
+
+def widen_lanes(table, times):
+    return jnp.concatenate([table] * times, axis=1)
+
+
+def call(kernel, name, place, steps, inputs, outputs, scratch=(), flops=0):
+    def fixed(rank):
+        return lambda s, place: (0,) * rank
+
+    def spec(shape, block, index):
+        return pl.BlockSpec(shape if block is None else block, fixed(len(shape)) if block is None else index)
+
+    return pl.pallas_call(
+        kernel,
+        grid_spec=pltpu.PrefetchScalarGridSpec(
+            num_scalar_prefetch=1,
+            grid=(steps,),
+            in_specs=[spec(array.shape, block, index) for array, block, index in inputs],
+            out_specs=[spec(shape, block, index) for shape, _, block, index in outputs],
+            scratch_shapes=list(scratch),
+        ),
+        out_shape=[jax.ShapeDtypeStruct(shape, kind) for shape, kind, _, _ in outputs],
+        compiler_params=pltpu.CompilerParams(vmem_limit_bytes=48 << 20),
+        cost_estimate=pl.CostEstimate(flops=1, bytes_accessed=1, transcendentals=0),
+        name=name,
+    )(place, *[array for array, _, _ in inputs])
+
+
+ROWS = 512
+
+
+def rank_two(value):
+    return value.reshape(1, -1)
+
+
+def pick(index, left, right):
+    return jnp.where(index == 0, left, right)
+
+
+def rolled(rows, shift, width):
+    return pltpu.roll(
+        jnp.concatenate([rows, jnp.zeros((rows.shape[0], width - rows.shape[1]), FLOAT)], axis=1), shift, 1
+    )
+
+
+def stacked(rows, width):
+    rows = list(rows) + [jnp.zeros((16 - len(rows), width), FLOAT)]
+    return jnp.concatenate(rows, axis=0).astype(LOW)
+
+
+def pack_attend_kernel(place, project, out, gain, shift, first_bias, second_bias, third, piece):
+    y, me = place[0], place[12]
+    share = project.shape[1]
+    inner = out.shape[1] // 2
+    width = piece.shape[1]
+    parts = []
+    for c in range(3):
+        block = project[c].astype(FLOAT)
+        parts.append(pick(y, block[:, :inner], block[:, inner:]))
+    parts.append(pick(y, out[:, :inner].astype(FLOAT), out[:, inner:].astype(FLOAT)))
+    piece[:share, :] = jnp.concatenate(parts, axis=1).astype(LOW)
+    rows = [rolled(ref[...].astype(FLOAT), me * share, width) for ref in (gain, shift, first_bias, second_bias)]
+    bias = rolled(third[...].astype(FLOAT), me * third.shape[1], 2 * inner)
+    bias = pick(y, bias[:, :inner], bias[:, inner:])
+    bias = jnp.concatenate([bias[c : c + 1] for c in range(3)] + [jnp.zeros((1, width - 3 * inner), FLOAT)], axis=1)
+    piece[share:, :] = stacked([rows[0], rows[1], bias, rows[2], rows[3]], width)
+
+
+def pack_feed_kernel(place, wide, narrow, gain, shift, bias, piece):
+    y, me = place[0], place[12]
+    share = wide.shape[0]
+    units = narrow.shape[1] // 2
+    width = piece.shape[1]
+    piece[:share, :] = pick(y, wide[:, :units].astype(FLOAT), wide[:, units:].astype(FLOAT)).astype(LOW)
+    piece[share : 2 * share, :] = pick(
+        y, narrow[:, :units].astype(FLOAT), narrow[:, units:].astype(FLOAT)
+    ).astype(LOW)
+    rows = [rolled(ref[...].astype(FLOAT), me * share, width) for ref in (gain, shift)]
+    full = rolled(bias[...].astype(FLOAT), me * bias.shape[1], 2 * units)
+    rows.append(pick(y, full[:, :units], full[:, units:]))
+    piece[2 * share :, :] = stacked(rows, width)
+
+
+def place_pieces(place, pieces, first, target, at, share):
+    for spot, piece in enumerate(pieces):
+        rows = pl.ds(pl.multiple_of(at + place[spot + 2] * share, 32), share)
+        target[rows, :] = piece[first : first + share, :]
+
+
+def sum_rows(pieces, first):
+    total = pieces[0][first:, :].astype(FLOAT)
+    for piece in pieces[1:]:
+        total = total + piece[first:, :].astype(FLOAT)
+    return total
+
+
+def prepare_kernel(place, own_x, peer_x, coarse, fine, *refs):
+    pieces, (q_out, k_out, v_out, weight, lines) = refs[:-5], refs[-5:]
+    inner = q_out.shape[1]
+    step = pl.program_id(0)
+    half = pl.num_programs(0) // 2
+    share = weight.shape[0] // 8
+
+    @pl.when(step == 0)
+    def _():
+        place_pieces(place, pieces, 0, weight, 0, share)
+        lines[...] = sum_rows(pieces, share)
+
+    def work(x_ref):
+        unit, _ = center(x_ref[...].astype(FLOAT))
+        normed = (unit * lines[0:1, :] + lines[1:2, :]).astype(LOW)
+        raw = nn(normed, weight[:, : 3 * inner + 64]) + lines[2:3, : 3 * inner + 64]
+        both = raw[:, : 2 * inner]
+        times = 2 * inner // 128
+        tiles = ROWS // TILE
+        block = jnp.where(step < half, place[0] * half + step, (1 - place[0]) * half + step - half)
+        cosine, left, right = turns(place, 13 + block * tiles, tiles, coarse, fine)
+        turned = (
+            both * widen_lanes(cosine, times)
+            + pltpu.roll(both, 2 * inner - ROTARY // 2, 1) * widen_lanes(left, times)
+            + pltpu.roll(both, ROTARY // 2, 1) * widen_lanes(right, times)
+        )
+        q_out[...] = (turned[:, :inner] * HEAD_DIM ** (-0.5)).astype(LOW)
+        k_out[...] = turned[:, inner:].astype(LOW)
+        v_out[...] = raw[:, 2 * inner : 3 * inner].astype(LOW)
+
+    @pl.when(step < half)
+    def _():
+        work(own_x)
+
+    @pl.when(step >= half)
+    def _():
+        work(peer_x)
+
+
+def turning():
+    lane = np.arange(128)
+    rate = 10000.0 ** (-2.0 * (lane % (ROTARY // 2)) / ROTARY) * (lane % HEAD_DIM < ROTARY)
+    coarse = TILE * np.arange(16)[:, None] * rate[None, :]
+    fine = np.arange(TILE)[:, None] * rate[None, :]
+    tables = [np.concatenate([np.cos(t), np.sin(t)], axis=1) for t in (coarse, fine)]
+    return [jnp.asarray(t.astype(np.float32)) for t in tables]
+
+
+def turns(scalars, at, count, coarse, fine):
+    lane = lax.broadcasted_iota(jnp.int32, (1, 128), 1) % HEAD_DIM
+    cosines, sines = [], []
+    for tile in range(count):
+        row = coarse[pl.ds(scalars[at + tile], 1), :]
+        cosines.append(row[:, :128] * fine[:, :128] - row[:, 128:] * fine[:, 128:])
+        sines.append(row[:, 128:] * fine[:, :128] + row[:, :128] * fine[:, 128:])
+    cosine = jnp.concatenate(cosines, axis=0)
+    sine = jnp.concatenate(sines, axis=0)
+    left = jnp.where(lane < ROTARY // 2, -sine, 0.0)
+    right = jnp.where((lane >= ROTARY // 2) & (lane < ROTARY), sine, 0.0)
+    return cosine, left, right
+
+
+def halves(half):
+    def own(s, place):
+        return (jnp.minimum(s, half - 1), 0)
+
+    def peer(s, place):
+        return (jnp.maximum(s - half, 0), 0)
+
+    def target(s, place):
+        return (jnp.where(s < half, place[0] * half + s, (1 - place[0]) * half + s - half), 0)
+
+    return own, peer, target
+
+
+def prepare(place, own_x, peer_x, tables, pieces, inner):
+    rows, width = own_x.shape
+    half = rows // ROWS
+    own, peer, target = halves(half)
+    block = (ROWS, width)
+    thin = ((2 * rows, inner), LOW, (ROWS, inner), target)
+    return call(
+        prepare_kernel,
+        "prepare",
+        place,
+        2 * half,
+        [(own_x, block, own), (peer_x, block, peer)]
+        + [(table, None, None) for table in tables]
+        + [(piece, None, None) for piece in pieces],
+        [thin, thin, thin, ((width, 4 * inner), LOW, None, None), ((16, width), FLOAT, None, None)],
+        flops=4 * rows * width * 3 * inner,
+    )
+
+
+def spread(source, target, head, heads):
+    rows = source.shape[0]
+    for h in range(heads):
+        target[h * rows : (h + 1) * rows, :] = jnp.where(head == h, source, 0.0).astype(LOW)
+
+
+def span(j):
+    return pl.ds(pl.multiple_of(j * BLOCK, BLOCK), BLOCK)
+
+
+def diagonal(raw, block, start, stop, heads):
+    key = lax.broadcasted_iota(jnp.int32, raw.shape, 0) + block * BLOCK
+    itself = widen_lanes(lax.broadcasted_iota(jnp.int32, (1, BLOCK), 1) + block * BLOCK, heads)
+    return jnp.where(((key >= start) & (key < stop)) | (key == itself), raw, -1e30)
+
+
+def forward_kernel(
+    first, q_ref, k_ref, v_ref, start_ref, stop_ref,
+    heads_out, total_out, exact_out,
+    vt, qm, scores, ot,
+):
+    inner = q_ref.shape[1]
+    heads = inner // HEAD_DIM
+    wide = heads * BLOCK
+    step = pl.program_id(0)
+    count = pl.num_programs(0)
+    block = count - 1 - step
+
+    @pl.when(step == 0)
+    def _():
+        ot[...] = jnp.zeros_like(ot)
+
+        @pl.loop(0, count)
+        def _(j):
+            vt[:, span(j)] = jnp.transpose(v_ref[span(j), :].astype(FLOAT)).astype(LOW)
+
+    head = lax.broadcasted_iota(jnp.int32, (BLOCK, inner), 1) // HEAD_DIM
+    spread(q_ref[...].astype(FLOAT), qm, head, heads)
+    start = widen_lanes(start_ref[...], heads)
+    stop = widen_lanes(stop_ref[...], heads)
+    low = first[block]
+    row = lax.broadcasted_iota(jnp.int32, (BLOCK, wide), 0)
+
+    def score(j, top):
+        raw = nt(k_ref[span(j), :], qm[...])
+        raw = jnp.where(row >= start - j * BLOCK, raw, -1e30)
+        scores[span(j), :] = raw
+        return jnp.maximum(top, jnp.max(raw, axis=0, keepdims=True))
+
+    raw = diagonal(nt(k_ref[span(block), :], qm[...]), block, start, stop, heads)
+    scores[span(block), :] = raw
+    top = lax.fori_loop(low, block, score, jnp.max(raw, axis=0, keepdims=True))
+    ot[:inner, :] = jnp.zeros((inner, BLOCK), FLOAT)
+
+    def weigh(j, total):
+        weight = jnp.exp(scores[span(j), :] - top)
+        rounded = weight.astype(LOW)
+        for h in range(heads):
+            lines = slice(h * HEAD_DIM, (h + 1) * HEAD_DIM)
+            ot[lines, :] += nn(vt[lines, span(j)], rounded[:, h * BLOCK : (h + 1) * BLOCK])
+        return total + jnp.sum(weight, axis=0, keepdims=True)
+
+    total = lax.fori_loop(low, block + 1, weigh, jnp.zeros((1, wide), FLOAT))
+    total_out[...] = (jnp.log(total) + top).reshape(1, 1, wide)
+    scale = 1.0 / total
+    for h in range(heads):
+        lines = slice(h * HEAD_DIM, (h + 1) * HEAD_DIM)
+        ot[lines, :] = ot[lines, :] * scale[:, h * BLOCK : (h + 1) * BLOCK]
+    exact_out[...] = ot[:inner, :]
+    heads_out[...] = jnp.transpose(ot[...])[:, :inner].astype(LOW)
+
+
+def forward(first, q, k, v, start, stop):
+    group, inner = q.shape
+    count = group // BLOCK
+    wide = inner // HEAD_DIM * BLOCK
+
+    def rows(s, first):
+        return (count - 1 - s, 0)
+
+    def lanes(s, first):
+        return (0, count - 1 - s)
+
+    def deep(s, first):
+        return (count - 1 - s, 0, 0)
+
+    thin = (BLOCK, inner)
+    stat = ((count, 1, wide), FLOAT, (1, 1, wide), deep)
+    return call(
+        forward_kernel,
+        "forward",
+        first,
+        count,
+        [(q, thin, rows), (k, None, None), (v, None, None)]
+        + [(start, (1, BLOCK), lanes), (stop, (1, BLOCK), lanes)],
+        [((group, inner), LOW, thin, rows), stat, ((inner, group), FLOAT, (inner, BLOCK), lanes)],
+        [
+            pltpu.VMEM((inner, group), LOW),
+            pltpu.VMEM((wide, inner), LOW),
+            pltpu.VMEM((group, wide), FLOAT),
+            pltpu.VMEM((BLOCK, BLOCK), FLOAT),
+        ],
+        flops=8 * group * group * inner,
+    )
+
+
+def backward_kernel(
+    first, q_ref, k_ref, v_ref, o_ref, start_ref, stop_ref, total_ref, exact_ref, coarse, fine,
+    slope_out,
+    kt, qm, om, dk, dv, dqt,
+):
+    inner = q_ref.shape[1]
+    heads = inner // HEAD_DIM
+    wide = heads * BLOCK
+    step = pl.program_id(0)
+    count = pl.num_programs(0)
+    block = count - 1 - step
+
+    @pl.when(step == 0)
+    def _():
+        dk[...] = jnp.zeros_like(dk)
+        dv[...] = jnp.zeros_like(dv)
+        dqt[...] = jnp.zeros_like(dqt)
+
+        @pl.loop(0, count)
+        def _(j):
+            kt[:, span(j)] = jnp.transpose(k_ref[span(j), :].astype(FLOAT)).astype(LOW)
+
+    head = lax.broadcasted_iota(jnp.int32, (BLOCK, inner), 1) // HEAD_DIM
+    spread(q_ref[...].astype(FLOAT), qm, head, heads)
+    outer = o_ref[...].astype(FLOAT)
+    spread(outer, om, head, heads)
+    product = exact_ref[...] * jnp.transpose(outer)
+    start = widen_lanes(start_ref[...], heads)
+    stop = widen_lanes(stop_ref[...], heads)
+    total = total_ref[0]
+    balance = jnp.concatenate(
+        [
+            jnp.sum(product[h * HEAD_DIM : (h + 1) * HEAD_DIM, :], axis=0, keepdims=True)
+            for h in range(heads)
+        ],
+        axis=1,
+    )
+    row = lax.broadcasted_iota(jnp.int32, (BLOCK, wide), 0)
+    dqt[:inner, :] = jnp.zeros((inner, BLOCK), FLOAT)
+
+    def spend(j, raw):
+        normal = jnp.exp(raw - total)
+        weight = normal.astype(LOW)
+        change = (normal * (nt(v_ref[span(j), :], om[...]) - balance)).astype(LOW)
+        dv[span(j), :] += nn(weight, om[...])
+        dk[span(j), :] += nn(change, qm[...])
+        for h in range(heads):
+            lines = slice(h * HEAD_DIM, (h + 1) * HEAD_DIM)
+            dqt[lines, :] += nn(kt[lines, span(j)], change[:, h * BLOCK : (h + 1) * BLOCK])
+
+    @pl.loop(first[block], block)
+    def _(j):
+        raw = nt(k_ref[span(j), :], qm[...])
+        spend(j, jnp.where(row >= start - j * BLOCK, raw, -1e30))
+
+    spend(block, diagonal(nt(k_ref[span(block), :], qm[...]), block, start, stop, heads))
+    dq = jnp.transpose(dqt[...])[:, :inner] * HEAD_DIM ** (-0.5)
+    both = jnp.concatenate([dq, dk[span(block), :]], axis=1)
+    times = 2 * inner // 128
+    tiles = BLOCK // TILE
+    cosine, left, right = turns(first, count + block * tiles, tiles, coarse, fine)
+    turned = (
+        both * widen_lanes(cosine, times)
+        - pltpu.roll(both, 2 * inner - ROTARY // 2, 1) * widen_lanes(left, times)
+        - pltpu.roll(both, ROTARY // 2, 1) * widen_lanes(right, times)
+    )
+    slope_out[...] = jnp.concatenate([turned, dv[span(block), :]], axis=1).astype(LOW)
+
+
+def backward(first, q, k, v, o, start, stop, total, exact, tables):
+    group, inner = q.shape
+    count = group // BLOCK
+    wide = inner // HEAD_DIM * BLOCK
+
+    def rows(s, first):
+        return (count - 1 - s, 0)
+
+    def lanes(s, first):
+        return (0, count - 1 - s)
+
+    def deep(s, first):
+        return (count - 1 - s, 0, 0)
+
+    thin = (BLOCK, inner)
+    return call(
+        backward_kernel,
+        "backward",
+        first,
+        count,
+        [(q, thin, rows), (k, None, None), (v, None, None), (o, thin, rows)]
+        + [(start, (1, BLOCK), lanes), (stop, (1, BLOCK), lanes)]
+        + [(total, (1, 1, wide), deep), (exact, (inner, BLOCK), lanes)]
+        + [(table, None, None) for table in tables],
+        [((group, 3 * inner), LOW, (BLOCK, 3 * inner), rows)],
+        [
+            pltpu.VMEM((inner, group), LOW),
+            pltpu.VMEM((wide, inner), LOW),
+            pltpu.VMEM((wide, inner), LOW),
+            pltpu.VMEM((group, inner), FLOAT),
+            pltpu.VMEM((group, inner), FLOAT),
+            pltpu.VMEM((BLOCK, BLOCK), FLOAT),
+        ],
+        flops=16 * group * group * inner,
+    )[0]
+
+
+def mix_kernel(place, own_g, peer_g, heads_ref, weight, o_out, own_out, peer_out, extra, outer):
+    inner = heads_ref.shape[1]
+    step = pl.program_id(0)
+    half = pl.num_programs(0) // 2
+    share = weight.shape[0] // 8
+
+    @pl.when(step == 0)
+    def _():
+        outer[...] = jnp.zeros_like(outer)
+
+    def work(g_ref, target):
+        heads = heads_ref[...]
+        slope = g_ref[...]
+        lower = jnp.concatenate([jnp.zeros((heads.shape[0], 64), LOW), heads], axis=1)
+        o_out[...] = nn(slope, weight[:, 3 * inner - 64 :])[:, 64:].astype(LOW)
+        target[...] = nt(lower, weight[:, 3 * inner - 64 :]).astype(LOW)
+        outer[...] += tn(slope, heads)
+
+    @pl.when(step < half)
+    def _():
+        work(own_g, own_out)
+
+    @pl.when(step >= half)
+    def _():
+        work(peer_g, peer_out)
+
+    @pl.when(step == 2 * half - 1)
+    def _():
+        for f in range(8):
+            parts = [outer[f * share + 32 * c : f * share + 32 * (c + 1), :] for c in range(3)]
+            parts.append(jnp.zeros((32, extra.shape[2] - 3 * inner), FLOAT))
+            extra[f] = jnp.concatenate(parts, axis=1).astype(LOW)
+
+
+def mix(place, own_g, peer_g, heads, weight):
+    rows, width = own_g.shape
+    inner = heads.shape[1]
+    half = rows // ROWS
+    own, peer, target = halves(half)
+    block = (ROWS, width)
+    thin = (ROWS, inner)
+    return call(
+        mix_kernel,
+        "mix",
+        place,
+        2 * half,
+        [(own_g, block, own), (peer_g, block, peer), (heads, thin, target), (weight, None, None)],
+        [
+            ((2 * rows, inner), LOW, thin, target),
+            ((rows, width), LOW, block, own),
+            ((rows, width), LOW, block, peer),
+            ((8, 32, width), LOW, None, None),
+        ],
+        [pltpu.VMEM((width, inner), FLOAT)],
+        12 * rows * width * inner,
+    )
+
+
+def write_parts(x, parts, kept, sent):
+    for own in range(2):
+
+        @pl.when(x == own)
+        def _(own=own):
+            for f in range(8):
+                target = kept if f % 2 == own else sent
+                for first, value in parts(f):
+                    target[f // 2, first : first + value.shape[0], : value.shape[1]] = value
+
+
+def feed_kernel(closing, place, x_ref, g_ref, m_in, *refs):
+    if closing:
+        weight, lines, total_in, sums_in, extra = refs[:5]
+        m_far, m_near, e_out, kept, sent, total, sums_all = refs[5:]
+    else:
+        pieces = refs[:8]
+        m_far, m_near, e_out, weight, lines, total, sums_all = refs[8:]
+    step = pl.program_id(0)
+    width = x_ref.shape[1]
+    share = width // 8
+
+    @pl.when(step == 0)
+    def _():
+        if closing:
+            total[...] = total_in[...]
+            sums_all[...] = sums_in[...]
+        else:
+            place_pieces(place, pieces, 0, weight, 0, share)
+            place_pieces(place, pieces, share, weight, width, share)
+            lines[...] = sum_rows(pieces, 2 * share)
+            total[...] = jnp.zeros_like(total)
+            sums_all[...] = jnp.zeros_like(sums_all)
+
+    gain = lines[0:1, :]
+    unit, _ = center(x_ref[...].astype(FLOAT))
+    normed = (unit * gain + lines[1:2, :]).astype(LOW)
+    slope = g_ref[...]
+    hidden = nn(normed, weight[:width, :]) + lines[2:3, :]
+    phi = 0.5 * (1.0 + lax.erf(hidden * 0.7071067811865476))
+    active = (hidden * phi).astype(LOW)
+    fed = (nt(active, weight[width:, :]) + m_in[...].astype(FLOAT)).astype(LOW)
+    inside = phi + hidden * jnp.exp(-0.5 * hidden * hidden) * 0.3989422804014327
+    change = (nn(slope, weight[width:, :]) * inside).astype(LOW)
+    back = nt(change, weight[:width, :])
+    e_out[...] = (back * gain).astype(LOW)
+    total[:width, :] += tn(normed, change)
+    total[width:, :] += tn(slope, active)
+    rows = [
+        jnp.sum(back * unit, axis=0, keepdims=True),
+        jnp.sum(back, axis=0, keepdims=True),
+        jnp.sum(change.astype(FLOAT), axis=0, keepdims=True),
+    ]
+    if not closing:
+        once = jnp.where(place[1] == 0, 1.0, 0.0)
+        rows.append(jnp.sum(slope.astype(FLOAT), axis=0, keepdims=True) * once)
+    rows.append(jnp.zeros((16 - len(rows), width), FLOAT))
+    sums_all[...] += jnp.concatenate(rows, axis=0)
+
+    @pl.when(step == 0)
+    def _():
+        m_far[...] = fed
+
+    @pl.when(step == 1)
+    def _():
+        m_near[...] = fed
+        if closing:
+            vectors = sums_all[...].astype(LOW)
+
+            def parts(f):
+                lines_of = slice(f * share, (f + 1) * share)
+                later = slice(width + f * share, width + (f + 1) * share)
+                return [
+                    (0, total[lines_of, :].astype(LOW)),
+                    (share, total[later, :].astype(LOW)),
+                    (2 * share, vectors),
+                    (2 * share + 16, extra[f]),
+                ]
+
+            write_parts(place[10], parts, kept, sent)
+
+
+def crossed(s, place):
+    return (jnp.where(s == 0, 1 - place[1], place[1]), 0)
+
+
+def feed(place, x, g, m, pieces=None, weight=None, lines=None, sums=None, extra=None):
+    rows, width = x.shape
+    block = (ROWS, width)
+    closing = sums is not None
+    inputs = [(x, block, crossed), (g, block, crossed), (m, block, crossed)]
+    outputs = [((ROWS, width), LOW, None, None)] * 2 + [((rows, width), LOW, block, crossed)]
+    scratch = []
+    if closing:
+        inputs += [(array, None, None) for array in (weight, lines) + sums + (extra,)]
+        outputs += [((4, width // 4 + 48, width), LOW, None, None)] * 2
+        scratch = [pltpu.VMEM((2 * width, width), FLOAT), pltpu.VMEM((16, width), FLOAT)]
+    else:
+        inputs += [(piece, None, None) for piece in pieces]
+        outputs += [
+            ((2 * width, width), LOW, None, None),
+            ((16, width), FLOAT, None, None),
+            ((2 * width, width), FLOAT, None, None),
+            ((16, width), FLOAT, None, None),
+        ]
+    kernel = functools.partial(feed_kernel, closing)
+    return call(kernel, "feed", place, 2, inputs, outputs, scratch, 12 * rows * width * width)
+
+
+def finish_kernel(
+    place, own_x, peer_x, own_e, peer_e, slope_ref, lines, weight,
+    peer_far, peer_near, own_far, own_near, kept, sent,
+    total, sums_all,
+):
+    step = pl.program_id(0)
+    half = pl.num_programs(0) // 2
+    width, size = total.shape
+    share = width // 8
+
+    @pl.when(step == 0)
+    def _():
+        total[...] = jnp.zeros_like(total)
+        sums_all[...] = jnp.zeros_like(sums_all)
+
+    slope = jnp.concatenate([slope_ref[...], jnp.zeros((slope_ref.shape[0], 64), LOW)], axis=1)
+
+    def work(x_ref, e_ref, targets):
+        unit, _ = center(x_ref[...].astype(FLOAT))
+        total[...] += tn(unit.astype(LOW), slope)
+        sums_all[0:1, :] += jnp.sum(slope.astype(FLOAT), axis=0, keepdims=True)
+        back = nt(slope, weight[:, :size])
+        value = (back * lines[0:1, :] + e_ref[...].astype(FLOAT)).astype(LOW)
+        for spot, target in enumerate(targets):
+
+            @pl.when(step % half == spot)
+            def _(target=target):
+                target[...] = value
+
+    @pl.when(step < half)
+    def _():
+        work(peer_x, peer_e, (peer_far, peer_near))
+
+    @pl.when(step >= half)
+    def _():
+        work(own_x, own_e, (own_far, own_near))
+
+    @pl.when(step == 2 * half - 1)
+    def _():
+        column = jnp.transpose(jnp.concatenate([lines[...], jnp.zeros((112, width), FLOAT)], axis=0))
+        flat = sums_all[0:1, :]
+        part = weight[:, :size].astype(FLOAT)
+        lane = lax.broadcasted_iota(jnp.int32, (1, size), 1)
+        part = jnp.where(lane < size - 64, part, 0.0)
+        gain_part = jnp.sum(part * total[...], axis=1, keepdims=True)
+        shift_part = jnp.sum(part * flat, axis=1, keepdims=True)
+        both = jnp.concatenate([gain_part, shift_part, jnp.zeros((width, 126), FLOAT)], axis=1)
+        both = jnp.transpose(both)
+        middle = width // 2
+        none = jnp.zeros((1, size - middle), FLOAT)
+        vectors = [
+            jnp.concatenate([both[line : line + 1, a : a + middle], none], axis=1)
+            for line in range(2)
+            for a in (0, middle)
+        ]
+        vectors = stacked(vectors + [flat], size)
+        total[...] = total[...] * column[:, 0:1] + column[:, 1:2] * flat
+
+        def parts(f):
+            return [(0, total[f * share : (f + 1) * share, :].astype(LOW)), (share, vectors)]
+
+        write_parts(place[10], parts, kept, sent)
+
+
+def finish(place, own_x, peer_x, own_e, peer_e, slope, lines, weight):
+    rows, width = own_x.shape
+    size = slope.shape[1] + 64
+    block = (ROWS, width)
+
+    def peer(s, place):
+        return (jnp.where(s == 0, 1 - place[1], place[1]), 0)
+
+    def own(s, place):
+        return (jnp.where(s < 3, 1 - place[1], place[1]), 0)
+
+    def target(s, place):
+        side = jnp.where(s < 2, 1 - place[0], place[0])
+        return (2 * side + jnp.where(s % 2 == 0, 1 - place[1], place[1]), 0)
+
+    return call(
+        finish_kernel,
+        "finish",
+        place,
+        4,
+        [(own_x, block, own), (peer_x, block, peer), (own_e, block, own), (peer_e, block, peer)]
+        + [(slope, (ROWS, slope.shape[1]), target), (lines, None, None), (weight, None, None)],
+        [((ROWS, width), LOW, None, None)] * 4 + [((4, width // 8 + 16, size), LOW, None, None)] * 2,
+        [pltpu.VMEM((width, size), FLOAT), pltpu.VMEM((8, size), FLOAT)],
+    )
+
+
+def cross_kernel(place, kept, got, own, *sent):
+    for step, target in enumerate((own,) + sent):
+        spot = lax.rem(place[11] + step, 4)
+        target[...] = (kept[spot].astype(FLOAT) + got[spot].astype(FLOAT)).astype(LOW)
+
+
+def cross(place, kept, got):
+    return call(
+        cross_kernel,
+        "cross",
+        place,
+        1,
+        [(kept, None, None), (got, None, None)],
+        [(kept.shape[1:], LOW, None, None)] * 4,
+    )
+
+
+def last_feed_kernel(place, own, far, wide, narrow, out, sums, units):
+    y = place[0]
+    width = own.shape[1]
+    share = width // 8
+    inner = out.shape[1] // 2
+
+    def both(first, count):
+        mine = own[first : first + count, :].astype(FLOAT)
+        theirs = far[first : first + count, :].astype(FLOAT)
+        return mine, theirs, pick(y, mine, theirs), pick(y, theirs, mine)
+
+    _, _, low, high = both(0, share)
+    wide[...] = jnp.concatenate([low, high], axis=1)
+    _, _, low, high = both(share, share)
+    narrow[...] = jnp.concatenate([low, high], axis=1)
+    mine, theirs, low, high = both(2 * share, 16)
+    sums[...] = mine + theirs
+    units[...] = jnp.concatenate([low[2:3, :], high[2:3, :]], axis=1)
+    _, _, low, high = both(2 * share + 16, 32)
+
+    def column(value):
+        return jnp.concatenate([value[:, c * inner : (c + 1) * inner] for c in range(3)], axis=0)
+
+    out[...] = jnp.concatenate([column(low), column(high)], axis=1)
+
+
+def last_feed(place, own, far, inner):
+    width = own.shape[1]
+    share = width // 8
+    return call(
+        last_feed_kernel,
+        "last_feed",
+        place,
+        1,
+        [(own, None, None), (far, None, None)],
+        [
+            ((share, 2 * width), FLOAT, None, None),
+            ((share, 2 * width), FLOAT, None, None),
+            ((share, 2 * inner), FLOAT, None, None),
+            ((16, width), FLOAT, None, None),
+            ((1, 2 * width), FLOAT, None, None),
+        ],
+    )
+
+
+def last_attend_kernel(place, own, far, project, sums, bias):
+    y = place[0]
+    _, share, double = project.shape
+    inner = double // 2
+    mine = own[:share, :].astype(FLOAT)
+    theirs = far[:share, :].astype(FLOAT)
+    low, high = pick(y, mine, theirs), pick(y, theirs, mine)
+    for c in range(3):
+        lanes = slice(c * inner, (c + 1) * inner)
+        project[c] = jnp.concatenate([low[:, lanes], high[:, lanes]], axis=1)
+    mine = own[share:, :].astype(FLOAT)
+    theirs = far[share:, :].astype(FLOAT)
+    sums[...] = mine + theirs
+    low, high = pick(y, mine, theirs), pick(y, theirs, mine)
+    rows = []
+    for c in range(3):
+        lanes = slice(c * inner, (c + 1) * inner)
+        rows.append(jnp.concatenate([low[4:5, lanes], high[4:5, lanes]], axis=1))
+    bias[...] = jnp.concatenate(rows, axis=0)
+
+
+def last_attend(place, own, far, inner):
+    share = own.shape[0] - 16
+    return call(
+        last_attend_kernel,
+        "last_attend",
+        place,
+        1,
+        [(own, None, None), (far, None, None)],
+        [
+            ((3, share, 2 * inner), FLOAT, None, None),
+            ((16, own.shape[1]), FLOAT, None, None),
+            ((3, 2 * inner), FLOAT, None, None),
+        ],
+    )
+
+
+def settle_kernel(slope, place, x_ref, other_ref, mine, theirs, out):
+    step = pl.program_id(0)
+    source = x_ref[...].astype(FLOAT)
+
+    def work(total):
+        if slope:
+            unit, factor = center(source)
+            change = (
+                total
+                - jnp.mean(total, axis=-1, keepdims=True)
+                - unit * jnp.mean(total * unit, axis=-1, keepdims=True)
+            )
+            out[...] = other_ref[...].astype(FLOAT) + factor * change
+        else:
+            out[...] = (source + total + (other_ref[3:4, :] + other_ref[4:5, :])).astype(LOW)
+
+    @pl.when(step == place[1])
+    def _():
+        work(mine[...].astype(FLOAT))
+
+    @pl.when(step != place[1])
+    def _():
+        work(theirs[...].astype(FLOAT))
+
+
+def settle(place, slope, x, other, mine, theirs):
+    rows, width = x.shape
+    block = (ROWS, width)
+
+    def moving(s, place):
+        return (s, 0)
+
+    return call(
+        functools.partial(settle_kernel, slope),
+        "settle",
+        place,
+        2,
+        [(x, block, moving), (other, block, moving) if slope else (other, None, None)]
+        + [(mine, None, None), (theirs, None, None)],
+        [((rows, width), FLOAT if slope else LOW, block, moving)],
+    )[0]
+
+
+PAIR = [(0, 1), (1, 0)]
+
+
+def swap(value, axis):
+    return lax.ppermute(value, axis, PAIR)
+
+
+def ring_order():
+    return list(range(0, 8, 2)) + list(range(7, 0, -2))
+
+
+def ring_owners(me):
+    spot = jnp.where(me % 2 == 0, me // 2, 7 - me // 2)
+    offsets = [0, -1, 1, -2, 2, -3, 3, -4]
+    positions = [(spot + offset + 8) % 8 for offset in offsets]
+    return [jnp.where(p < 4, 2 * p, 15 - 2 * p) for p in positions]
+
+
+class Ring:
+    def __init__(self, piece):
+        self.pieces = [piece]
+        self.ends = [piece, piece]
+        order = ring_order()
+        forward = [(order[i], order[(i + 1) % 8]) for i in range(8)]
+        self.ways = [forward, [(b, a) for a, b in forward]]
+
+    def step(self):
+        ways = self.ways[: 8 - len(self.pieces)]
+        self.ends = [lax.ppermute(end, "fsdp", way) for end, way in zip(self.ends, ways)]
+        self.pieces += self.ends
+
+    def newest(self):
+        return tuple(self.ends)
+
+
+def send_along(pieces):
+    got = []
+    for step, piece in enumerate(pieces, 1):
+        pairs = [(2 * a + b, 2 * ((a + step) % 4) + b) for a in range(4) for b in range(2)]
+        got.append(lax.ppermute(piece, "fsdp", pairs))
+    return got
+
+
+def add_along(own, got):
+    total = own.astype(FLOAT)
+    for piece in got:
+        total = total + piece.astype(FLOAT)
+    return total.astype(LOW)
+
+
+def swap_x(value):
+    return lax.ppermute(value, "fsdp", [(i, i ^ 1) for i in range(8)])
+
+
+def after(values, *earlier):
+    return lax.optimization_barrier((values, earlier))[0]
+
+
+def add(*values):
+    total = values[0].astype(FLOAT)
+    for value in values[1:]:
+        total = total + value.astype(FLOAT)
+    return total.astype(LOW)
+
+
+def ordered(own, peer, index, axis=0):
+    first = jnp.where(index == 0, own, peer)
+    second = jnp.where(index == 0, peer, own)
+    return jnp.concatenate([first, second], axis=axis)
+
+
+def take_half(value, index, axis=0):
+    size = value.shape[axis] // 2
+    return lax.dynamic_slice_in_dim(value, index * size, size, axis)
+
+
+def split_body(
+    tokens,
+    pack_lengths,
+    cotangent,
+    projection,
+    projection_bias,
+    outgoing,
+    outgoing_bias,
+    widening,
+    widening_bias,
+    narrowing,
+    narrowing_bias,
+    first_gain,
+    first_shift,
+    second_gain,
+    second_shift,
+):
+    _, local, width = tokens.shape
+    group = 2 * local
+    share = width // 8
+    y = lax.axis_index("context")
+    core = lax.axis_index("tensor")
+    me = lax.axis_index("fsdp")
+    own_x = tokens.reshape(local, width)
+    own_g = cotangent.reshape(local, width)
+    inner = outgoing.shape[0] // 2
+    third = projection_bias.shape[1]
+    owners = ring_owners(me)
+    place = jnp.stack([y, core] + owners + [me % 2, me // 2, me])
+    other = jnp.stack([1 - y, core] + owners + [me % 2, me // 2, me])
+
+    def whole(*arrays):
+        return [(array if array.ndim > 1 else rank_two(array), None, None) for array in arrays]
+
+    attend_piece = call(
+        pack_attend_kernel,
+        "pack_attend",
+        place,
+        1,
+        whole(projection.transpose(1, 0, 2), outgoing.T, first_gain, first_shift, outgoing_bias, narrowing_bias)
+        + whole(projection_bias),
+        [((share + 16, width), LOW, None, None)],
+    )[0]
+    index = jnp.arange(group, dtype=jnp.int32)
+    number, position, valid = layout(pack_lengths[0], index)
+    begin = index - position
+    labels = jnp.arange(SEQS, dtype=jnp.int32)
+    length = jnp.sum(
+        jnp.where(number[:, None] == labels[None, :], pack_lengths[0][None, :], 0), axis=1
+    )
+    stop = jnp.minimum(index + 1, begin + length).reshape(1, group)
+    start = jnp.where(number == SEQS, index, begin)
+    first = jnp.min(start.reshape(group // BLOCK, BLOCK), axis=1) // BLOCK
+    start = start.reshape(1, group)
+    tiles = position.reshape(group // TILE, TILE)[:, 0] // TILE
+    first = jnp.concatenate([first, tiles])
+    tables = turning()
+    place = jnp.concatenate([place, tiles])
+
+    far_x = swap(take_half(own_x, core), "context")
+    attend_ring = Ring(attend_piece)
+    attend_ring.step()
+    attend_ring.step()
+    feed_piece = call(
+        pack_feed_kernel,
+        "pack_feed",
+        place,
+        1,
+        whole(widening, narrowing.T, second_gain, second_shift, widening_bias),
+        [((2 * share + 16, width), LOW, None, None)],
+    )[0]
+    feed_ring = Ring(after(feed_piece, attend_ring.newest()))
+    attend_ring.step()
+    far_x = after(far_x, attend_ring.newest())
+    far_g = swap(after(take_half(own_g, core), far_x), "context")
+    peer_x = ordered(far_x, swap(far_x, "tensor"), core)
+    feed_ring.step()
+    attend_ring.step()
+    peer_x = after(peer_x, feed_ring.newest())
+    feed_ring.step()
+    q, k, v, attend_weight, attend_lines = prepare(place, own_x, peer_x, tables, attend_ring.pieces, inner)
+    q, far_g = after((q, far_g), feed_ring.newest())
+    feed_ring.step()
+    near_g = swap(far_g, "tensor")
+    heads, total, exact = forward(first, q, k, v, start, stop)
+    heads, near_g, feed_ring.ends = after((heads, near_g, feed_ring.ends))
+    feed_ring.step()
+    peer_g = ordered(far_g, near_g, core)
+    o, mixed_own, mixed_peer, extra = mix(place, own_g, peer_g, heads, attend_weight)
+
+    own_far, own_near, e_own, weight, lines, totals, sums = feed(place, own_x, own_g, mixed_own, pieces=feed_ring.pieces)
+    peer_far, peer_near, e_peer, kept, sent = feed(
+        place, peer_x, peer_g, mixed_peer, weight=weight, lines=lines, sums=(totals, sums), extra=extra
+    )
+    got = swap_x(sent)
+    gone = add(peer_near, swap(peer_far, "tensor"))
+    mixed_far = swap(gone, "context")
+    own_got = swap(own_far, "tensor")
+
+    o = after(o, gone, own_got)
+    slope = backward(first, q, k, v, o, start, stop, total, exact, tables)
+    slope, got, mixed_far = after((slope, got, mixed_far))
+    feed_cross = cross(place, kept, got)
+    slope = after(slope, feed_cross)
+    feed_got = send_along(feed_cross[1:])
+    peer_far, peer_near, far_own, near_own, kept, sent = finish(
+        place, own_x, peer_x, own_e=e_own, peer_e=e_peer, slope=slope, lines=attend_lines, weight=attend_weight
+    )
+    attend_got = swap_x(sent)
+    peer_got = swap(peer_far, "tensor")
+    e_got_own = swap(far_own, "tensor")
+    gone = add(peer_near, peer_got)
+    e_far = swap(gone, "context")
+    feed_got = after(feed_got, gone)
+    feed_sum = add_along(feed_cross[0], feed_got)
+    feed_far = swap(feed_sum, "context")
+    own_near = after(own_near, feed_sum)
+    mine = add(own_near, own_got, mixed_far)
+    mixed = settle(place, False, own_x, attend_lines, mine, swap(mine, "tensor"))
+    attend_got = after(attend_got, feed_sum)
+    attend_cross = cross(place, kept, attend_got)
+    attend_along = send_along(attend_cross[1:])
+    e_far = after(e_far, attend_cross[0])
+    mine = add(near_own, e_got_own, e_far)
+    attend_along = after(attend_along, mine)
+    attend_sum = add_along(attend_cross[0], attend_along)
+    attend_far = swap(attend_sum, "context")
+    tokens_gradient = settle(place, True, own_x, own_g, mine, swap(mine, "tensor"))
+
+    wide_slope, narrow_slope, outgoing_slope, feed_sums, unit_slope = last_feed(place, feed_sum, feed_far, inner)
+    projection_slope, attend_sums, bias_slope = last_attend(place, attend_sum, attend_far, inner)
+
+    def across(rows):
+        part = lax.dynamic_slice_in_dim(rows.astype(LOW), me * share, share, 1)
+        return part.astype(FLOAT) + swap(part, "tensor").astype(FLOAT)
+
+    feed_lines = across(feed_sums[:8])
+    attend_slopes = across(attend_sums[:4, : width // 2].reshape(2, width))
+    unit_slope = lax.dynamic_slice_in_dim(unit_slope[0], me * (width // 4), width // 4)
+    bias_slope = lax.dynamic_slice_in_dim(bias_slope, me * third, third, 1)
+    return (
+        mixed.reshape(tokens.shape),
+        tokens_gradient.reshape(tokens.shape),
+        projection_slope.transpose(1, 0, 2),
+        bias_slope,
+        outgoing_slope.T,
+        feed_lines[3],
+        wide_slope,
+        unit_slope,
+        narrow_slope.T,
+        feed_lines[3],
+        attend_slopes[0],
+        attend_slopes[1],
+        feed_lines[0],
+        feed_lines[1],
+    )
+
+
+def body(*arrays):
+    tokens, outgoing, narrowing = arrays[0], arrays[5], arrays[9]
+    fits = (
+        lax.axis_size("fsdp") == 8
+        and lax.axis_size("context") == 2
+        and lax.axis_size("tensor") == 2
+        and tokens.shape[0] == 1
+        and tokens.shape[1] == 2 * ROWS
+        and outgoing.shape[0] == 6 * HEAD_DIM
+        and tokens.shape[2] * 2 == narrowing.shape[0]
+    )
+    return split_body(*arrays) if fits else general_body(*arrays)
+
+
 def solution(mesh):
     return jax.shard_map(
         body,

time: 811 us -> 246 us (0.30)
  waiting for transfers between devices: 325 us -> 57.1 us
  matrix products: 194 us -> 0 us
  blocking collectives: 130 us -> 0 us
  Pallas kernels: 0 us -> 109 us
  other arithmetic: 106 us -> 12.1 us
  starting transfers between devices: 0.82 us -> 55.4 us
  local copies, waits for them, and re-layouts: 31.3 us -> 10.7 us
  between operations: 17.6 us -> 1.28 us
    reduce_scatter x6 -> x0, waiting for transfers between devices: 211 us -> none  [the longest x1 71.8 us: body(): lax.psum_scatter(narrowing_slope.astype(jnp.bfloat16), 'fsdp', scatter_di...]
    dot_general x18 -> x0, matrix products: 194 us -> none  [the longest x1 35.6 us: body(): jnp.einsum('qhd,khd->hqk', outer, value_block, preferred_element_type=jnp...]
    pallas_call x0 -> x15, Pallas kernels: none -> 109 us  [call(): pl.pallas_call(kernel, grid_spec=pltpu.PrefetchScalarGridSpec(num_scalar_...]
    unnamed x2 -> x0, blocking collectives: 76.5 us -> none
    psum x2 -> x0, waiting for transfers between devices: 66.3 us -> none  [the longest x1 37.8 us: body(): lax.psum(owned[0].astype(jnp.bfloat16), 'context').astype(jnp.float32)]
    ppermute x0 -> x38, waiting for transfers between devices: none -> 57.1 us  [the longest x6 21 us: send_along(): got.append(lax.ppermute(piece, 'fsdp', pairs))]
    ppermute x0 -> x38, starting transfers between devices: none -> 55.4 us  [the longest x6 29.8 us: send_along(): got.append(lax.ppermute(piece, 'fsdp', pairs))]
    all_gather x2 -> x0, blocking collectives: 48.3 us -> none  [the longest x1 31.6 us: body(): lax.all_gather(outgoing, 'fsdp', axis=1, tiled=True)]
  transfers between devices with their start and end apart: 14 -> 38, of which waited for: 6 -> 15; matrix products, arithmetic and copies ran while one was open for 38% -> 6% of each run, Pallas kernels for 0% -> 24%
where the time goes in v2:
time: 246 us
  Pallas kernels  109 us (44%)
  waiting for transfers between devices  57.1 us (23%)
  starting transfers between devices  55.4 us (23%)
  other arithmetic  12.1 us (5%)
  local copies, waits for them, and re-layouts  10.7 us (4%)
    pallas_call x15, Pallas kernels, call(): pl.pallas_call(kernel, grid_spec=pltpu.PrefetchScalarGridSpec(num_scalar_...  109 us
    ppermute x6, starting transfers between devices, send_along(): got.append(lax.ppermute(piece, 'fsdp', pairs))  29.8 us
    ppermute x6, waiting for transfers between devices, send_along(): got.append(lax.ppermute(piece, 'fsdp', pairs))  21 us
    ppermute x14, waiting for transfers between devices, step(): lax.ppermute(end, 'fsdp', way)  17.3 us
    ppermute x14, starting transfers between devices, step(): lax.ppermute(end, 'fsdp', way)  15.5 us
    ppermute x16, waiting for transfers between devices, swap(): return lax.ppermute(value, axis, PAIR)  9.56 us
    ppermute x2, waiting for transfers between devices, swap_x(): return lax.ppermute(value, 'fsdp', [(i, i ^ 1) for i in range(8)])  9.22 us
    ppermute x16, starting transfers between devices, swap(): return lax.ppermute(value, axis, PAIR)  7.89 us
  transfers between devices with their start and end apart: 38, of which 15 were waited for; matrix products, arithmetic and copies ran while one was open for 6% of the time, Pallas kernels for 24%

profile of v2, /device:TPU:0, one launch (start us, length us, event | category | flops | bytes accessed | tf_op | source)
XLA Modules:
  0.0 245.5 jit_solution(13945124054314670682)
XLA Ops:
  0.8 2.3 dynamic-slice_bitcast_fusion.1
  3.1 3.0 %collective-permute-start = (bf16[512,768]{1,0:T(8,128)(2,1)}, bf16[512,768]{1,0:T(8,128)(2,1)}, u32[]{:S(2)}, u32[]{:S(2)}) collective-permute-start(bf16[512,768]{1,0:T(8,128)(2,1)} %dynamic-slice_bitcast_fusion.1), channel_id=1, source_target_pairs={{0,2},{2,0},{1,3},{3,1},{4,6},{6,4},{5,7},{7,5},{8,10},{10,8},{9,1... | collective-permute-start | bytes 2359304 | tf_op jit(solution)/shard_map/ppermute | solution.py:1190
  7.0 1.6 collective-permute-start.1
  9.0 3.8 %collective-permute-done.1.refs_1_ = bf16[112,768]{1,0:T(8,128)(2,1)S(1)} collective-permute-done((bf16[112,768]{1,0:T(8,128)(2,1)S(1)}, bf16[112,768]{1,0:T(8,128)(2,1)S(1)}, u32[]{:S(2)}, u32[]{:S(2)}) %collective-permute-start.1) | collective-permute-done | bytes 172064 | tf_op jit(solution)/shard_map/ppermute | solution.py:1214
  12.8 1.6 collective-permute-start.2
  14.9 3.4 %collective-permute-done.2.refs_3_ = bf16[112,768]{1,0:T(8,128)(2,1)S(1)} collective-permute-done((bf16[112,768]{1,0:T(8,128)(2,1)S(1)}, bf16[112,768]{1,0:T(8,128)(2,1)S(1)}, u32[]{:S(2)}, u32[]{:S(2)}) %collective-permute-start.2) | collective-permute-done | bytes 172064 | tf_op jit(solution)/shard_map/ppermute | solution.py:1214
  18.2 1.6 collective-permute-start.3
  21.1 2.5 %collective-permute-done.3.refs_5_ = bf16[112,768]{1,0:T(8,128)(2,1)S(1)} collective-permute-done((bf16[112,768]{1,0:T(8,128)(2,1)S(1)}, bf16[112,768]{1,0:T(8,128)(2,1)S(1)}, u32[]{:S(2)}, u32[]{:S(2)}) %collective-permute-start.3) | collective-permute-done | bytes 172064 | tf_op jit(solution)/shard_map/ppermute | solution.py:1214
  23.7 1.6 collective-permute-done.6.refs_6_
  27.8 1.6 collective-permute-start.8
  30.5 1.6 collective-permute-start.10
  32.1 6.0 %collective-permute-done.8.refs_1_ = bf16[208,768]{1,0:T(8,128)(2,1)S(1)} collective-permute-done((bf16[208,768]{1,0:T(8,128)(2,1)S(1)}, bf16[208,768]{1,0:T(8,128)(2,1)S(1)}, u32[]{:S(2)}, u32[]{:S(2)}) %collective-permute-start.8) | collective-permute-done | bytes 319520 | tf_op jit(solution)/shard_map/ppermute | solution.py:1214
  38.2 1.6 collective-permute-start.12
  40.2 1.5 broadcast_select_fusion.3
  41.8 1.2 pad_maximum_fusion.peer_x.x_ref
  43.4 7.8 %prepare.1 = (bf16[2048,192]{1,0:T(8,128)(2,1)S(1)}, bf16[2048,192]{1,0:T(8,128)(2,1)S(1)}, bf16[2048,192]{1,0:T(8,128)(2,1)S(1)}, bf16[768,768]{1,0:T(8,128)(2,1)S(1)}, f32[16,768]{1,0:T(8,128)S(1)}) custom-call(s32[29]{0:T(128)S(1)} %concatenate.13.place, bf16[1024,768]{1,0:T(8,128)(2,1)} %bitcast.51, bf16[1024,768]{1,0:T(8,128)(2,1)} %pad_maximum_fusion.peer_x.x_ref, ...), custom_call_target="tpu_custom_call" | custom-call | flops 1 | bytes 1 | tf_op jit(solution)/shard_map/prepare/pallas_call | solution.py:396
  51.5 1.6 collective-permute-start.15
  53.6 14.8 %forward.1 = (bf16[2048,192]{1,0:T(8,128)(2,1)S(1)}, f32[8,1,768]{2,1,0:T(1,128)S(1)}, f32[192,2048]{1,0:T(8,128)S(1)}) custom-call(s32[24]{0:T(128)S(1)} %pad_add_fusion.first, bf16[2048,192]{1,0:T(8,128)(2,1)S(1)} %get-tuple-element.90.q_ref, bf16[2048,192]{1,0:T(8,128)(2,1)S(1)} %get-tuple-element.91.k_ref, ...), custom_call_target="tpu_custom_call" | custom-call | flops 1 | bytes 1 | tf_op jit(solution)/shard_map/forward/pallas_call | solution.py:396
  68.5 1.6 collective-permute-start.17
  70.1 1.3 broadcast_select_fusion.1
  71.5 1.3 pad_maximum_fusion.1.peer_g.g_ref
  72.7 6.8 %mix.1 = (bf16[2048,192]{1,0:T(8,128)(2,1)S(1)}, bf16[1024,768]{1,0:T(8,128)(2,1)S(1)}, bf16[1024,768]{1,0:T(8,128)(2,1)}, bf16[8,32,768]{2,1,0:T(8,128)(2,1)S(1)}) custom-call(s32[29]{0:T(128)S(1)} %concatenate.13.place, bf16[1024,768]{1,0:T(8,128)(2,1)} %bitcast.56, bf16[1024,768]{1,0:T(8,128)(2,1)} %pad_maximum_fusion.1.peer_g.g_ref, ...), custom_call_target="tpu_custom_call" | custom-call | flops 1 | bytes 1 | tf_op jit(solution)/shard_map/mix/pallas_call | solution.py:396
  79.5 1.2 copy-done.4
  80.7 14.6 %feed.2 = (bf16[512,768]{1,0:T(8,128)(2,1)S(1)}, bf16[512,768]{1,0:T(8,128)(2,1)S(1)}, bf16[1024,768]{1,0:T(8,128)(2,1)S(1)}, bf16[1536,768]{1,0:T(8,128)(2,1)},...) custom-call(s32[29]{0:T(128)S(1)} %concatenate.13.place, bf16[1024,768]{1,0:T(8,128)(2,1)} %bitcast.52, ...), custom_call_target="tpu_custom_call" | custom-call | flops 1 | bytes 1 | tf_op jit(solution)/shard_map/feed/pallas_call | solution.py:396
  95.2 1.2 copy-done.3
  96.5 15.0 %feed.3 = (bf16[512,768]{1,0:T(8,128)(2,1)S(1)}, bf16[512,768]{1,0:T(8,128)(2,1)S(1)}, bf16[1024,768]{1,0:T(8,128)(2,1)}, bf16[4,240,768]{2,1,0:T(8,128)(2,1)S(1)}, bf16[4,240,768]{2,1,0:T(8,128)(2,1)S(1)}) custom-call(s32[29]{0:T(128)S(1)} %concatenate.13.place, bf16[1024,768]{1,0:T(8,128)(2,1)} %pad_maximum_fusion.peer_x.x_ref, ...), custom_call_target="tpu_custom_call" | custom-call | flops 1 | bytes 1 | tf_op jit(solution)/shard_map/feed/pallas_call | solution.py:396
  112.2 1.6 collective-permute-done.18
  114.9 22.1 %backward.1.slope_ref = bf16[2048,576]{1,0:T(8,128)(2,1)} custom-call(s32[24]{0:T(128)S(1)} %pad_add_fusion.first, bf16[2048,192]{1,0:T(8,128)(2,1)S(1)} %get-tuple-element.90.q_ref, bf16[2048,192]{1,0:T(8,128)(2,1)S(1)} %get-tuple-element.91.k_ref, bf16[2048,192]{1,0:T(8,128)(2,1)S(1)} %get-tuple-element.92.v_ref, ...), custom_call_target="tpu_custom_call" | custom-call | flops 1 | bytes 1 | tf_op jit(solution)/shard_map/backward/pallas_call | solution.py:396
  137.0 9.2 %collective-permute-done.20.got = bf16[4,240,768]{2,1,0:T(8,128)(2,1)S(1)} collective-permute-done((bf16[4,240,768]{2,1,0:T(8,128)(2,1)S(1)}, bf16[4,240,768]{2,1,0:T(8,128)(2,1)S(1)}, u32[]{:S(2)}, u32[]{:S(2)}) %collective-permute-start.20) | collective-permute-done | bytes 1474592 | tf_op jit(solution)/shard_map/ppermute | solution.py:1237
  147.1 13.3 %finish.1 = (bf16[512,768]{1,0:T(8,128)(2,1)S(1)}, bf16[512,768]{1,0:T(8,128)(2,1)S(1)}, bf16[512,768]{1,0:T(8,128)(2,1)}, bf16[512,768]{1,0:T(8,128)(2,1)S(1)},...) custom-call(s32[29]{0:T(128)S(1)} %concatenate.13.place, bf16[1024,768]{1,0:T(8,128)(2,1)} %bitcast.53, ...), custom_call_target="tpu_custom_call" | custom-call | flops 1 | bytes 1 | tf_op jit(solution)/shard_map/finish/pallas_call | solution.py:396
  160.4 1.9 collective-permute-start.22
  162.2 4.4 %collective-permute-start.23 = (bf16[240,768]{1,0:T(8,128)(2,1)S(1)}, bf16[240,768]{1,0:T(8,128)(2,1)S(1)}, u32[]{:S(2)}, u32[]{:S(2)}) collective-permute-start(bf16[240,768]{1,0:T(8,128)(2,1)S(1)} %get-tuple-element.118), channel_id=1, source_target_pairs={{0,16},{4,20},{8,24},{12,28},{16,0},{20,4},{24,8},{28,12},{1,17},{... | collective-permute-start | bytes 1105928 | tf_op jit(solution)/shard_map/ppermute | solution.py:1225
  167.5 1.7 collective-permute-start.29
  169.3 1.1 add_convert_fusion.2
  170.4 5.3 %collective-permute-done.22 = bf16[240,768]{1,0:T(8,128)(2,1)S(1)} collective-permute-done((bf16[240,768]{1,0:T(8,128)(2,1)S(1)}, bf16[240,768]{1,0:T(8,128)(2,1)S(1)}, u32[]{:S(2)}, u32[]{:S(2)}) %collective-permute-start.22) | collective-permute-done | bytes 368672 | tf_op jit(solution)/shard_map/ppermute | solution.py:1225
  175.6 15.5 %collective-permute-done.23 = bf16[240,768]{1,0:T(8,128)(2,1)S(1)} collective-permute-done((bf16[240,768]{1,0:T(8,128)(2,1)S(1)}, bf16[240,768]{1,0:T(8,128)(2,1)S(1)}, u32[]{:S(2)}, u32[]{:S(2)}) %collective-permute-start.23) | collective-permute-done | bytes 368672 | tf_op jit(solution)/shard_map/ppermute | solution.py:1225
  192.3 1.2 collective-permute-start.28
  193.5 1.7 add_convert_fusion.1.mine
  196.4 8.5 %collective-permute-start.31 = (bf16[112,640]{1,0:T(8,128)(2,1)S(1)}, bf16[112,640]{1,0:T(8,128)(2,1)S(1)}, u32[]{:S(2)}, u32[]{:S(2)}) collective-permute-start(bf16[112,640]{1,0:T(8,128)(2,1)S(1)} %get-tuple-element.138), channel_id=1, source_target_pairs={{0,8},{4,12},{8,16},{12,20},{16,24},{20,28},{24,0},{28,4},{1,9},{5... | collective-permute-start | bytes 430088 | tf_op jit(solution)/shard_map/ppermute | solution.py:1225
  204.9 2.7 %last_feed.1 = (f32[96,1536]{1,0:T(8,128)}, f32[96,1536]{1,0:T(8,128)}, f32[96,384]{1,0:T(8,128)}, f32[16,768]{1,0:T(8,128)S(1)}, f32[1,1536]{1,0:T(1,128)S(1)}) custom-call(s32[29]{0:T(128)S(1)} %concatenate.13.place, bf16[240,768]{1,0:T(8,128)(2,1)S(1)} %add_convert_fusion.4.own, bf16[240,768]{1,0:T(8,128)(2,1)} %collective-permute-done.35.far), custom_call_target="tpu_custom_call" | custom-call | flops 1 | bytes 1 | tf_op jit(solution)/shard_map/last_feed/pallas_call | solution.py:396
  208.9 5.5 %collective-permute-start.32 = (bf16[112,640]{1,0:T(8,128)(2,1)S(1)}, bf16[112,640]{1,0:T(8,128)(2,1)S(1)}, u32[]{:S(2)}, u32[]{:S(2)}) collective-permute-start(bf16[112,640]{1,0:T(8,128)(2,1)S(1)} %get-tuple-element.139), channel_id=1, source_target_pairs={{0,16},{4,20},{8,24},{12,28},{16,0},{20,4},{24,8},{28,12},{1,17},{... | collective-permute-start | bytes 430088 | tf_op jit(solution)/shard_map/ppermute | solution.py:1225
  214.5 4.4 %collective-permute-done.28 = bf16[512,768]{1,0:T(8,128)(2,1)} collective-permute-done((bf16[512,768]{1,0:T(8,128)(2,1)}, bf16[512,768]{1,0:T(8,128)(2,1)}, u32[]{:S(2)}, u32[]{:S(2)}) %collective-permute-start.28) | collective-permute-done | bytes 786464 | tf_op jit(solution)/shard_map/ppermute | solution.py:1190
  218.9 8.7 %collective-permute-start.33 = (bf16[112,640]{1,0:T(8,128)(2,1)S(1)}, bf16[112,640]{1,0:T(8,128)(2,1)S(1)}, u32[]{:S(2)}, u32[]{:S(2)}) collective-permute-start(bf16[112,640]{1,0:T(8,128)(2,1)S(1)} %get-tuple-element.140), channel_id=1, source_target_pairs={{0,24},{4,28},{8,0},{12,4},{16,8},{20,12},{24,16},{28,20},{1,25},{... | collective-permute-start | bytes 430088 | tf_op jit(solution)/shard_map/ppermute | solution.py:1225
  227.6 2.7 %add_convert_fusion.mine = bf16[512,768]{1,0:T(8,128)(2,1)} fusion(bf16[512,768]{1,0:T(8,128)(2,1)} %collective-permute-done.28, bf16[512,768]{1,0:T(8,128)(2,1)} %collective-permute-done.27, bf16[512,768]{1,0:T(8,128)(2,1)S(1)} %get-tuple-element.131), kind=kLoop, calls=%fused_computation.2 | loop fusion | flops 2359296 | bytes 3145728 | tf_op jit(solution)/shard_map/convert_element_type | solution.py:1248
  232.0 2.4 settle.2
  234.4 2.2 collective-permute-done.34.far
  236.6 1.4 last_attend.1
  239.8 5.2 %settle.3 = f32[1024,768]{1,0:T(8,128)} custom-call(s32[29]{0:T(128)S(1)} %concatenate.13.place, bf16[1024,768]{1,0:T(8,128)(2,1)S(1)} %bitcast.55, bf16[1024,768]{1,0:T(8,128)(2,1)S(1)} %bitcast.58, bf16[512,768]{1,0:T(8,128)(2,1)} %add_convert_fusion.mine, bf16[512,768]{1,0:T(8,128)(2,1)} %collective-permute-done.30.theirs), custom_call_target="tpu_custom_call" | custom-call | flops 1 | bytes 1 | tf_op jit(solution)/shard_map/settle/pallas_call | solution.py:396
  (164 shorter events, 19.8 us)
Async XLA Ops:
  0.7 25.4 %copy-start.39 = (bf16[192]{0:T(256)(128)(2,1)S(1)}, bf16[192]{0:T(256)(128)(2,1)}, u32[]{:S(2)}) copy-start(bf16[192]{0:T(256)(128)(2,1)} %param.25) | copy-start | bytes 1156
  0.7 25.4 %copy-start.11 = (bf16[96,1536]{1,0:T(8,128)(2,1)S(1)}, bf16[96,1536]{1,0:T(8,128)(2,1)}, u32[]{:S(2)}) copy-start(bf16[96,1536]{1,0:T(8,128)(2,1)} %wide.1) | copy-start | bytes 884740
  0.8 25.4 %copy-start.12 = (bf16[1536,96]{0,1:T(8,128)(2,1)S(1)}, bf16[1536,96]{0,1:T(8,128)(2,1)}, u32[]{:S(2)}) copy-start(bf16[1536,96]{0,1:T(8,128)(2,1)} %param.26) | copy-start | bytes 884740
  0.8 25.4 %copy-start.25 = (bf16[96]{0:T(256)(128)(2,1)S(1)}, bf16[96]{0:T(256)(128)(2,1)}, u32[]{:S(2)}) copy-start(bf16[96]{0:T(256)(128)(2,1)} %param.30) | copy-start | bytes 580
  0.8 25.4 %copy-start.26 = (bf16[96]{0:T(256)(128)(2,1)S(1)}, bf16[96]{0:T(256)(128)(2,1)}, u32[]{:S(2)}) copy-start(bf16[96]{0:T(256)(128)(2,1)} %param.31) | copy-start | bytes 580
  0.8 26.1 %copy-start.1 = (bf16[1,1024,768]{2,1,0:T(8,128)(2,1)S(1)}, bf16[1,1024,768]{2,1,0:T(8,128)(2,1)}, u32[]{:S(2)}) copy-start(bf16[1,1024,768]{2,1,0:T(8,128)(2,1)} %param.19) | copy-start | bytes 4718596
  3.1 22.9 %collective-permute-start = (bf16[512,768]{1,0:T(8,128)(2,1)}, bf16[512,768]{1,0:T(8,128)(2,1)}, u32[]{:S(2)}, u32[]{:S(2)}) collective-permute-start(bf16[512,768]{1,0:T(8,128)(2,1)} %dynamic-slice_bitcast_fusion.1), channel_id=1, source_target_pairs={{0,2},{2,0},{1,3},{3,1},{4,6},{6,4},{5,7},{7,5},{8,10},{10,8},{9,1... | collective-permute-start | bytes 2359304 | tf_op jit(solution)/shard_map/ppermute | solution.py:1190
  7.0 5.9 %collective-permute-start.1 = (bf16[112,768]{1,0:T(8,128)(2,1)S(1)}, bf16[112,768]{1,0:T(8,128)(2,1)S(1)}, u32[]{:S(2)}, u32[]{:S(2)}) collective-permute-start(bf16[112,768]{1,0:T(8,128)(2,1)S(1)} %pack_attend.1.refs_0_), channel_id=1, source_target_pairs={{0,8},{8,16},{16,24},{24,28},{28,20},{20,12},{12,4},{4,0},{1,9},{9... | collective-permute-start | bytes 516104 | tf_op jit(solution)/shard_map/ppermute | solution.py:1214
  8.6 5.8 %collective-permute-start.4 = (bf16[112,768]{1,0:T(8,128)(2,1)S(1)}, bf16[112,768]{1,0:T(8,128)(2,1)S(1)}, u32[]{:S(2)}, u32[]{:S(2)}) collective-permute-start(bf16[112,768]{1,0:T(8,128)(2,1)S(1)} %pack_attend.1.refs_0_), channel_id=1, source_target_pairs={{8,0},{16,8},{24,16},{28,24},{20,28},{12,20},{4,12},{0,4},{9,1},{1... | collective-permute-start | bytes 516104 | tf_op jit(solution)/shard_map/ppermute | solution.py:1214
  12.8 5.4 %collective-permute-start.2 = (bf16[112,768]{1,0:T(8,128)(2,1)S(1)}, bf16[112,768]{1,0:T(8,128)(2,1)S(1)}, u32[]{:S(2)}, u32[]{:S(2)}) collective-permute-start(bf16[112,768]{1,0:T(8,128)(2,1)S(1)} %collective-permute-done.1.refs_1_), channel_id=1, source_target_pairs={{0,8},{8,16},{16,24},{24,28},{28,20},{20,12},{12,4},{4,0},{1,9},{9... | collective-permute-start | bytes 516104 | tf_op jit(solution)/shard_map/ppermute | solution.py:1214
  14.4 5.4 %collective-permute-start.5 = (bf16[112,768]{1,0:T(8,128)(2,1)S(1)}, bf16[112,768]{1,0:T(8,128)(2,1)S(1)}, u32[]{:S(2)}, u32[]{:S(2)}) collective-permute-start(bf16[112,768]{1,0:T(8,128)(2,1)S(1)} %collective-permute-done.4.refs_2_), channel_id=1, source_target_pairs={{8,0},{16,8},{24,16},{28,24},{20,28},{12,20},{4,12},{0,4},{9,1},{1... | collective-permute-start | bytes 516104 | tf_op jit(solution)/shard_map/ppermute | solution.py:1214
  18.2 5.4 %collective-permute-start.3 = (bf16[112,768]{1,0:T(8,128)(2,1)S(1)}, bf16[112,768]{1,0:T(8,128)(2,1)S(1)}, u32[]{:S(2)}, u32[]{:S(2)}) collective-permute-start(bf16[112,768]{1,0:T(8,128)(2,1)S(1)} %collective-permute-done.2.refs_3_), channel_id=1, source_target_pairs={{0,8},{8,16},{16,24},{24,28},{28,20},{20,12},{12,4},{4,0},{1,9},{9... | collective-permute-start | bytes 516104 | tf_op jit(solution)/shard_map/ppermute | solution.py:1214
  19.8 5.4 %collective-permute-start.6 = (bf16[112,768]{1,0:T(8,128)(2,1)S(1)}, bf16[112,768]{1,0:T(8,128)(2,1)S(1)}, u32[]{:S(2)}, u32[]{:S(2)}) collective-permute-start(bf16[112,768]{1,0:T(8,128)(2,1)S(1)} %collective-permute-done.5.refs_4_), channel_id=1, source_target_pairs={{8,0},{16,8},{24,16},{28,24},{20,28},{12,20},{4,12},{0,4},{9,1},{1... | collective-permute-start | bytes 516104 | tf_op jit(solution)/shard_map/ppermute | solution.py:1214
  23.7 18.0 %copy-start.18 = (bf16[112,768]{1,0:T(8,128)(2,1)}, bf16[112,768]{1,0:T(8,128)(2,1)S(1)}, u32[]{:S(2)}) copy-start(bf16[112,768]{1,0:T(8,128)(2,1)S(1)} %collective-permute-done.3.refs_5_) | copy-start | bytes 516100
  25.9 14.3 %collective-permute-start.7 = (bf16[512,768]{1,0:T(8,128)(2,1)}, bf16[512,768]{1,0:T(8,128)(2,1)}, u32[]{:S(2)}, u32[]{:S(2)}) collective-permute-start(bf16[512,768]{1,0:T(8,128)(2,1)} %collective-permute-done), channel_id=1, source_target_pairs={{0,1},{1,0},{2,3},{3,2},{4,5},{5,4},{6,7},{7,6},{8,9},{9,8},{10,11... | collective-permute-start | bytes 2359304 | tf_op jit(solution)/shard_map/ppermute | solution.py:1190
  27.8 10.3 %collective-permute-start.8 = (bf16[208,768]{1,0:T(8,128)(2,1)S(1)}, bf16[208,768]{1,0:T(8,128)(2,1)S(1)}, u32[]{:S(2)}, u32[]{:S(2)}) collective-permute-start(bf16[208,768]{1,0:T(8,128)(2,1)S(1)} %pack_feed.1.refs_0_), channel_id=1, source_target_pairs={{0,8},{8,16},{16,24},{24,28},{28,20},{20,12},{12,4},{4,0},{1,9},{9... | collective-permute-start | bytes 958472 | tf_op jit(solution)/shard_map/ppermute | solution.py:1214
  29.4 10.3 %collective-permute-start.9 = (bf16[208,768]{1,0:T(8,128)(2,1)S(1)}, bf16[208,768]{1,0:T(8,128)(2,1)S(1)}, u32[]{:S(2)}, u32[]{:S(2)}) collective-permute-start(bf16[208,768]{1,0:T(8,128)(2,1)S(1)} %pack_feed.1.refs_0_), channel_id=1, source_target_pairs={{8,0},{16,8},{24,16},{28,24},{20,28},{12,20},{4,12},{0,4},{9,1},{1... | collective-permute-start | bytes 958472 | tf_op jit(solution)/shard_map/ppermute | solution.py:1214
  29.9 21.4 %collective-permute-start.11 = (bf16[512,768]{1,0:T(8,128)(2,1)}, bf16[512,768]{1,0:T(8,128)(2,1)S(1)}, u32[]{:S(2)}, u32[]{:S(2)}) collective-permute-start(bf16[512,768]{1,0:T(8,128)(2,1)} %dynamic-slice_bitcast_fusion), channel_id=1, source_target_pairs={{0,2},{2,0},{1,3},{3,1},{4,6},{6,4},{5,7},{7,5},{8,10},{10,8},{9,1... | collective-permute-start | bytes 2359304 | tf_op jit(solution)/shard_map/ppermute | solution.py:1190
  30.5 12.5 %collective-permute-start.10 = (bf16[112,768]{1,0:T(8,128)(2,1)S(1)}, bf16[112,768]{1,0:T(8,128)(2,1)S(1)}, u32[]{:S(2)}, u32[]{:S(2)}) collective-permute-start(bf16[112,768]{1,0:T(8,128)(2,1)S(1)} %collective-permute-done.3.refs_5_), channel_id=1, source_target_pairs={{0,8},{8,16},{16,24},{24,28},{28,20},{20,12},{12,4},{4,0},{1,9},{9... | collective-permute-start | bytes 516104 | tf_op jit(solution)/shard_map/ppermute | solution.py:1214
  38.2 13.0 %collective-permute-start.12 = (bf16[208,768]{1,0:T(8,128)(2,1)S(1)}, bf16[208,768]{1,0:T(8,128)(2,1)S(1)}, u32[]{:S(2)}, u32[]{:S(2)}) collective-permute-start(bf16[208,768]{1,0:T(8,128)(2,1)S(1)} %collective-permute-done.8.refs_1_), channel_id=1, source_target_pairs={{0,8},{8,16},{16,24},{24,28},{28,20},{20,12},{12,4},{4,0},{1,9},{9... | collective-permute-start | bytes 958472 | tf_op jit(solution)/shard_map/ppermute | solution.py:1214
  39.8 11.5 %collective-permute-start.13 = (bf16[208,768]{1,0:T(8,128)(2,1)S(1)}, bf16[208,768]{1,0:T(8,128)(2,1)S(1)}, u32[]{:S(2)}, u32[]{:S(2)}) collective-permute-start(bf16[208,768]{1,0:T(8,128)(2,1)S(1)} %collective-permute-done.9.refs_2_), channel_id=1, source_target_pairs={{8,0},{16,8},{24,16},{28,24},{20,28},{12,20},{4,12},{0,4},{9,1},{1... | collective-permute-start | bytes 958472 | tf_op jit(solution)/shard_map/ppermute | solution.py:1214
  51.2 17.3 %copy-start.7 = (bf16[208,768]{1,0:T(8,128)(2,1)}, bf16[208,768]{1,0:T(8,128)(2,1)S(1)}, u32[]{:S(2)}) copy-start(bf16[208,768]{1,0:T(8,128)(2,1)S(1)} %collective-permute-done.12.refs_3_) | copy-start | bytes 958468
  51.2 17.3 %copy-start.33 = (bf16[512,768]{1,0:T(8,128)(2,1)}, bf16[512,768]{1,0:T(8,128)(2,1)S(1)}, u32[]{:S(2)}) copy-start(bf16[512,768]{1,0:T(8,128)(2,1)S(1)} %collective-permute-done.11) | copy-start | bytes 2359300
  51.3 17.3 %collective-permute-start.14 = (bf16[512,768]{1,0:T(8,128)(2,1)S(1)}, bf16[512,768]{1,0:T(8,128)(2,1)S(1)}, u32[]{:S(2)}, u32[]{:S(2)}) collective-permute-start(bf16[512,768]{1,0:T(8,128)(2,1)S(1)} %collective-permute-done.11), channel_id=1, source_target_pairs={{0,1},{1,0},{2,3},{3,2},{4,5},{5,4},{6,7},{7,6},{8,9},{9,8},{10,11... | collective-permute-start | bytes 2359304 | tf_op jit(solution)/shard_map/ppermute | solution.py:1190
  51.5 17.0 %collective-permute-start.15 = (bf16[208,768]{1,0:T(8,128)(2,1)S(1)}, bf16[208,768]{1,0:T(8,128)(2,1)S(1)}, u32[]{:S(2)}, u32[]{:S(2)}) collective-permute-start(bf16[208,768]{1,0:T(8,128)(2,1)S(1)} %collective-permute-done.12.refs_3_), channel_id=1, source_target_pairs={{0,8},{8,16},{16,24},{24,28},{28,20},{20,12},{12,4},{4,0},{1,9},{9... | collective-permute-start | bytes 958472 | tf_op jit(solution)/shard_map/ppermute | solution.py:1214
  53.2 15.3 %collective-permute-start.16 = (bf16[208,768]{1,0:T(8,128)(2,1)S(1)}, bf16[208,768]{1,0:T(8,128)(2,1)S(1)}, u32[]{:S(2)}, u32[]{:S(2)}) collective-permute-start(bf16[208,768]{1,0:T(8,128)(2,1)S(1)} %collective-permute-done.13.refs_4_), channel_id=1, source_target_pairs={{8,0},{16,8},{24,16},{28,24},{20,28},{12,20},{4,12},{0,4},{9,1},{1... | collective-permute-start | bytes 958472 | tf_op jit(solution)/shard_map/ppermute | solution.py:1214
  68.5 12.1 %collective-permute-start.17 = (bf16[208,768]{1,0:T(8,128)(2,1)S(1)}, bf16[208,768]{1,0:T(8,128)(2,1)S(1)}, u32[]{:S(2)}, u32[]{:S(2)}) collective-permute-start(bf16[208,768]{1,0:T(8,128)(2,1)S(1)} %collective-permute-done.15.refs_5_), channel_id=1, source_target_pairs={{0,8},{8,16},{16,24},{24,28},{28,20},{20,12},{12,4},{4,0},{1,9},{9... | collective-permute-start | bytes 958472 | tf_op jit(solution)/shard_map/ppermute | solution.py:1214
  111.5 2.3 collective-permute-start.18
  111.5 34.7 %collective-permute-start.20 = (bf16[4,240,768]{2,1,0:T(8,128)(2,1)S(1)}, bf16[4,240,768]{2,1,0:T(8,128)(2,1)S(1)}, u32[]{:S(2)}, u32[]{:S(2)}) collective-permute-start(bf16[4,240,768]{2,1,0:T(8,128)(2,1)S(1)} %get-tuple-element.114), channel_id=1, source_target_pairs={{0,4},{4,0},{8,12},{12,8},{16,20},{20,16},{24,28},{28,24},{1,5},{5... | collective-permute-start | bytes 4423688 | tf_op jit(solution)/shard_map/ppermute | solution.py:1237
  112.0 2.9 %collective-permute-start.19 = (bf16[512,768]{1,0:T(8,128)(2,1)S(1)}, bf16[512,768]{1,0:T(8,128)(2,1)S(1)}, u32[]{:S(2)}, u32[]{:S(2)}) collective-permute-start(bf16[512,768]{1,0:T(8,128)(2,1)S(1)} %get-tuple-element.110), channel_id=1, source_target_pairs={{0,1},{1,0},{2,3},{3,2},{4,5},{5,4},{6,7},{7,6},{8,9},{9,8},{10,11... | collective-permute-start | bytes 2359304 | tf_op jit(solution)/shard_map/ppermute | solution.py:1190
  114.0 32.2 %collective-permute-start.21 = (bf16[512,768]{1,0:T(8,128)(2,1)S(1)}, bf16[512,768]{1,0:T(8,128)(2,1)S(1)}, u32[]{:S(2)}, u32[]{:S(2)}) collective-permute-start(bf16[512,768]{1,0:T(8,128)(2,1)S(1)} %add_convert_fusion.3), channel_id=1, source_target_pairs={{0,2},{2,0},{1,3},{3,1},{4,6},{6,4},{5,7},{7,5},{8,10},{10,8},{9,1... | collective-permute-start | bytes 2359304 | tf_op jit(solution)/shard_map/ppermute | solution.py:1190
  114.9 31.3 %copy-start.31 = (bf16[512,768]{1,0:T(8,128)(2,1)}, bf16[512,768]{1,0:T(8,128)(2,1)S(1)}, u32[]{:S(2)}) copy-start(bf16[512,768]{1,0:T(8,128)(2,1)S(1)} %collective-permute-done.19) | copy-start | bytes 2359300
  160.4 8.9 %collective-permute-start.25 = (bf16[512,768]{1,0:T(8,128)(2,1)S(1)}, bf16[512,768]{1,0:T(8,128)(2,1)S(1)}, u32[]{:S(2)}, u32[]{:S(2)}) collective-permute-start(bf16[512,768]{1,0:T(8,128)(2,1)S(1)} %get-tuple-element.125), channel_id=1, source_target_pairs={{0,1},{1,0},{2,3},{3,2},{4,5},{5,4},{6,7},{7,6},{8,9},{9,8},{10,11... | collective-permute-start | bytes 2359304 | tf_op jit(solution)/shard_map/ppermute | solution.py:1190
  160.4 15.3 %collective-permute-start.22 = (bf16[240,768]{1,0:T(8,128)(2,1)S(1)}, bf16[240,768]{1,0:T(8,128)(2,1)S(1)}, u32[]{:S(2)}, u32[]{:S(2)}) collective-permute-start(bf16[240,768]{1,0:T(8,128)(2,1)S(1)} %get-tuple-element.117), channel_id=1, source_target_pairs={{0,8},{4,12},{8,16},{12,20},{16,24},{20,28},{24,0},{28,4},{1,9},{5... | collective-permute-start | bytes 1105928 | tf_op jit(solution)/shard_map/ppermute | solution.py:1225
  162.2 28.9 %collective-permute-start.23 = (bf16[240,768]{1,0:T(8,128)(2,1)S(1)}, bf16[240,768]{1,0:T(8,128)(2,1)S(1)}, u32[]{:S(2)}, u32[]{:S(2)}) collective-permute-start(bf16[240,768]{1,0:T(8,128)(2,1)S(1)} %get-tuple-element.118), channel_id=1, source_target_pairs={{0,16},{4,20},{8,24},{12,28},{16,0},{20,4},{24,8},{28,12},{1,17},{... | collective-permute-start | bytes 1105928 | tf_op jit(solution)/shard_map/ppermute | solution.py:1225
  166.6 24.5 %collective-permute-start.24 = (bf16[240,768]{1,0:T(8,128)(2,1)S(1)}, bf16[240,768]{1,0:T(8,128)(2,1)S(1)}, u32[]{:S(2)}, u32[]{:S(2)}) collective-permute-start(bf16[240,768]{1,0:T(8,128)(2,1)S(1)} %get-tuple-element.119), channel_id=1, source_target_pairs={{0,24},{4,28},{8,0},{12,4},{16,8},{20,12},{24,16},{28,20},{1,25},{... | collective-permute-start | bytes 1105928 | tf_op jit(solution)/shard_map/ppermute | solution.py:1225
  167.5 28.2 %collective-permute-start.29 = (bf16[4,112,640]{2,1,0:T(8,128)(2,1)}, bf16[4,112,640]{2,1,0:T(8,128)(2,1)S(1)}, u32[]{:S(2)}, u32[]{:S(2)}) collective-permute-start(bf16[4,112,640]{2,1,0:T(8,128)(2,1)} %get-tuple-element.134), channel_id=1, source_target_pairs={{0,4},{4,0},{8,12},{12,8},{16,20},{20,16},{24,28},{28,24},{1,5},{5... | collective-permute-start | bytes 1720328 | tf_op jit(solution)/shard_map/ppermute | solution.py:1237
  191.4 13.5 %collective-permute-start.35 = (bf16[240,768]{1,0:T(8,128)(2,1)S(1)}, bf16[240,768]{1,0:T(8,128)(2,1)}, u32[]{:S(2)}, u32[]{:S(2)}) collective-permute-start(bf16[240,768]{1,0:T(8,128)(2,1)S(1)} %add_convert_fusion.4.own), channel_id=1, source_target_pairs={{0,2},{2,0},{1,3},{3,1},{4,6},{6,4},{5,7},{7,5},{8,10},{10,8},{9,1... | collective-permute-start | bytes 1105928 | tf_op jit(solution)/shard_map/ppermute | solution.py:1190
  192.3 26.6 %collective-permute-start.28 = (bf16[512,768]{1,0:T(8,128)(2,1)}, bf16[512,768]{1,0:T(8,128)(2,1)}, u32[]{:S(2)}, u32[]{:S(2)}) collective-permute-start(bf16[512,768]{1,0:T(8,128)(2,1)} %add_convert_fusion.2), channel_id=1, source_target_pairs={{0,2},{2,0},{1,3},{3,1},{4,6},{6,4},{5,7},{7,5},{8,10},{10,8},{9,1... | collective-permute-start | bytes 2359304 | tf_op jit(solution)/shard_map/ppermute | solution.py:1190
  193.5 34.1 %collective-permute-start.27 = (bf16[512,768]{1,0:T(8,128)(2,1)}, bf16[512,768]{1,0:T(8,128)(2,1)}, u32[]{:S(2)}, u32[]{:S(2)}) collective-permute-start(bf16[512,768]{1,0:T(8,128)(2,1)} %get-tuple-element.132), channel_id=1, source_target_pairs={{0,1},{1,0},{2,3},{3,2},{4,5},{5,4},{6,7},{7,6},{8,9},{9,8},{10,11... | collective-permute-start | bytes 2359304 | tf_op jit(solution)/shard_map/ppermute | solution.py:1190
  195.1 36.9 %collective-permute-start.26 = (bf16[512,768]{1,0:T(8,128)(2,1)S(1)}, bf16[512,768]{1,0:T(8,128)(2,1)S(1)}, u32[]{:S(2)}, u32[]{:S(2)}) collective-permute-start(bf16[512,768]{1,0:T(8,128)(2,1)S(1)} %add_convert_fusion.1.mine), channel_id=1, source_target_pairs={{0,1},{1,0},{2,3},{3,2},{4,5},{5,4},{6,7},{7,6},{8,9},{9,8},{10,11... | collective-permute-start | bytes 2359304 | tf_op jit(solution)/shard_map/ppermute | solution.py:1190
  196.4 33.8 %collective-permute-start.31 = (bf16[112,640]{1,0:T(8,128)(2,1)S(1)}, bf16[112,640]{1,0:T(8,128)(2,1)S(1)}, u32[]{:S(2)}, u32[]{:S(2)}) collective-permute-start(bf16[112,640]{1,0:T(8,128)(2,1)S(1)} %get-tuple-element.138), channel_id=1, source_target_pairs={{0,8},{4,12},{8,16},{12,20},{16,24},{20,28},{24,0},{28,4},{1,9},{5... | collective-permute-start | bytes 430088 | tf_op jit(solution)/shard_map/ppermute | solution.py:1225
  207.7 1.2 collective-permute-start.36
  208.9 21.4 %collective-permute-start.32 = (bf16[112,640]{1,0:T(8,128)(2,1)S(1)}, bf16[112,640]{1,0:T(8,128)(2,1)S(1)}, u32[]{:S(2)}, u32[]{:S(2)}) collective-permute-start(bf16[112,640]{1,0:T(8,128)(2,1)S(1)} %get-tuple-element.139), channel_id=1, source_target_pairs={{0,16},{4,20},{8,24},{12,28},{16,0},{20,4},{24,8},{28,12},{1,17},{... | collective-permute-start | bytes 430088 | tf_op jit(solution)/shard_map/ppermute | solution.py:1225
  218.9 11.6 %collective-permute-start.33 = (bf16[112,640]{1,0:T(8,128)(2,1)S(1)}, bf16[112,640]{1,0:T(8,128)(2,1)S(1)}, u32[]{:S(2)}, u32[]{:S(2)}) collective-permute-start(bf16[112,640]{1,0:T(8,128)(2,1)S(1)} %get-tuple-element.140), channel_id=1, source_target_pairs={{0,24},{4,28},{8,0},{12,4},{16,8},{20,12},{24,16},{28,20},{1,25},{... | collective-permute-start | bytes 430088 | tf_op jit(solution)/shard_map/ppermute | solution.py:1225
  230.3 9.6 %collective-permute-start.30 = (bf16[512,768]{1,0:T(8,128)(2,1)}, bf16[512,768]{1,0:T(8,128)(2,1)}, u32[]{:S(2)}, u32[]{:S(2)}) collective-permute-start(bf16[512,768]{1,0:T(8,128)(2,1)} %add_convert_fusion.mine), channel_id=1, source_target_pairs={{0,1},{1,0},{2,3},{3,2},{4,5},{5,4},{6,7},{7,6},{8,9},{9,8},{10,11... | collective-permute-start | bytes 2359304 | tf_op jit(solution)/shard_map/ppermute | solution.py:1190
  230.6 6.0 %collective-permute-start.34 = (bf16[112,640]{1,0:T(8,128)(2,1)S(1)}, bf16[112,640]{1,0:T(8,128)(2,1)S(1)}, u32[]{:S(2)}, u32[]{:S(2)}) collective-permute-start(bf16[112,640]{1,0:T(8,128)(2,1)S(1)} %add_convert_fusion.5.own), channel_id=1, source_target_pairs={{0,2},{2,0},{1,3},{3,1},{4,6},{6,4},{5,7},{7,5},{8,10},{10,8},{9,1... | collective-permute-start | bytes 430088 | tf_op jit(solution)/shard_map/ppermute | solution.py:1190
  238.1 1.1 collective-permute-start.37
  (30 other events, 176.1 us)

commit v3 on v2

--- a/solution.py
+++ b/solution.py
@@ -577,8 +577,14 @@
         target[h * rows : (h + 1) * rows, :] = jnp.where(head == h, source, 0.0).astype(LOW)
 
 
-def span(j):
-    return pl.ds(pl.multiple_of(j * BLOCK, BLOCK), BLOCK)
+def span(j, size=1):
+    return pl.ds(pl.multiple_of(j * BLOCK, BLOCK), size * BLOCK)
+
+
+def sweep(first, last, work, carry):
+    pairs = (last - first) // 2
+    carry = lax.fori_loop(0, pairs, lambda i, kept: work(2, first + 2 * i, kept), carry)
+    return lax.fori_loop(first + 2 * pairs, last, lambda j, kept: work(1, j, kept), carry)
 
 
 def diagonal(raw, block, start, stop, heads):
@@ -614,26 +620,30 @@
     low = first[block]
     row = lax.broadcasted_iota(jnp.int32, (BLOCK, wide), 0)
 
-    def score(j, top):
-        raw = nt(k_ref[span(j), :], qm[...])
-        raw = jnp.where(row >= start - j * BLOCK, raw, -1e30)
-        scores[span(j), :] = raw
+    def score(masked, size, j, top):
+        raw = nt(k_ref[span(j, size), :], qm[...])
+        if masked:
+            raw = jnp.where(row >= start - j * BLOCK, raw, -1e30)
+        scores[span(j, size), :] = raw
         return jnp.maximum(top, jnp.max(raw, axis=0, keepdims=True))
 
     raw = diagonal(nt(k_ref[span(block), :], qm[...]), block, start, stop, heads)
     scores[span(block), :] = raw
-    top = lax.fori_loop(low, block, score, jnp.max(raw, axis=0, keepdims=True))
+    clear = first[count + count * (BLOCK // TILE) + block]
+    top = jnp.max(raw, axis=0, keepdims=True)
+    top = lax.fori_loop(low, clear, functools.partial(score, True, 1), top)
+    top = sweep(clear, block, functools.partial(score, False), top)
     ot[:inner, :] = jnp.zeros((inner, BLOCK), FLOAT)
 
-    def weigh(j, total):
-        weight = jnp.exp(scores[span(j), :] - top)
+    def weigh(size, j, total):
+        weight = jnp.exp(scores[span(j, size), :] - top)
         rounded = weight.astype(LOW)
         for h in range(heads):
             lines = slice(h * HEAD_DIM, (h + 1) * HEAD_DIM)
-            ot[lines, :] += nn(vt[lines, span(j)], rounded[:, h * BLOCK : (h + 1) * BLOCK])
+            ot[lines, :] += nn(vt[lines, span(j, size)], rounded[:, h * BLOCK : (h + 1) * BLOCK])
         return total + jnp.sum(weight, axis=0, keepdims=True)
 
-    total = lax.fori_loop(low, block + 1, weigh, jnp.zeros((1, wide), FLOAT))
+    total = sweep(low, block + 1, weigh, jnp.zeros((1, wide), FLOAT))
     total_out[...] = (jnp.log(total) + top).reshape(1, 1, wide)
     scale = 1.0 / total
     for h in range(heads):
@@ -717,20 +727,28 @@
     row = lax.broadcasted_iota(jnp.int32, (BLOCK, wide), 0)
     dqt[:inner, :] = jnp.zeros((inner, BLOCK), FLOAT)
 
-    def spend(j, raw):
+    def spend(j, raw, size=1):
         normal = jnp.exp(raw - total)
         weight = normal.astype(LOW)
-        change = (normal * (nt(v_ref[span(j), :], om[...]) - balance)).astype(LOW)
-        dv[span(j), :] += nn(weight, om[...])
-        dk[span(j), :] += nn(change, qm[...])
+        change = (normal * (nt(v_ref[span(j, size), :], om[...]) - balance)).astype(LOW)
+        dv[span(j, size), :] += nn(weight, om[...])
+        dk[span(j, size), :] += nn(change, qm[...])
         for h in range(heads):
             lines = slice(h * HEAD_DIM, (h + 1) * HEAD_DIM)
-            dqt[lines, :] += nn(kt[lines, span(j)], change[:, h * BLOCK : (h + 1) * BLOCK])
-
-    @pl.loop(first[block], block)
+            dqt[lines, :] += nn(kt[lines, span(j, size)], change[:, h * BLOCK : (h + 1) * BLOCK])
+
+    clear = first[count + count * (BLOCK // TILE) + block]
+
+    @pl.loop(first[block], clear)
     def _(j):
         raw = nt(k_ref[span(j), :], qm[...])
         spend(j, jnp.where(row >= start - j * BLOCK, raw, -1e30))
+
+    def plain(size, j, carry):
+        spend(j, nt(k_ref[span(j, size), :], qm[...]), size)
+        return carry
+
+    sweep(clear, block, plain, 0)
 
     spend(block, diagonal(nt(k_ref[span(block), :], qm[...]), block, start, stop, heads))
     dq = jnp.transpose(dqt[...])[:, :inner] * HEAD_DIM ** (-0.5)
@@ -852,102 +870,106 @@
                     target[f // 2, first : first + value.shape[0], : value.shape[1]] = value
 
 
-def feed_kernel(closing, place, x_ref, g_ref, m_in, *refs):
-    if closing:
-        weight, lines, total_in, sums_in, extra = refs[:5]
-        m_far, m_near, e_out, kept, sent, total, sums_all = refs[5:]
-    else:
-        pieces = refs[:8]
-        m_far, m_near, e_out, weight, lines, total, sums_all = refs[8:]
+def feed_kernel(place, own_x, peer_x, own_g, peer_g, own_m, peer_m, *refs):
+    pieces, extra, refs = refs[:8], refs[8], refs[9:]
+    own_far, own_near, peer_far, peer_near, own_e, peer_e, kept, sent, *later, weight, lines, total, sums_all = refs
     step = pl.program_id(0)
-    width = x_ref.shape[1]
+    half = pl.num_programs(0) // 2
+    width = own_x.shape[1]
     share = width // 8
 
     @pl.when(step == 0)
     def _():
-        if closing:
-            total[...] = total_in[...]
-            sums_all[...] = sums_in[...]
-        else:
-            place_pieces(place, pieces, 0, weight, 0, share)
-            place_pieces(place, pieces, share, weight, width, share)
-            lines[...] = sum_rows(pieces, 2 * share)
-            total[...] = jnp.zeros_like(total)
-            sums_all[...] = jnp.zeros_like(sums_all)
-
-    gain = lines[0:1, :]
-    unit, _ = center(x_ref[...].astype(FLOAT))
-    normed = (unit * gain + lines[1:2, :]).astype(LOW)
-    slope = g_ref[...]
-    hidden = nn(normed, weight[:width, :]) + lines[2:3, :]
-    phi = 0.5 * (1.0 + lax.erf(hidden * 0.7071067811865476))
-    active = (hidden * phi).astype(LOW)
-    fed = (nt(active, weight[width:, :]) + m_in[...].astype(FLOAT)).astype(LOW)
-    inside = phi + hidden * jnp.exp(-0.5 * hidden * hidden) * 0.3989422804014327
-    change = (nn(slope, weight[width:, :]) * inside).astype(LOW)
-    back = nt(change, weight[:width, :])
-    e_out[...] = (back * gain).astype(LOW)
-    total[:width, :] += tn(normed, change)
-    total[width:, :] += tn(slope, active)
-    rows = [
-        jnp.sum(back * unit, axis=0, keepdims=True),
-        jnp.sum(back, axis=0, keepdims=True),
-        jnp.sum(change.astype(FLOAT), axis=0, keepdims=True),
-    ]
-    if not closing:
-        once = jnp.where(place[1] == 0, 1.0, 0.0)
-        rows.append(jnp.sum(slope.astype(FLOAT), axis=0, keepdims=True) * once)
-    rows.append(jnp.zeros((16 - len(rows), width), FLOAT))
-    sums_all[...] += jnp.concatenate(rows, axis=0)
-
-    @pl.when(step == 0)
-    def _():
-        m_far[...] = fed
-
-    @pl.when(step == 1)
-    def _():
-        m_near[...] = fed
-        if closing:
-            vectors = sums_all[...].astype(LOW)
-
-            def parts(f):
-                lines_of = slice(f * share, (f + 1) * share)
-                later = slice(width + f * share, width + (f + 1) * share)
-                return [
-                    (0, total[lines_of, :].astype(LOW)),
-                    (share, total[later, :].astype(LOW)),
-                    (2 * share, vectors),
-                    (2 * share + 16, extra[f]),
-                ]
-
-            write_parts(place[10], parts, kept, sent)
-
-
-def crossed(s, place):
-    return (jnp.where(s == 0, 1 - place[1], place[1]), 0)
-
-
-def feed(place, x, g, m, pieces=None, weight=None, lines=None, sums=None, extra=None):
-    rows, width = x.shape
+        place_pieces(place, pieces, 0, weight, 0, share)
+        place_pieces(place, pieces, share, weight, width, share)
+        lines[...] = sum_rows(pieces, 2 * share)
+        total[...] = jnp.zeros_like(total)
+        sums_all[...] = jnp.zeros_like(sums_all)
+
+    def work(x_ref, g_ref, m_ref, e_out, targets, once):
+        gain = lines[0:1, :]
+        unit, _ = center(x_ref[...].astype(FLOAT))
+        normed = (unit * gain + lines[1:2, :]).astype(LOW)
+        slope = g_ref[...]
+        hidden = nn(normed, weight[:width, :]) + lines[2:3, :]
+        phi = 0.5 * (1.0 + lax.erf(hidden * 0.7071067811865476))
+        active = (hidden * phi).astype(LOW)
+        fed = (nt(active, weight[width:, :]) + m_ref[...].astype(FLOAT)).astype(LOW)
+        inside = phi + hidden * jnp.exp(-0.5 * hidden * hidden) * 0.3989422804014327
+        change = (nn(slope, weight[width:, :]) * inside).astype(LOW)
+        back = nt(change, weight[:width, :])
+        e_out[...] = (back * gain).astype(LOW)
+        total[:width, :] += tn(normed, change)
+        total[width:, :] += tn(slope, active)
+        rows = [
+            jnp.sum(back * unit, axis=0, keepdims=True),
+            jnp.sum(back, axis=0, keepdims=True),
+            jnp.sum(change.astype(FLOAT), axis=0, keepdims=True),
+            jnp.sum(slope.astype(FLOAT), axis=0, keepdims=True) * once,
+            jnp.zeros((12, width), FLOAT),
+        ]
+        sums_all[...] += jnp.concatenate(rows, axis=0)
+        for spot, target in enumerate(targets):
+
+            @pl.when(step % half == spot)
+            def _(target=target):
+                target[...] = fed
+
+    @pl.when(step < half)
+    def _():
+        work(own_x, own_g, own_m, own_e, (own_far, own_near), jnp.where(place[1] == 0, 1.0, 0.0))
+
+    @pl.when(step >= half)
+    def _():
+        work(peer_x, peer_g, peer_m, peer_e, (peer_far, peer_near), 0.0)
+
+    @pl.when(step == 2 * half - 1)
+    def _():
+        vectors = sums_all[...].astype(LOW)
+
+        def parts(f):
+            return [(0, total[f * share : (f + 1) * share, :].astype(LOW)), (share, vectors)]
+
+        write_parts(place[10], parts, kept, sent)
+        for ahead, target in enumerate(later):
+            depth = lax.rem(place[11] + ahead, 4)
+            for side in range(2):
+                f = 2 * depth + side
+                target[side, :share, :] = total[pl.ds(pl.multiple_of(width + f * share, 32), share), :].astype(LOW)
+                target[side, share:, :] = extra[f]
+
+
+def crossed(first):
+    def index(s, place):
+        return (jnp.where(s <= first, 1 - place[1], place[1]), 0)
+
+    return index
+
+
+def feed(place, own_x, peer_x, own_g, peer_g, own_m, peer_m, pieces, extra):
+    rows, width = own_x.shape
     block = (ROWS, width)
-    closing = sums is not None
-    inputs = [(x, block, crossed), (g, block, crossed), (m, block, crossed)]
-    outputs = [((ROWS, width), LOW, None, None)] * 2 + [((rows, width), LOW, block, crossed)]
-    scratch = []
-    if closing:
-        inputs += [(array, None, None) for array in (weight, lines) + sums + (extra,)]
-        outputs += [((4, width // 4 + 48, width), LOW, None, None)] * 2
-        scratch = [pltpu.VMEM((2 * width, width), FLOAT), pltpu.VMEM((16, width), FLOAT)]
-    else:
-        inputs += [(piece, None, None) for piece in pieces]
-        outputs += [
-            ((2 * width, width), LOW, None, None),
-            ((16, width), FLOAT, None, None),
-            ((2 * width, width), FLOAT, None, None),
-            ((16, width), FLOAT, None, None),
-        ]
-    kernel = functools.partial(feed_kernel, closing)
-    return call(kernel, "feed", place, 2, inputs, outputs, scratch, 12 * rows * width * width)
+    own, peer = crossed(0), crossed(2)
+    half = ((ROWS, width), LOW, None, None)
+    return call(
+        feed_kernel,
+        "feed",
+        place,
+        4,
+        [(own_x, block, own), (peer_x, block, peer), (own_g, block, own), (peer_g, block, peer)]
+        + [(own_m, block, own), (peer_m, block, peer)]
+        + [(array, None, None) for array in (*pieces, extra)],
+        [half] * 4
+        + [((rows, width), LOW, block, own), ((rows, width), LOW, block, peer)]
+        + [((4, width // 8 + 16, width), LOW, None, None)] * 2
+        + [((2, width // 8 + 32, width), LOW, None, None)] * 4,
+        [
+            pltpu.VMEM((2 * width, width), LOW),
+            pltpu.VMEM((16, width), FLOAT),
+            pltpu.VMEM((2 * width, width), FLOAT),
+            pltpu.VMEM((16, width), FLOAT),
+        ],
+    )
 
 
 def finish_kernel(
@@ -1058,6 +1080,46 @@
     )
 
 
+def cross_feed_kernel(place, kept, got, mine, *refs):
+    later, (own, one, two, three, own_late, sent_late) = refs[:3], refs[3:]
+    cross_kernel(place, kept, got, own, one, two, three)
+    for target, side in ((own_late, place[10]), (sent_late, 1 - place[10])):
+        total = mine[side].astype(FLOAT)
+        for part in later:
+            total = total + part[side].astype(FLOAT)
+        target[...] = total.astype(LOW)
+
+
+def cross_feed(place, kept, got, mine, later):
+    return call(
+        cross_feed_kernel,
+        "cross_feed",
+        place,
+        1,
+        [(array, None, None) for array in (kept, got, mine, *later)],
+        [(kept.shape[1:], LOW, None, None)] * 4 + [(mine.shape[1:], LOW, None, None)] * 2,
+    )
+
+
+def join_kernel(place, own, one, two, three, own_late, got_late, out):
+    first = own.shape[0]
+    total = own[...].astype(FLOAT) + one[...].astype(FLOAT) + two[...].astype(FLOAT) + three[...].astype(FLOAT)
+    out[:first, :] = total.astype(LOW)
+    out[first:, :] = (own_late[...].astype(FLOAT) + got_late[...].astype(FLOAT)).astype(LOW)
+
+
+def join(place, own, got, own_late, got_late):
+    rows = own.shape[0] + own_late.shape[0]
+    return call(
+        join_kernel,
+        "join",
+        place,
+        1,
+        [(array, None, None) for array in (own, *got, own_late, got_late)],
+        [((rows, own.shape[1]), LOW, None, None)],
+    )[0]
+
+
 def last_feed_kernel(place, own, far, wide, narrow, out, sums, units):
     y = place[0]
     width = own.shape[1]
@@ -1071,9 +1133,9 @@
 
     _, _, low, high = both(0, share)
     wide[...] = jnp.concatenate([low, high], axis=1)
-    _, _, low, high = both(share, share)
+    _, _, low, high = both(share + 16, share)
     narrow[...] = jnp.concatenate([low, high], axis=1)
-    mine, theirs, low, high = both(2 * share, 16)
+    mine, theirs, low, high = both(share, 16)
     sums[...] = mine + theirs
     units[...] = jnp.concatenate([low[2:3, :], high[2:3, :]], axis=1)
     _, _, low, high = both(2 * share + 16, 32)
@@ -1311,10 +1373,13 @@
     )
     stop = jnp.minimum(index + 1, begin + length).reshape(1, group)
     start = jnp.where(number == SEQS, index, begin)
-    first = jnp.min(start.reshape(group // BLOCK, BLOCK), axis=1) // BLOCK
+    blocks = start.reshape(group // BLOCK, BLOCK)
+    first = jnp.min(blocks, axis=1) // BLOCK
+    clear = (jnp.max(blocks, axis=1) + BLOCK - 1) // BLOCK
+    clear = jnp.minimum(jnp.maximum(clear, first), jnp.arange(group // BLOCK, dtype=jnp.int32))
     start = start.reshape(1, group)
     tiles = position.reshape(group // TILE, TILE)[:, 0] // TILE
-    first = jnp.concatenate([first, tiles])
+    first = jnp.concatenate([first, tiles, clear])
     tables = turning()
     place = jnp.concatenate([place, tiles])
 
@@ -1337,7 +1402,7 @@
     peer_x = ordered(far_x, swap(far_x, "tensor"), core)
     feed_ring.step()
     attend_ring.step()
-    peer_x = after(peer_x, feed_ring.newest())
+    peer_x, feed_ring.ends = after((peer_x, feed_ring.ends))
     feed_ring.step()
     q, k, v, attend_weight, attend_lines = prepare(place, own_x, peer_x, tables, attend_ring.pieces, inner)
     q, far_g = after((q, far_g), feed_ring.newest())
@@ -1349,44 +1414,46 @@
     peer_g = ordered(far_g, near_g, core)
     o, mixed_own, mixed_peer, extra = mix(place, own_g, peer_g, heads, attend_weight)
 
-    own_far, own_near, e_own, weight, lines, totals, sums = feed(place, own_x, own_g, mixed_own, pieces=feed_ring.pieces)
-    peer_far, peer_near, e_peer, kept, sent = feed(
-        place, peer_x, peer_g, mixed_peer, weight=weight, lines=lines, sums=(totals, sums), extra=extra
+    own_far, own_near, peer_far, peer_near, e_own, e_peer, kept, sent, *late = feed(
+        place, own_x, peer_x, own_g, peer_g, mixed_own, mixed_peer, feed_ring.pieces, extra
     )
     got = swap_x(sent)
+    late_got = send_along(late[1:])
     gone = add(peer_near, swap(peer_far, "tensor"))
     mixed_far = swap(gone, "context")
     own_got = swap(own_far, "tensor")
 
     o = after(o, gone, own_got)
     slope = backward(first, q, k, v, o, start, stop, total, exact, tables)
-    slope, got, mixed_far = after((slope, got, mixed_far))
-    feed_cross = cross(place, kept, got)
+    slope, got, late_got, mixed_far = after((slope, got, late_got, mixed_far))
+    feed_cross = cross_feed(place, kept, got, late[0], late_got)
     slope = after(slope, feed_cross)
-    feed_got = send_along(feed_cross[1:])
+    feed_got = send_along(feed_cross[1:4])
+    late_got = swap_x(feed_cross[5])
     peer_far, peer_near, far_own, near_own, kept, sent = finish(
         place, own_x, peer_x, own_e=e_own, peer_e=e_peer, slope=slope, lines=attend_lines, weight=attend_weight
     )
+    sent, peer_far, far_own, feed_got, late_got = after((sent, peer_far, far_own, feed_got, late_got))
     attend_got = swap_x(sent)
     peer_got = swap(peer_far, "tensor")
     e_got_own = swap(far_own, "tensor")
     gone = add(peer_near, peer_got)
     e_far = swap(gone, "context")
-    feed_got = after(feed_got, gone)
-    feed_sum = add_along(feed_cross[0], feed_got)
-    feed_far = swap(feed_sum, "context")
-    own_near = after(own_near, feed_sum)
+    feed_got, own_near = after((feed_got, own_near), gone)
+    feed_sum = join(place, feed_cross[0], feed_got, feed_cross[4], late_got)
     mine = add(own_near, own_got, mixed_far)
-    mixed = settle(place, False, own_x, attend_lines, mine, swap(mine, "tensor"))
-    attend_got = after(attend_got, feed_sum)
+    theirs = swap(mine, "tensor")
+    mixed = settle(place, False, own_x, attend_lines, mine, theirs)
+    attend_got = after(attend_got, mixed)
     attend_cross = cross(place, kept, attend_got)
     attend_along = send_along(attend_cross[1:])
     e_far = after(e_far, attend_cross[0])
     mine = add(near_own, e_got_own, e_far)
-    attend_along = after(attend_along, mine)
+    feed_far = swap(after(feed_sum, e_far), "context")
+    tokens_gradient = settle(place, True, own_x, own_g, mine, swap(mine, "tensor"))
+    attend_along = after(attend_along, tokens_gradient)
     attend_sum = add_along(attend_cross[0], attend_along)
     attend_far = swap(attend_sum, "context")
-    tokens_gradient = settle(place, True, own_x, own_g, mine, swap(mine, "tensor"))
 
     wide_slope, narrow_slope, outgoing_slope, feed_sums, unit_slope = last_feed(place, feed_sum, feed_far, inner)
     projection_slope, attend_sums, bias_slope = last_attend(place, attend_sum, attend_far, inner)

time: 246 us -> 217 us (0.88)
  waiting for transfers between devices: 57.1 us -> 45.6 us
  Pallas kernels: 109 us -> 99.7 us
  starting transfers between devices: 55.4 us -> 51.1 us
  other arithmetic: 12.1 us -> 9.35 us
    ppermute x6 -> x9, waiting for transfers between devices: 21 us -> 2.32 us  [send_along(): got.append(lax.ppermute(piece, 'fsdp', pairs))]
    ppermute x6 -> x9, starting transfers between devices: 29.8 us -> 19.7 us  [send_along(): got.append(lax.ppermute(piece, 'fsdp', pairs))]
    pallas_call x15, Pallas kernels: 109 us -> 99.7 us  [call(): pl.pallas_call(kernel, grid_spec=pltpu.PrefetchScalarGridSpec(num_scalar_...]
    ppermute x16, waiting for transfers between devices: 9.56 us -> 15.6 us  [swap(): return lax.ppermute(value, axis, PAIR)]
    ppermute x2 -> x3, starting transfers between devices: 2.26 us -> 5.68 us  [swap_x(): return lax.ppermute(value, 'fsdp', [(i, i ^ 1) for i in range(8)])]
    convert_element_type x4, other arithmetic: 5.63 us -> 3.11 us  [add(): return total.astype(LOW)]
    ppermute x2 -> x3, waiting for transfers between devices: 9.22 us -> 10.9 us  [swap_x(): return lax.ppermute(value, 'fsdp', [(i, i ^ 1) for i in range(8)])]
  transfers between devices with their start and end apart: 38 -> 42, of which waited for: 15 -> 17; matrix products, arithmetic and copies ran while one was open for 6% -> 5% of each run, Pallas kernels for 24% -> 34%
where the time goes in v3:
time: 217 us; the launch traced here: 215 us
  Pallas kernels  99.7 us (46%)
  starting transfers between devices  51.1 us (24%)
  waiting for transfers between devices  45.6 us (21%)
  other arithmetic  9.35 us (4%)
  local copies, waits for them, and re-layouts  8.41 us (4%)
    pallas_call x15, Pallas kernels, call(): pl.pallas_call(kernel, grid_spec=pltpu.PrefetchScalarGridSpec(num_scalar_...  99.7 us
    ppermute x9, starting transfers between devices, send_along(): got.append(lax.ppermute(piece, 'fsdp', pairs))  19.7 us
    ppermute x14, waiting for transfers between devices, step(): lax.ppermute(end, 'fsdp', way)  16.8 us
    ppermute x14, starting transfers between devices, step(): lax.ppermute(end, 'fsdp', way)  16 us
    ppermute x16, waiting for transfers between devices, swap(): return lax.ppermute(value, axis, PAIR)  15.6 us
    ppermute x3, waiting for transfers between devices, swap_x(): return lax.ppermute(value, 'fsdp', [(i, i ^ 1) for i in range(8)])  10.9 us
    ppermute x16, starting transfers between devices, swap(): return lax.ppermute(value, axis, PAIR)  9.69 us
    ppermute x3, starting transfers between devices, swap_x(): return lax.ppermute(value, 'fsdp', [(i, i ^ 1) for i in range(8)])  5.68 us
  transfers between devices with their start and end apart: 42, of which 17 were waited for; matrix products, arithmetic and copies ran while one was open for 5% of the time, Pallas kernels for 34%

profile of v3, /device:TPU:0, one launch (start us, length us, event | category | flops | bytes accessed | tf_op | source)
XLA Modules:
  0.0 215.5 jit_solution(15822388726269065737)
XLA Ops:
  0.8 2.3 %dynamic-slice_bitcast_fusion.1 = bf16[512,768]{1,0:T(8,128)(2,1)} fusion(bf16[1,1024,768]{2,1,0:T(8,128)(2,1)} %param.17, s32[]{:T(128)S(6)} %select_n.179), kind=kLoop, calls=%fused_computation.7 | loop fusion | bytes 1572868 | tf_op jit(solution)/shard_map/dynamic_slice | solution.py:1321
  3.1 3.0 %collective-permute-start = (bf16[512,768]{1,0:T(8,128)(2,1)}, bf16[512,768]{1,0:T(8,128)(2,1)}, u32[]{:S(2)}, u32[]{:S(2)}) collective-permute-start(bf16[512,768]{1,0:T(8,128)(2,1)} %dynamic-slice_bitcast_fusion.1), channel_id=1, source_target_pairs={{0,2},{2,0},{1,3},{3,1},{4,6},{6,4},{5,7},{7,5},{8,10},{10,8},{9,1... | collective-permute-start | bytes 2359304 | tf_op jit(solution)/shard_map/ppermute | solution.py:1252
  7.0 1.6 collective-permute-start.1
  9.0 3.8 %collective-permute-done.1.refs_1_ = bf16[112,768]{1,0:T(8,128)(2,1)S(1)} collective-permute-done((bf16[112,768]{1,0:T(8,128)(2,1)S(1)}, bf16[112,768]{1,0:T(8,128)(2,1)S(1)}, u32[]{:S(2)}, u32[]{:S(2)}) %collective-permute-start.1) | collective-permute-done | bytes 172064 | tf_op jit(solution)/shard_map/ppermute | solution.py:1276
  12.8 1.6 collective-permute-start.2
  14.9 3.4 %collective-permute-done.2.refs_3_ = bf16[112,768]{1,0:T(8,128)(2,1)S(1)} collective-permute-done((bf16[112,768]{1,0:T(8,128)(2,1)S(1)}, bf16[112,768]{1,0:T(8,128)(2,1)S(1)}, u32[]{:S(2)}, u32[]{:S(2)}) %collective-permute-start.2) | collective-permute-done | bytes 172064 | tf_op jit(solution)/shard_map/ppermute | solution.py:1276
  18.2 1.6 collective-permute-start.3
  20.4 3.3 %collective-permute-done.3.refs_5_ = bf16[112,768]{1,0:T(8,128)(2,1)S(1)} collective-permute-done((bf16[112,768]{1,0:T(8,128)(2,1)S(1)}, bf16[112,768]{1,0:T(8,128)(2,1)S(1)}, u32[]{:S(2)}, u32[]{:S(2)}) %collective-permute-start.3) | collective-permute-done | bytes 172064 | tf_op jit(solution)/shard_map/ppermute | solution.py:1276
  23.7 1.6 collective-permute-done.6.refs_6_
  28.0 1.6 collective-permute-start.8
  30.0 1.6 collective-permute-start.10
  32.1 1.5 broadcast_select_fusion.3
  34.8 3.5 %collective-permute-done.8.refs_1_ = bf16[208,768]{1,0:T(8,128)(2,1)S(1)} collective-permute-done((bf16[208,768]{1,0:T(8,128)(2,1)S(1)}, bf16[208,768]{1,0:T(8,128)(2,1)S(1)}, u32[]{:S(2)}, u32[]{:S(2)}) %collective-permute-start.8) | collective-permute-done | bytes 319520 | tf_op jit(solution)/shard_map/ppermute | solution.py:1276
  39.2 1.6 collective-permute-start.12
  41.8 7.8 %prepare.1 = (bf16[2048,192]{1,0:T(8,128)(2,1)S(1)}, bf16[2048,192]{1,0:T(8,128)(2,1)S(1)}, bf16[2048,192]{1,0:T(8,128)(2,1)S(1)}, bf16[768,768]{1,0:T(8,128)(2,1)S(1)}, f32[16,768]{1,0:T(8,128)S(1)}) custom-call(s32[29]{0:T(128)S(1)} %concatenate.13.place, bf16[1024,768]{1,0:T(8,128)(2,1)} %bitcast.51, bf16[1024,768]{1,0:T(8,128)(2,1)} %pad_maximum_fusion.peer_x, ...), custom_call_target="tpu_custom_call" | custom-call | flops 1 | bytes 1 | tf_op jit(solution)/shard_map/prepare/pallas_call | solution.py:396
  49.6 1.4 collective-permute-done.11
  51.2 1.6 collective-permute-start.15
  53.3 12.9 %forward.1 = (bf16[2048,192]{1,0:T(8,128)(2,1)S(1)}, f32[8,1,768]{2,1,0:T(1,128)S(1)}, f32[192,2048]{1,0:T(8,128)S(1)}) custom-call(s32[32]{0:T(128)S(1)} %pad_add_fusion.first, bf16[2048,192]{1,0:T(8,128)(2,1)S(1)} %get-tuple-element.107.q_ref, bf16[2048,192]{1,0:T(8,128)(2,1)S(1)} %get-tuple-element.108.k_ref, ...), custom_call_target="tpu_custom_call" | custom-call | flops 1 | bytes 1 | tf_op jit(solution)/shard_map/forward/pallas_call | solution.py:396
  66.3 2.1 collective-permute-start.17
  68.4 1.3 broadcast_select_fusion.1
  71.0 6.6 %mix.1 = (bf16[2048,192]{1,0:T(8,128)(2,1)S(1)}, bf16[1024,768]{1,0:T(8,128)(2,1)S(1)}, bf16[1024,768]{1,0:T(8,128)(2,1)}, bf16[8,32,768]{2,1,0:T(8,128)(2,1)S(1)}) custom-call(s32[29]{0:T(128)S(1)} %concatenate.13.place, bf16[1024,768]{1,0:T(8,128)(2,1)} %bitcast.56, bf16[1024,768]{1,0:T(8,128)(2,1)} %pad_maximum_fusion.1.peer_g, ...), custom_call_target="tpu_custom_call" | custom-call | flops 1 | bytes 1 | tf_op jit(solution)/shard_map/mix/pallas_call | solution.py:396
  78.8 24.1 %feed.1 = (bf16[512,768]{1,0:T(8,128)(2,1)}, bf16[512,768]{1,0:T(8,128)(2,1)}, bf16[512,768]{1,0:T(8,128)(2,1)}, bf16[512,768]{1,0:T(8,128)(2,1)}, bf16[1024,768...) custom-call(s32[29]{0:T(128)S(1)} %concatenate.13.place, ...), custom_call_target="tpu_custom_call" | custom-call | flops 1 | bytes 1 | tf_op jit(solution)/shard_map/feed/pallas_call | solution.py:396
  103.5 2.0 collective-permute-done.18
  105.5 1.3 add_convert_fusion.3
  107.4 1.7 collective-permute-start.20
  109.1 2.0 collective-permute-start.21
  112.3 2.9 %collective-permute-start.23 = (bf16[2,128,768]{2,1,0:T(8,128)(2,1)S(1)}, bf16[2,128,768]{2,1,0:T(8,128)(2,1)S(1)}, u32[]{:S(2)}, u32[]{:S(2)}) collective-permute-start(bf16[2,128,768]{2,1,0:T(8,128)(2,1)S(1)} %get-tuple-element.130), channel_id=1, source_target_pairs={{0,24},{4,28},{8,0},{12,4},{16,8},{20,12},{24,16},{28,20},{1,25},{... | collective-permute-start | bytes 1179656 | tf_op jit(solution)/shard_map/ppermute | solution.py:1287
  115.3 20.9 %backward.1.slope_ref = bf16[2048,576]{1,0:T(8,128)(2,1)} custom-call(s32[32]{0:T(128)S(1)} %pad_add_fusion.first, bf16[2048,192]{1,0:T(8,128)(2,1)S(1)} %get-tuple-element.107.q_ref, bf16[2048,192]{1,0:T(8,128)(2,1)S(1)} %get-tuple-element.108.k_ref, bf16[2048,192]{1,0:T(8,128)(2,1)S(1)} %get-tuple-element.109.v_ref, ...), custom_call_target="tpu_custom_call" | custom-call | flops 1 | bytes 1 | tf_op jit(solution)/shard_map/backward/pallas_call | solution.py:396
  136.2 2.3 %collective-permute-done.22.refs_1_ = bf16[2,128,768]{2,1,0:T(8,128)(2,1)S(1)} collective-permute-done((bf16[2,128,768]{2,1,0:T(8,128)(2,1)S(1)}, bf16[2,128,768]{2,1,0:T(8,128)(2,1)S(1)}, u32[]{:S(2)}, u32[]{:S(2)}) %collective-permute-start.22) | collective-permute-done | bytes 393248 | tf_op jit(solution)/shard_map/ppermute | solution.py:1287
  139.4 2.4 %collective-permute-start.28 = (bf16[128,768]{1,0:T(8,128)(2,1)S(1)}, bf16[128,768]{1,0:T(8,128)(2,1)S(1)}, u32[]{:S(2)}, u32[]{:S(2)}) collective-permute-start(bf16[128,768]{1,0:T(8,128)(2,1)S(1)} %get-tuple-element.143), channel_id=1, source_target_pairs={{0,4},{4,0},{8,12},{12,8},{16,20},{20,16},{24,28},{28,24},{1,5},{5... | collective-permute-start | bytes 589832 | tf_op jit(solution)/shard_map/ppermute | solution.py:1299
  141.8 7.0 %collective-permute-start.25 = (bf16[112,768]{1,0:T(8,128)(2,1)S(1)}, bf16[112,768]{1,0:T(8,128)(2,1)S(1)}, u32[]{:S(2)}, u32[]{:S(2)}) collective-permute-start(bf16[112,768]{1,0:T(8,128)(2,1)S(1)} %get-tuple-element.139), channel_id=1, source_target_pairs={{0,8},{4,12},{8,16},{12,20},{16,24},{20,28},{24,0},{28,4},{1,9},{5... | collective-permute-start | bytes 516104 | tf_op jit(solution)/shard_map/ppermute | solution.py:1287
  148.7 2.2 %collective-permute-start.26 = (bf16[112,768]{1,0:T(8,128)(2,1)S(1)}, bf16[112,768]{1,0:T(8,128)(2,1)S(1)}, u32[]{:S(2)}, u32[]{:S(2)}) collective-permute-start(bf16[112,768]{1,0:T(8,128)(2,1)S(1)} %get-tuple-element.140), channel_id=1, source_target_pairs={{0,16},{4,20},{8,24},{12,28},{16,0},{20,4},{24,8},{28,12},{1,17},{... | collective-permute-start | bytes 516104 | tf_op jit(solution)/shard_map/ppermute | solution.py:1287
  151.1 12.2 %finish.1 = (bf16[512,768]{1,0:T(8,128)(2,1)S(1)}, bf16[512,768]{1,0:T(8,128)(2,1)S(1)}, bf16[512,768]{1,0:T(8,128)(2,1)S(1)}, bf16[512,768]{1,0:T(8,128)(2,1)S(...) custom-call(s32[29]{0:T(128)S(1)} %concatenate.13.place, bf16[1024,768]{1,0:T(8,128)(2,1)} %bitcast.53, ...), custom_call_target="tpu_custom_call" | custom-call | flops 1 | bytes 1 | tf_op jit(solution)/shard_map/finish/pallas_call | solution.py:396
  163.5 2.3 %collective-permute-done.29 = bf16[512,768]{1,0:T(8,128)(2,1)S(1)} collective-permute-done((bf16[512,768]{1,0:T(8,128)(2,1)S(1)}, bf16[512,768]{1,0:T(8,128)(2,1)S(1)}, u32[]{:S(2)}, u32[]{:S(2)}) %collective-permute-start.29) | collective-permute-done | bytes 786464 | tf_op jit(solution)/shard_map/ppermute | solution.py:1252
  166.5 1.5 collective-permute-start.32
  168.1 1.7 collective-permute-start.33
  170.5 2.1 settle.2
  172.6 10.9 %collective-permute-done.33.got = bf16[4,112,640]{2,1,0:T(8,128)(2,1)S(1)} collective-permute-done((bf16[4,112,640]{2,1,0:T(8,128)(2,1)S(1)}, bf16[4,112,640]{2,1,0:T(8,128)(2,1)S(1)}, u32[]{:S(2)}, u32[]{:S(2)}) %collective-permute-start.33) | collective-permute-done | bytes 573472 | tf_op jit(solution)/shard_map/ppermute | solution.py:1299
  184.2 2.1 collective-permute-done.32
  186.3 1.5 collective-permute-start.39
  189.2 1.8 collective-permute-start.35
  191.0 1.8 collective-permute-start.36
  193.4 3.0 %collective-permute-done.39.far = bf16[240,768]{1,0:T(8,128)(2,1)} collective-permute-done((bf16[240,768]{1,0:T(8,128)(2,1)S(1)}, bf16[240,768]{1,0:T(8,128)(2,1)}, u32[]{:S(2)}, u32[]{:S(2)}) %collective-permute-start.39) | collective-permute-done | bytes 368672 | tf_op jit(solution)/shard_map/ppermute | solution.py:1252
  196.5 2.7 %last_feed.1 = (f32[96,1536]{1,0:T(8,128)}, f32[96,1536]{1,0:T(8,128)}, f32[96,384]{1,0:T(8,128)}, f32[16,768]{1,0:T(8,128)S(1)}, f32[1,1536]{1,0:T(1,128)S(1)}) custom-call(s32[29]{0:T(128)S(1)} %concatenate.13.place, bf16[240,768]{1,0:T(8,128)(2,1)S(1)} %join.1.own, bf16[240,768]{1,0:T(8,128)(2,1)} %collective-permute-done.39.far), custom_call_target="tpu_custom_call" | custom-call | flops 1 | bytes 1 | tf_op jit(solution)/shard_map/last_feed/pallas_call | solution.py:396
  200.6 5.2 %settle.3 = f32[1024,768]{1,0:T(8,128)} custom-call(s32[29]{0:T(128)S(1)} %concatenate.13.place, bf16[1024,768]{1,0:T(8,128)(2,1)S(1)} %bitcast.55, bf16[1024,768]{1,0:T(8,128)(2,1)S(1)} %bitcast.58, bf16[512,768]{1,0:T(8,128)(2,1)} %add_convert_fusion.mine, bf16[512,768]{1,0:T(8,128)(2,1)} %collective-permute-done.34.theirs), custom_call_target="tpu_custom_call" | custom-call | flops 1 | bytes 1 | tf_op jit(solution)/shard_map/settle/pallas_call | solution.py:396
  205.8 1.6 collective-permute-start.38
  207.9 3.8 %collective-permute-done.38.far = bf16[112,640]{1,0:T(8,128)(2,1)S(1)} collective-permute-done((bf16[112,640]{1,0:T(8,128)(2,1)S(1)}, bf16[112,640]{1,0:T(8,128)(2,1)S(1)}, u32[]{:S(2)}, u32[]{:S(2)}) %collective-permute-start.38) | collective-permute-done | bytes 143392 | tf_op jit(solution)/shard_map/ppermute | solution.py:1252
  211.7 1.4 last_attend.1
  (159 shorter events, 24.2 us)
Async XLA Ops:
  0.7 25.5 %copy-start.33 = (bf16[192]{0:T(256)(128)(2,1)S(1)}, bf16[192]{0:T(256)(128)(2,1)}, u32[]{:S(2)}) copy-start(bf16[192]{0:T(256)(128)(2,1)} %param.25) | copy-start | bytes 1156
  0.7 25.5 %copy-start.5 = (bf16[96,1536]{1,0:T(8,128)(2,1)S(1)}, bf16[96,1536]{1,0:T(8,128)(2,1)}, u32[]{:S(2)}) copy-start(bf16[96,1536]{1,0:T(8,128)(2,1)} %wide.1) | copy-start | bytes 884740
  0.8 25.5 %copy-start.6 = (bf16[1536,96]{0,1:T(8,128)(2,1)S(1)}, bf16[1536,96]{0,1:T(8,128)(2,1)}, u32[]{:S(2)}) copy-start(bf16[1536,96]{0,1:T(8,128)(2,1)} %param.26) | copy-start | bytes 884740
  0.8 25.5 %copy-start.17 = (bf16[96]{0:T(256)(128)(2,1)S(1)}, bf16[96]{0:T(256)(128)(2,1)}, u32[]{:S(2)}) copy-start(bf16[96]{0:T(256)(128)(2,1)} %param.30) | copy-start | bytes 580
  0.8 25.5 %copy-start.18 = (bf16[96]{0:T(256)(128)(2,1)S(1)}, bf16[96]{0:T(256)(128)(2,1)}, u32[]{:S(2)}) copy-start(bf16[96]{0:T(256)(128)(2,1)} %param.31) | copy-start | bytes 580
  0.8 26.2 %copy-start.1 = (bf16[1,1024,768]{2,1,0:T(8,128)(2,1)S(1)}, bf16[1,1024,768]{2,1,0:T(8,128)(2,1)}, u32[]{:S(2)}) copy-start(bf16[1,1024,768]{2,1,0:T(8,128)(2,1)} %param.19) | copy-start | bytes 4718596
  3.1 22.9 %collective-permute-start = (bf16[512,768]{1,0:T(8,128)(2,1)}, bf16[512,768]{1,0:T(8,128)(2,1)}, u32[]{:S(2)}, u32[]{:S(2)}) collective-permute-start(bf16[512,768]{1,0:T(8,128)(2,1)} %dynamic-slice_bitcast_fusion.1), channel_id=1, source_target_pairs={{0,2},{2,0},{1,3},{3,1},{4,6},{6,4},{5,7},{7,5},{8,10},{10,8},{9,1... | collective-permute-start | bytes 2359304 | tf_op jit(solution)/shard_map/ppermute | solution.py:1252
  7.0 5.9 %collective-permute-start.1 = (bf16[112,768]{1,0:T(8,128)(2,1)S(1)}, bf16[112,768]{1,0:T(8,128)(2,1)S(1)}, u32[]{:S(2)}, u32[]{:S(2)}) collective-permute-start(bf16[112,768]{1,0:T(8,128)(2,1)S(1)} %pack_attend.1.refs_0_), channel_id=1, source_target_pairs={{0,8},{8,16},{16,24},{24,28},{28,20},{20,12},{12,4},{4,0},{1,9},{9... | collective-permute-start | bytes 516104 | tf_op jit(solution)/shard_map/ppermute | solution.py:1276
  8.6 5.8 %collective-permute-start.4 = (bf16[112,768]{1,0:T(8,128)(2,1)S(1)}, bf16[112,768]{1,0:T(8,128)(2,1)S(1)}, u32[]{:S(2)}, u32[]{:S(2)}) collective-permute-start(bf16[112,768]{1,0:T(8,128)(2,1)S(1)} %pack_attend.1.refs_0_), channel_id=1, source_target_pairs={{8,0},{16,8},{24,16},{28,24},{20,28},{12,20},{4,12},{0,4},{9,1},{1... | collective-permute-start | bytes 516104 | tf_op jit(solution)/shard_map/ppermute | solution.py:1276
  12.8 5.4 %collective-permute-start.2 = (bf16[112,768]{1,0:T(8,128)(2,1)S(1)}, bf16[112,768]{1,0:T(8,128)(2,1)S(1)}, u32[]{:S(2)}, u32[]{:S(2)}) collective-permute-start(bf16[112,768]{1,0:T(8,128)(2,1)S(1)} %collective-permute-done.1.refs_1_), channel_id=1, source_target_pairs={{0,8},{8,16},{16,24},{24,28},{28,20},{20,12},{12,4},{4,0},{1,9},{9... | collective-permute-start | bytes 516104 | tf_op jit(solution)/shard_map/ppermute | solution.py:1276
  14.4 5.4 %collective-permute-start.5 = (bf16[112,768]{1,0:T(8,128)(2,1)S(1)}, bf16[112,768]{1,0:T(8,128)(2,1)S(1)}, u32[]{:S(2)}, u32[]{:S(2)}) collective-permute-start(bf16[112,768]{1,0:T(8,128)(2,1)S(1)} %collective-permute-done.4.refs_2_), channel_id=1, source_target_pairs={{8,0},{16,8},{24,16},{28,24},{20,28},{12,20},{4,12},{0,4},{9,1},{1... | collective-permute-start | bytes 516104 | tf_op jit(solution)/shard_map/ppermute | solution.py:1276
  18.2 5.4 %collective-permute-start.3 = (bf16[112,768]{1,0:T(8,128)(2,1)S(1)}, bf16[112,768]{1,0:T(8,128)(2,1)S(1)}, u32[]{:S(2)}, u32[]{:S(2)}) collective-permute-start(bf16[112,768]{1,0:T(8,128)(2,1)S(1)} %collective-permute-done.2.refs_3_), channel_id=1, source_target_pairs={{0,8},{8,16},{16,24},{24,28},{28,20},{20,12},{12,4},{4,0},{1,9},{9... | collective-permute-start | bytes 516104 | tf_op jit(solution)/shard_map/ppermute | solution.py:1276
  19.8 5.4 %collective-permute-start.6 = (bf16[112,768]{1,0:T(8,128)(2,1)S(1)}, bf16[112,768]{1,0:T(8,128)(2,1)S(1)}, u32[]{:S(2)}, u32[]{:S(2)}) collective-permute-start(bf16[112,768]{1,0:T(8,128)(2,1)S(1)} %collective-permute-done.5.refs_4_), channel_id=1, source_target_pairs={{8,0},{16,8},{24,16},{28,24},{20,28},{12,20},{4,12},{0,4},{9,1},{1... | collective-permute-start | bytes 516104 | tf_op jit(solution)/shard_map/ppermute | solution.py:1276
  25.9 6.2 %collective-permute-start.7 = (bf16[512,768]{1,0:T(8,128)(2,1)}, bf16[512,768]{1,0:T(8,128)(2,1)}, u32[]{:S(2)}, u32[]{:S(2)}) collective-permute-start(bf16[512,768]{1,0:T(8,128)(2,1)} %collective-permute-done), channel_id=1, source_target_pairs={{0,1},{1,0},{2,3},{3,2},{4,5},{5,4},{6,7},{7,6},{8,9},{9,8},{10,11... | collective-permute-start | bytes 2359304 | tf_op jit(solution)/shard_map/ppermute | solution.py:1252
  28.0 10.3 %collective-permute-start.8 = (bf16[208,768]{1,0:T(8,128)(2,1)S(1)}, bf16[208,768]{1,0:T(8,128)(2,1)S(1)}, u32[]{:S(2)}, u32[]{:S(2)}) collective-permute-start(bf16[208,768]{1,0:T(8,128)(2,1)S(1)} %pack_feed.1.refs_0_), channel_id=1, source_target_pairs={{0,8},{8,16},{16,24},{24,28},{28,20},{20,12},{12,4},{4,0},{1,9},{9... | collective-permute-start | bytes 958472 | tf_op jit(solution)/shard_map/ppermute | solution.py:1276
  29.5 9.7 %collective-permute-start.9 = (bf16[208,768]{1,0:T(8,128)(2,1)S(1)}, bf16[208,768]{1,0:T(8,128)(2,1)S(1)}, u32[]{:S(2)}, u32[]{:S(2)}) collective-permute-start(bf16[208,768]{1,0:T(8,128)(2,1)S(1)} %pack_feed.1.refs_0_), channel_id=1, source_target_pairs={{8,0},{16,8},{24,16},{28,24},{20,28},{12,20},{4,12},{0,4},{9,1},{1... | collective-permute-start | bytes 958472 | tf_op jit(solution)/shard_map/ppermute | solution.py:1276
  30.0 11.8 %collective-permute-start.10 = (bf16[112,768]{1,0:T(8,128)(2,1)S(1)}, bf16[112,768]{1,0:T(8,128)(2,1)S(1)}, u32[]{:S(2)}, u32[]{:S(2)}) collective-permute-start(bf16[112,768]{1,0:T(8,128)(2,1)S(1)} %copy-done.9), channel_id=1, source_target_pairs={{0,8},{8,16},{16,24},{24,28},{28,20},{20,12},{12,4},{4,0},{1,9},{9... | collective-permute-start | bytes 516104 | tf_op jit(solution)/shard_map/ppermute | solution.py:1276
  31.6 19.4 %collective-permute-start.11 = (bf16[512,768]{1,0:T(8,128)(2,1)}, bf16[512,768]{1,0:T(8,128)(2,1)}, u32[]{:S(2)}, u32[]{:S(2)}) collective-permute-start(bf16[512,768]{1,0:T(8,128)(2,1)} %dynamic-slice_bitcast_fusion), channel_id=1, source_target_pairs={{0,2},{2,0},{1,3},{3,1},{4,6},{6,4},{5,7},{7,5},{8,10},{10,8},{9,1... | collective-permute-start | bytes 2359304 | tf_op jit(solution)/shard_map/ppermute | solution.py:1252
  39.2 11.8 %collective-permute-start.12 = (bf16[208,768]{1,0:T(8,128)(2,1)S(1)}, bf16[208,768]{1,0:T(8,128)(2,1)S(1)}, u32[]{:S(2)}, u32[]{:S(2)}) collective-permute-start(bf16[208,768]{1,0:T(8,128)(2,1)S(1)} %collective-permute-done.8.refs_1_), channel_id=1, source_target_pairs={{0,8},{8,16},{16,24},{24,28},{28,20},{20,12},{12,4},{4,0},{1,9},{9... | collective-permute-start | bytes 958472 | tf_op jit(solution)/shard_map/ppermute | solution.py:1276
  40.8 10.2 %collective-permute-start.13 = (bf16[208,768]{1,0:T(8,128)(2,1)S(1)}, bf16[208,768]{1,0:T(8,128)(2,1)S(1)}, u32[]{:S(2)}, u32[]{:S(2)}) collective-permute-start(bf16[208,768]{1,0:T(8,128)(2,1)S(1)} %collective-permute-done.9.refs_2_), channel_id=1, source_target_pairs={{8,0},{16,8},{24,16},{28,24},{20,28},{12,20},{4,12},{0,4},{9,1},{1... | collective-permute-start | bytes 958472 | tf_op jit(solution)/shard_map/ppermute | solution.py:1276
  51.0 15.3 %collective-permute-start.14 = (bf16[512,768]{1,0:T(8,128)(2,1)}, bf16[512,768]{1,0:T(8,128)(2,1)S(1)}, u32[]{:S(2)}, u32[]{:S(2)}) collective-permute-start(bf16[512,768]{1,0:T(8,128)(2,1)} %collective-permute-done.11), channel_id=1, source_target_pairs={{0,1},{1,0},{2,3},{3,2},{4,5},{5,4},{6,7},{7,6},{8,9},{9,8},{10,11... | collective-permute-start | bytes 2359304 | tf_op jit(solution)/shard_map/ppermute | solution.py:1252
  51.2 15.1 %collective-permute-start.15 = (bf16[208,768]{1,0:T(8,128)(2,1)S(1)}, bf16[208,768]{1,0:T(8,128)(2,1)S(1)}, u32[]{:S(2)}, u32[]{:S(2)}) collective-permute-start(bf16[208,768]{1,0:T(8,128)(2,1)S(1)} %collective-permute-done.12.refs_3_), channel_id=1, source_target_pairs={{0,8},{8,16},{16,24},{24,28},{28,20},{20,12},{12,4},{4,0},{1,9},{9... | collective-permute-start | bytes 958472 | tf_op jit(solution)/shard_map/ppermute | solution.py:1276
  52.8 13.4 %collective-permute-start.16 = (bf16[208,768]{1,0:T(8,128)(2,1)S(1)}, bf16[208,768]{1,0:T(8,128)(2,1)S(1)}, u32[]{:S(2)}, u32[]{:S(2)}) collective-permute-start(bf16[208,768]{1,0:T(8,128)(2,1)S(1)} %collective-permute-done.13.refs_4_), channel_id=1, source_target_pairs={{8,0},{16,8},{24,16},{28,24},{20,28},{12,20},{4,12},{0,4},{9,1},{1... | collective-permute-start | bytes 958472 | tf_op jit(solution)/shard_map/ppermute | solution.py:1276
  66.3 12.5 %collective-permute-start.17 = (bf16[208,768]{1,0:T(8,128)(2,1)S(1)}, bf16[208,768]{1,0:T(8,128)(2,1)S(1)}, u32[]{:S(2)}, u32[]{:S(2)}) collective-permute-start(bf16[208,768]{1,0:T(8,128)(2,1)S(1)} %collective-permute-done.15.refs_5_), channel_id=1, source_target_pairs={{0,8},{8,16},{16,24},{24,28},{28,20},{20,12},{12,4},{4,0},{1,9},{9... | collective-permute-start | bytes 958472 | tf_op jit(solution)/shard_map/ppermute | solution.py:1276
  102.9 2.6 %collective-permute-start.18 = (bf16[512,768]{1,0:T(8,128)(2,1)}, bf16[512,768]{1,0:T(8,128)(2,1)S(1)}, u32[]{:S(2)}, u32[]{:S(2)}) collective-permute-start(bf16[512,768]{1,0:T(8,128)(2,1)} %get-tuple-element.122), channel_id=1, source_target_pairs={{0,1},{1,0},{2,3},{3,2},{4,5},{5,4},{6,7},{7,6},{8,9},{9,8},{10,11... | collective-permute-start | bytes 2359304 | tf_op jit(solution)/shard_map/ppermute | solution.py:1252
  103.0 9.3 %collective-permute-start.19 = (bf16[512,768]{1,0:T(8,128)(2,1)}, bf16[512,768]{1,0:T(8,128)(2,1)S(1)}, u32[]{:S(2)}, u32[]{:S(2)}) collective-permute-start(bf16[512,768]{1,0:T(8,128)(2,1)} %get-tuple-element.123), channel_id=1, source_target_pairs={{0,1},{1,0},{2,3},{3,2},{4,5},{5,4},{6,7},{7,6},{8,9},{9,8},{10,11... | collective-permute-start | bytes 2359304 | tf_op jit(solution)/shard_map/ppermute | solution.py:1252
  106.8 31.6 %collective-permute-start.24 = (bf16[512,768]{1,0:T(8,128)(2,1)S(1)}, bf16[512,768]{1,0:T(8,128)(2,1)S(1)}, u32[]{:S(2)}, u32[]{:S(2)}) collective-permute-start(bf16[512,768]{1,0:T(8,128)(2,1)S(1)} %add_convert_fusion.3), channel_id=1, source_target_pairs={{0,2},{2,0},{1,3},{3,1},{4,6},{6,4},{5,7},{7,5},{8,10},{10,8},{9,1... | collective-permute-start | bytes 2359304 | tf_op jit(solution)/shard_map/ppermute | solution.py:1252
  107.4 31.1 %collective-permute-start.20 = (bf16[4,112,768]{2,1,0:T(8,128)(2,1)S(1)}, bf16[4,112,768]{2,1,0:T(8,128)(2,1)S(1)}, u32[]{:S(2)}, u32[]{:S(2)}) collective-permute-start(bf16[4,112,768]{2,1,0:T(8,128)(2,1)S(1)} %get-tuple-element.127), channel_id=1, source_target_pairs={{0,4},{4,0},{8,12},{12,8},{16,20},{20,16},{24,28},{28,24},{1,5},{5... | collective-permute-start | bytes 2064392 | tf_op jit(solution)/shard_map/ppermute | solution.py:1299
  109.1 27.1 %collective-permute-start.21 = (bf16[2,128,768]{2,1,0:T(8,128)(2,1)S(1)}, bf16[2,128,768]{2,1,0:T(8,128)(2,1)S(1)}, u32[]{:S(2)}, u32[]{:S(2)}) collective-permute-start(bf16[2,128,768]{2,1,0:T(8,128)(2,1)S(1)} %get-tuple-element.128), channel_id=1, source_target_pairs={{0,8},{4,12},{8,16},{12,20},{16,24},{20,28},{24,0},{28,4},{1,9},{5... | collective-permute-start | bytes 1179656 | tf_op jit(solution)/shard_map/ppermute | solution.py:1287
  111.1 27.4 %collective-permute-start.22 = (bf16[2,128,768]{2,1,0:T(8,128)(2,1)S(1)}, bf16[2,128,768]{2,1,0:T(8,128)(2,1)S(1)}, u32[]{:S(2)}, u32[]{:S(2)}) collective-permute-start(bf16[2,128,768]{2,1,0:T(8,128)(2,1)S(1)} %get-tuple-element.129), channel_id=1, source_target_pairs={{0,16},{4,20},{8,24},{12,28},{16,0},{20,4},{24,8},{28,12},{1,17},{... | collective-permute-start | bytes 1179656 | tf_op jit(solution)/shard_map/ppermute | solution.py:1287
  112.3 26.1 %collective-permute-start.23 = (bf16[2,128,768]{2,1,0:T(8,128)(2,1)S(1)}, bf16[2,128,768]{2,1,0:T(8,128)(2,1)S(1)}, u32[]{:S(2)}, u32[]{:S(2)}) collective-permute-start(bf16[2,128,768]{2,1,0:T(8,128)(2,1)S(1)} %get-tuple-element.130), channel_id=1, source_target_pairs={{0,24},{4,28},{8,0},{12,4},{16,8},{20,12},{24,16},{28,20},{1,25},{... | collective-permute-start | bytes 1179656 | tf_op jit(solution)/shard_map/ppermute | solution.py:1287
  139.4 24.0 %collective-permute-start.28 = (bf16[128,768]{1,0:T(8,128)(2,1)S(1)}, bf16[128,768]{1,0:T(8,128)(2,1)S(1)}, u32[]{:S(2)}, u32[]{:S(2)}) collective-permute-start(bf16[128,768]{1,0:T(8,128)(2,1)S(1)} %get-tuple-element.143), channel_id=1, source_target_pairs={{0,4},{4,0},{8,12},{12,8},{16,20},{20,16},{24,28},{28,24},{1,5},{5... | collective-permute-start | bytes 589832 | tf_op jit(solution)/shard_map/ppermute | solution.py:1299
  141.8 21.6 %collective-permute-start.25 = (bf16[112,768]{1,0:T(8,128)(2,1)S(1)}, bf16[112,768]{1,0:T(8,128)(2,1)S(1)}, u32[]{:S(2)}, u32[]{:S(2)}) collective-permute-start(bf16[112,768]{1,0:T(8,128)(2,1)S(1)} %get-tuple-element.139), channel_id=1, source_target_pairs={{0,8},{4,12},{8,16},{12,20},{16,24},{20,28},{24,0},{28,4},{1,9},{5... | collective-permute-start | bytes 516104 | tf_op jit(solution)/shard_map/ppermute | solution.py:1287
  148.7 14.6 %collective-permute-start.26 = (bf16[112,768]{1,0:T(8,128)(2,1)S(1)}, bf16[112,768]{1,0:T(8,128)(2,1)S(1)}, u32[]{:S(2)}, u32[]{:S(2)}) collective-permute-start(bf16[112,768]{1,0:T(8,128)(2,1)S(1)} %get-tuple-element.140), channel_id=1, source_target_pairs={{0,16},{4,20},{8,24},{12,28},{16,0},{20,4},{24,8},{28,12},{1,17},{... | collective-permute-start | bytes 516104 | tf_op jit(solution)/shard_map/ppermute | solution.py:1287
  151.0 12.4 %collective-permute-start.27 = (bf16[112,768]{1,0:T(8,128)(2,1)S(1)}, bf16[112,768]{1,0:T(8,128)(2,1)S(1)}, u32[]{:S(2)}, u32[]{:S(2)}) collective-permute-start(bf16[112,768]{1,0:T(8,128)(2,1)S(1)} %get-tuple-element.141), channel_id=1, source_target_pairs={{0,24},{4,28},{8,0},{12,4},{16,8},{20,12},{24,16},{28,20},{1,25},{... | collective-permute-start | bytes 516104 | tf_op jit(solution)/shard_map/ppermute | solution.py:1287
  163.4 2.4 %collective-permute-start.29 = (bf16[512,768]{1,0:T(8,128)(2,1)S(1)}, bf16[512,768]{1,0:T(8,128)(2,1)S(1)}, u32[]{:S(2)}, u32[]{:S(2)}) collective-permute-start(bf16[512,768]{1,0:T(8,128)(2,1)S(1)} %get-tuple-element.153), channel_id=1, source_target_pairs={{0,1},{1,0},{2,3},{3,2},{4,5},{5,4},{6,7},{7,6},{8,9},{9,8},{10,11... | collective-permute-start | bytes 2359304 | tf_op jit(solution)/shard_map/ppermute | solution.py:1252
  166.3 4.2 %collective-permute-start.30 = (bf16[512,768]{1,0:T(8,128)(2,1)S(1)}, bf16[512,768]{1,0:T(8,128)(2,1)S(1)}, u32[]{:S(2)}, u32[]{:S(2)}) collective-permute-start(bf16[512,768]{1,0:T(8,128)(2,1)S(1)} %add_convert_fusion.1.mine), channel_id=1, source_target_pairs={{0,1},{1,0},{2,3},{3,2},{4,5},{5,4},{6,7},{7,6},{8,9},{9,8},{10,11... | collective-permute-start | bytes 2359304 | tf_op jit(solution)/shard_map/ppermute | solution.py:1252
  166.5 19.8 %collective-permute-start.32 = (bf16[512,768]{1,0:T(8,128)(2,1)S(1)}, bf16[512,768]{1,0:T(8,128)(2,1)S(1)}, u32[]{:S(2)}, u32[]{:S(2)}) collective-permute-start(bf16[512,768]{1,0:T(8,128)(2,1)S(1)} %add_convert_fusion.2), channel_id=1, source_target_pairs={{0,2},{2,0},{1,3},{3,1},{4,6},{6,4},{5,7},{7,5},{8,10},{10,8},{9,1... | collective-permute-start | bytes 2359304 | tf_op jit(solution)/shard_map/ppermute | solution.py:1252
  168.0 19.8 %collective-permute-start.31 = (bf16[512,768]{1,0:T(8,128)(2,1)S(1)}, bf16[512,768]{1,0:T(8,128)(2,1)S(1)}, u32[]{:S(2)}, u32[]{:S(2)}) collective-permute-start(bf16[512,768]{1,0:T(8,128)(2,1)S(1)} %get-tuple-element.157), channel_id=1, source_target_pairs={{0,1},{1,0},{2,3},{3,2},{4,5},{5,4},{6,7},{7,6},{8,9},{9,8},{10,11... | collective-permute-start | bytes 2359304 | tf_op jit(solution)/shard_map/ppermute | solution.py:1252
  168.1 15.3 %collective-permute-start.33 = (bf16[4,112,640]{2,1,0:T(8,128)(2,1)S(1)}, bf16[4,112,640]{2,1,0:T(8,128)(2,1)S(1)}, u32[]{:S(2)}, u32[]{:S(2)}) collective-permute-start(bf16[4,112,640]{2,1,0:T(8,128)(2,1)S(1)} %get-tuple-element.159), channel_id=1, source_target_pairs={{0,4},{4,0},{8,12},{12,8},{16,20},{20,16},{24,28},{28,24},{1,5},{5... | collective-permute-start | bytes 1720328 | tf_op jit(solution)/shard_map/ppermute | solution.py:1299
  186.3 10.2 %collective-permute-start.39 = (bf16[240,768]{1,0:T(8,128)(2,1)S(1)}, bf16[240,768]{1,0:T(8,128)(2,1)}, u32[]{:S(2)}, u32[]{:S(2)}) collective-permute-start(bf16[240,768]{1,0:T(8,128)(2,1)S(1)} %join.1.own), channel_id=1, source_target_pairs={{0,2},{2,0},{1,3},{3,1},{4,6},{6,4},{5,7},{7,5},{8,10},{10,8},{9,1... | collective-permute-start | bytes 1105928 | tf_op jit(solution)/shard_map/ppermute | solution.py:1252
  189.1 11.4 %collective-permute-start.34 = (bf16[512,768]{1,0:T(8,128)(2,1)}, bf16[512,768]{1,0:T(8,128)(2,1)}, u32[]{:S(2)}, u32[]{:S(2)}) collective-permute-start(bf16[512,768]{1,0:T(8,128)(2,1)} %add_convert_fusion.mine), channel_id=1, source_target_pairs={{0,1},{1,0},{2,3},{3,2},{4,5},{5,4},{6,7},{7,6},{8,9},{9,8},{10,11... | collective-permute-start | bytes 2359304 | tf_op jit(solution)/shard_map/ppermute | solution.py:1252
  189.2 16.5 %collective-permute-start.35 = (bf16[112,640]{1,0:T(8,128)(2,1)}, bf16[112,640]{1,0:T(8,128)(2,1)S(1)}, u32[]{:S(2)}, u32[]{:S(2)}) collective-permute-start(bf16[112,640]{1,0:T(8,128)(2,1)} %copy-done.25), channel_id=1, source_target_pairs={{0,8},{4,12},{8,16},{12,20},{16,24},{20,28},{24,0},{28,4},{1,9},{5... | collective-permute-start | bytes 430088 | tf_op jit(solution)/shard_map/ppermute | solution.py:1287
  191.0 14.7 %collective-permute-start.36 = (bf16[112,640]{1,0:T(8,128)(2,1)}, bf16[112,640]{1,0:T(8,128)(2,1)S(1)}, u32[]{:S(2)}, u32[]{:S(2)}) collective-permute-start(bf16[112,640]{1,0:T(8,128)(2,1)} %copy-done.24), channel_id=1, source_target_pairs={{0,16},{4,20},{8,24},{12,28},{16,0},{20,4},{24,8},{28,12},{1,17},{... | collective-permute-start | bytes 430088 | tf_op jit(solution)/shard_map/ppermute | solution.py:1287
  192.8 12.9 %collective-permute-start.37 = (bf16[112,640]{1,0:T(8,128)(2,1)}, bf16[112,640]{1,0:T(8,128)(2,1)S(1)}, u32[]{:S(2)}, u32[]{:S(2)}) collective-permute-start(bf16[112,640]{1,0:T(8,128)(2,1)} %copy-done.23), channel_id=1, source_target_pairs={{0,24},{4,28},{8,0},{12,4},{16,8},{20,12},{24,16},{28,20},{1,25},{... | collective-permute-start | bytes 430088 | tf_op jit(solution)/shard_map/ppermute | solution.py:1287
  199.3 1.2 collective-permute-start.40
  205.8 5.9 %collective-permute-start.38 = (bf16[112,640]{1,0:T(8,128)(2,1)S(1)}, bf16[112,640]{1,0:T(8,128)(2,1)S(1)}, u32[]{:S(2)}, u32[]{:S(2)}) collective-permute-start(bf16[112,640]{1,0:T(8,128)(2,1)S(1)} %add_convert_fusion.4.own), channel_id=1, source_target_pairs={{0,2},{2,0},{1,3},{3,1},{4,6},{6,4},{5,7},{7,5},{8,10},{10,8},{9,1... | collective-permute-start | bytes 430088 | tf_op jit(solution)/shard_map/ppermute | solution.py:1252
  213.2 1.1 collective-permute-start.41
  (28 other events, 182.9 us)

commit v4 on v3

--- a/solution.py
+++ b/solution.py
@@ -928,15 +928,16 @@
         vectors = sums_all[...].astype(LOW)
 
         def parts(f):
-            return [(0, total[f * share : (f + 1) * share, :].astype(LOW)), (share, vectors)]
+            later_rows = slice(width + f * share, width + (f + 1) * share)
+            return [(0, total[later_rows, :].astype(LOW)), (share, extra[f])]
 
         write_parts(place[10], parts, kept, sent)
         for ahead, target in enumerate(later):
             depth = lax.rem(place[11] + ahead, 4)
             for side in range(2):
                 f = 2 * depth + side
-                target[side, :share, :] = total[pl.ds(pl.multiple_of(width + f * share, 32), share), :].astype(LOW)
-                target[side, share:, :] = extra[f]
+                target[side, :share, :] = total[pl.ds(pl.multiple_of(f * share, 32), share), :].astype(LOW)
+                target[side, share:, :] = vectors
 
 
 def crossed(first):
@@ -961,8 +962,8 @@
         + [(array, None, None) for array in (*pieces, extra)],
         [half] * 4
         + [((rows, width), LOW, block, own), ((rows, width), LOW, block, peer)]
-        + [((4, width // 8 + 16, width), LOW, None, None)] * 2
-        + [((2, width // 8 + 32, width), LOW, None, None)] * 4,
+        + [((4, width // 8 + 32, width), LOW, None, None)] * 2
+        + [((2, width // 8 + 16, width), LOW, None, None)] * 4,
         [
             pltpu.VMEM((2 * width, width), LOW),
             pltpu.VMEM((16, width), FLOAT),
@@ -1131,14 +1132,14 @@
         theirs = far[first : first + count, :].astype(FLOAT)
         return mine, theirs, pick(y, mine, theirs), pick(y, theirs, mine)
 
+    _, _, low, high = both(share + 32, share)
+    wide[...] = jnp.concatenate([low, high], axis=1)
     _, _, low, high = both(0, share)
-    wide[...] = jnp.concatenate([low, high], axis=1)
-    _, _, low, high = both(share + 16, share)
     narrow[...] = jnp.concatenate([low, high], axis=1)
-    mine, theirs, low, high = both(share, 16)
+    mine, theirs, low, high = both(2 * share + 32, 16)
     sums[...] = mine + theirs
     units[...] = jnp.concatenate([low[2:3, :], high[2:3, :]], axis=1)
-    _, _, low, high = both(2 * share + 16, 32)
+    _, _, low, high = both(share, 32)
 
     def column(value):
         return jnp.concatenate([value[:, c * inner : (c + 1) * inner] for c in range(3)], axis=0)

time: 217 us -> 221 us (1.018)
  starting transfers between devices: 51.1 us -> 56.7 us
    ppermute x14, starting transfers between devices: 16 us -> 23.8 us  [step(): lax.ppermute(end, 'fsdp', way)]
    ppermute x3, starting transfers between devices: 5.68 us -> 2.03 us  [swap_x(): return lax.ppermute(value, 'fsdp', [(i, i ^ 1) for i in range(8)])]
  transfers between devices with their start and end apart: 42 -> 42, of which waited for: 17 -> 17; matrix products, arithmetic and copies ran while one was open for 5% -> 5% of each run, Pallas kernels for 34% -> 32%
where the time goes in v4:
time: 221 us; the launch traced here: 220 us
  Pallas kernels  97.6 us (44%)
  starting transfers between devices  56.7 us (26%)
  waiting for transfers between devices  44.8 us (20%)
  local copies, waits for them, and re-layouts  9.94 us (4%)
  other arithmetic  9.28 us (4%)
    pallas_call x15, Pallas kernels, call(): pl.pallas_call(kernel, grid_spec=pltpu.PrefetchScalarGridSpec(num_scalar_...  97.6 us
    ppermute x14, starting transfers between devices, step(): lax.ppermute(end, 'fsdp', way)  23.8 us
    ppermute x9, starting transfers between devices, send_along(): got.append(lax.ppermute(piece, 'fsdp', pairs))  21.3 us
    ppermute x14, waiting for transfers between devices, step(): lax.ppermute(end, 'fsdp', way)  16.8 us
    ppermute x16, waiting for transfers between devices, swap(): return lax.ppermute(value, axis, PAIR)  14.1 us
    ppermute x3, waiting for transfers between devices, swap_x(): return lax.ppermute(value, 'fsdp', [(i, i ^ 1) for i in range(8)])  10.8 us
    ppermute x16, starting transfers between devices, swap(): return lax.ppermute(value, axis, PAIR)  9.65 us
  transfers between devices with their start and end apart: 42, of which 17 were waited for; matrix products, arithmetic and copies ran while one was open for 5% of the time, Pallas kernels for 32%

profile of v4, /device:TPU:0, one launch (start us, length us, event | category | flops | bytes accessed | tf_op | source)
XLA Modules:
  0.0 219.6 jit_solution(8593555506235670413)
XLA Ops:
  0.8 2.3 %dynamic-slice_bitcast_fusion.1 = bf16[512,768]{1,0:T(8,128)(2,1)} fusion(bf16[1,1024,768]{2,1,0:T(8,128)(2,1)} %param.17, s32[]{:T(128)S(6)} %select_n.179), kind=kLoop, calls=%fused_computation.7 | loop fusion | bytes 1572868 | tf_op jit(solution)/shard_map/dynamic_slice | solution.py:1322
  3.1 3.0 %collective-permute-start = (bf16[512,768]{1,0:T(8,128)(2,1)}, bf16[512,768]{1,0:T(8,128)(2,1)}, u32[]{:S(2)}, u32[]{:S(2)}) collective-permute-start(bf16[512,768]{1,0:T(8,128)(2,1)} %dynamic-slice_bitcast_fusion.1), channel_id=1, source_target_pairs={{0,2},{2,0},{1,3},{3,1},{4,6},{6,4},{5,7},{7,5},{8,10},{10,8},{9,1... | collective-permute-start | bytes 2359304 | tf_op jit(solution)/shard_map/ppermute | solution.py:1253
  7.0 1.6 collective-permute-start.1
  9.0 3.8 %collective-permute-done.1.refs_1_ = bf16[112,768]{1,0:T(8,128)(2,1)S(1)} collective-permute-done((bf16[112,768]{1,0:T(8,128)(2,1)S(1)}, bf16[112,768]{1,0:T(8,128)(2,1)S(1)}, u32[]{:S(2)}, u32[]{:S(2)}) %collective-permute-start.1) | collective-permute-done | bytes 172064 | tf_op jit(solution)/shard_map/ppermute | solution.py:1277
  12.8 1.6 collective-permute-start.2
  14.9 3.4 %collective-permute-done.2.refs_3_ = bf16[112,768]{1,0:T(8,128)(2,1)S(1)} collective-permute-done((bf16[112,768]{1,0:T(8,128)(2,1)S(1)}, bf16[112,768]{1,0:T(8,128)(2,1)S(1)}, u32[]{:S(2)}, u32[]{:S(2)}) %collective-permute-start.2) | collective-permute-done | bytes 172064 | tf_op jit(solution)/shard_map/ppermute | solution.py:1277
  18.2 1.6 collective-permute-start.3
  20.4 3.4 %collective-permute-done.3.refs_5_ = bf16[112,768]{1,0:T(8,128)(2,1)} collective-permute-done((bf16[112,768]{1,0:T(8,128)(2,1)S(1)}, bf16[112,768]{1,0:T(8,128)(2,1)}, u32[]{:S(2)}, u32[]{:S(2)}) %collective-permute-start.3) | collective-permute-done | bytes 172064 | tf_op jit(solution)/shard_map/ppermute | solution.py:1277
  23.8 1.5 collective-permute-done.6.refs_6_
  28.0 1.6 collective-permute-start.8
  30.0 1.6 collective-permute-start.10
  32.1 1.5 broadcast_select_fusion.3
  33.6 1.2 pad_maximum_fusion.peer_x
  34.9 3.4 %collective-permute-done.8.refs_1_ = bf16[208,768]{1,0:T(8,128)(2,1)S(1)} collective-permute-done((bf16[208,768]{1,0:T(8,128)(2,1)S(1)}, bf16[208,768]{1,0:T(8,128)(2,1)S(1)}, u32[]{:S(2)}, u32[]{:S(2)}) %collective-permute-start.8) | collective-permute-done | bytes 319520 | tf_op jit(solution)/shard_map/ppermute | solution.py:1277
  39.2 1.6 collective-permute-start.12
  41.8 7.8 %prepare.1 = (bf16[2048,192]{1,0:T(8,128)(2,1)S(1)}, bf16[2048,192]{1,0:T(8,128)(2,1)S(1)}, bf16[2048,192]{1,0:T(8,128)(2,1)S(1)}, bf16[768,768]{1,0:T(8,128)(2,1)S(1)}, f32[16,768]{1,0:T(8,128)S(1)}) custom-call(s32[29]{0:T(128)S(1)} %concatenate.13.place, bf16[1024,768]{1,0:T(8,128)(2,1)} %bitcast.51, bf16[1024,768]{1,0:T(8,128)(2,1)} %pad_maximum_fusion.peer_x, ...), custom_call_target="tpu_custom_call" | custom-call | flops 1 | bytes 1 | tf_op jit(solution)/shard_map/prepare/pallas_call | solution.py:396
  49.7 1.3 collective-permute-done.11
  51.2 1.6 collective-permute-start.15
  53.3 12.0 %forward.1 = (bf16[2048,192]{1,0:T(8,128)(2,1)S(1)}, f32[8,1,768]{2,1,0:T(1,128)S(1)}, f32[192,2048]{1,0:T(8,128)S(1)}) custom-call(s32[32]{0:T(128)S(1)} %pad_add_fusion.first, bf16[2048,192]{1,0:T(8,128)(2,1)S(1)} %get-tuple-element.107.q_ref, bf16[2048,192]{1,0:T(8,128)(2,1)S(1)} %get-tuple-element.108.k_ref, ...), custom_call_target="tpu_custom_call" | custom-call | flops 1 | bytes 1 | tf_op jit(solution)/shard_map/forward/pallas_call | solution.py:396
  65.4 9.9 %collective-permute-start.17 = (bf16[208,768]{1,0:T(8,128)(2,1)S(1)}, bf16[208,768]{1,0:T(8,128)(2,1)S(1)}, u32[]{:S(2)}, u32[]{:S(2)}) collective-permute-start(bf16[208,768]{1,0:T(8,128)(2,1)S(1)} %collective-permute-done.15.refs_5_), channel_id=1, source_target_pairs={{0,8},{8,16},{16,24},{24,28},{28,20},{20,12},{12,4},{4,0},{1,9},{9... | collective-permute-start | bytes 958472 | tf_op jit(solution)/shard_map/ppermute | solution.py:1277
  75.3 1.2 broadcast_select_fusion.1
  76.6 1.2 pad_maximum_fusion.1.peer_g
  77.8 6.6 %mix.1 = (bf16[2048,192]{1,0:T(8,128)(2,1)S(1)}, bf16[1024,768]{1,0:T(8,128)(2,1)S(1)}, bf16[1024,768]{1,0:T(8,128)(2,1)}, bf16[8,32,768]{2,1,0:T(8,128)(2,1)S(1)}) custom-call(s32[29]{0:T(128)S(1)} %concatenate.13.place, bf16[1024,768]{1,0:T(8,128)(2,1)} %bitcast.56, bf16[1024,768]{1,0:T(8,128)(2,1)} %pad_maximum_fusion.1.peer_g, ...), custom_call_target="tpu_custom_call" | custom-call | flops 1 | bytes 1 | tf_op jit(solution)/shard_map/mix/pallas_call | solution.py:396
  85.6 24.2 %feed.1 = (bf16[512,768]{1,0:T(8,128)(2,1)S(1)}, bf16[512,768]{1,0:T(8,128)(2,1)S(1)}, bf16[512,768]{1,0:T(8,128)(2,1)}, bf16[512,768]{1,0:T(8,128)(2,1)}, bf16[...) custom-call(s32[29]{0:T(128)S(1)} %concatenate.13.place, ...), custom_call_target="tpu_custom_call" | custom-call | flops 1 | bytes 1 | tf_op jit(solution)/shard_map/feed/pallas_call | solution.py:396
  110.4 2.3 %collective-permute-done.18 = bf16[512,768]{1,0:T(8,128)(2,1)S(1)} collective-permute-done((bf16[512,768]{1,0:T(8,128)(2,1)}, bf16[512,768]{1,0:T(8,128)(2,1)S(1)}, u32[]{:S(2)}, u32[]{:S(2)}) %collective-permute-start.18) | collective-permute-done | bytes 786464 | tf_op jit(solution)/shard_map/ppermute | solution.py:1253
  112.7 1.3 add_convert_fusion.3
  114.6 3.9 %collective-permute-start.23 = (bf16[2,112,768]{2,1,0:T(8,128)(2,1)S(1)}, bf16[2,112,768]{2,1,0:T(8,128)(2,1)S(1)}, u32[]{:S(2)}, u32[]{:S(2)}) collective-permute-start(bf16[2,112,768]{2,1,0:T(8,128)(2,1)S(1)} %get-tuple-element.130), channel_id=1, source_target_pairs={{0,24},{4,28},{8,0},{12,4},{16,8},{20,12},{24,16},{28,20},{1,25},{... | collective-permute-start | bytes 1032200 | tf_op jit(solution)/shard_map/ppermute | solution.py:1288
  118.5 19.5 %backward.1.slope_ref = bf16[2048,576]{1,0:T(8,128)(2,1)} custom-call(s32[32]{0:T(128)S(1)} %pad_add_fusion.first, bf16[2048,192]{1,0:T(8,128)(2,1)S(1)} %get-tuple-element.107.q_ref, bf16[2048,192]{1,0:T(8,128)(2,1)S(1)} %get-tuple-element.108.k_ref, bf16[2048,192]{1,0:T(8,128)(2,1)S(1)} %get-tuple-element.109.v_ref, ...), custom_call_target="tpu_custom_call" | custom-call | flops 1 | bytes 1 | tf_op jit(solution)/shard_map/backward/pallas_call | solution.py:396
  138.0 3.1 %collective-permute-done.22.refs_1_ = bf16[2,112,768]{2,1,0:T(8,128)(2,1)S(1)} collective-permute-done((bf16[2,112,768]{2,1,0:T(8,128)(2,1)S(1)}, bf16[2,112,768]{2,1,0:T(8,128)(2,1)S(1)}, u32[]{:S(2)}, u32[]{:S(2)}) %collective-permute-start.22) | collective-permute-done | bytes 344096 | tf_op jit(solution)/shard_map/ppermute | solution.py:1288
  143.0 9.8 %collective-permute-start.25 = (bf16[128,768]{1,0:T(8,128)(2,1)S(1)}, bf16[128,768]{1,0:T(8,128)(2,1)S(1)}, u32[]{:S(2)}, u32[]{:S(2)}) collective-permute-start(bf16[128,768]{1,0:T(8,128)(2,1)S(1)} %get-tuple-element.139), channel_id=1, source_target_pairs={{0,8},{4,12},{8,16},{12,20},{16,24},{20,28},{24,0},{28,4},{1,9},{5... | collective-permute-start | bytes 589832 | tf_op jit(solution)/shard_map/ppermute | solution.py:1288
  152.8 2.4 %collective-permute-start.27 = (bf16[128,768]{1,0:T(8,128)(2,1)S(1)}, bf16[128,768]{1,0:T(8,128)(2,1)S(1)}, u32[]{:S(2)}, u32[]{:S(2)}) collective-permute-start(bf16[128,768]{1,0:T(8,128)(2,1)S(1)} %get-tuple-element.141), channel_id=1, source_target_pairs={{0,24},{4,28},{8,0},{12,4},{16,8},{20,12},{24,16},{28,20},{1,25},{... | collective-permute-start | bytes 589832 | tf_op jit(solution)/shard_map/ppermute | solution.py:1288
  155.2 12.2 %finish.1 = (bf16[512,768]{1,0:T(8,128)(2,1)S(1)}, bf16[512,768]{1,0:T(8,128)(2,1)S(1)}, bf16[512,768]{1,0:T(8,128)(2,1)S(1)}, bf16[512,768]{1,0:T(8,128)(2,1)S(...) custom-call(s32[29]{0:T(128)S(1)} %concatenate.13.place, bf16[1024,768]{1,0:T(8,128)(2,1)} %bitcast.53, ...), custom_call_target="tpu_custom_call" | custom-call | flops 1 | bytes 1 | tf_op jit(solution)/shard_map/finish/pallas_call | solution.py:396
  167.6 2.3 %collective-permute-done.29 = bf16[512,768]{1,0:T(8,128)(2,1)S(1)} collective-permute-done((bf16[512,768]{1,0:T(8,128)(2,1)S(1)}, bf16[512,768]{1,0:T(8,128)(2,1)S(1)}, u32[]{:S(2)}, u32[]{:S(2)}) %collective-permute-start.29) | collective-permute-done | bytes 786464 | tf_op jit(solution)/shard_map/ppermute | solution.py:1253
  170.7 1.5 collective-permute-start.32
  172.3 2.0 collective-permute-start.33
  175.0 2.1 settle.2
  177.1 10.8 %collective-permute-done.33.got = bf16[4,112,640]{2,1,0:T(8,128)(2,1)S(1)} collective-permute-done((bf16[4,112,640]{2,1,0:T(8,128)(2,1)S(1)}, bf16[4,112,640]{2,1,0:T(8,128)(2,1)S(1)}, u32[]{:S(2)}, u32[]{:S(2)}) %collective-permute-start.33) | collective-permute-done | bytes 573472 | tf_op jit(solution)/shard_map/ppermute | solution.py:1300
  189.2 1.2 collective-permute-done.32
  190.5 1.5 collective-permute-start.39
  192.0 1.3 add_convert_fusion.mine
  193.3 1.7 collective-permute-start.35
  195.0 3.4 %collective-permute-start.36 = (bf16[112,640]{1,0:T(8,128)(2,1)}, bf16[112,640]{1,0:T(8,128)(2,1)S(1)}, u32[]{:S(2)}, u32[]{:S(2)}) collective-permute-start(bf16[112,640]{1,0:T(8,128)(2,1)} %copy-done.27), channel_id=1, source_target_pairs={{0,16},{4,20},{8,24},{12,28},{16,0},{20,4},{24,8},{28,12},{1,17},{... | collective-permute-start | bytes 430088 | tf_op jit(solution)/shard_map/ppermute | solution.py:1288
  198.4 2.2 %collective-permute-done.39.far = bf16[240,768]{1,0:T(8,128)(2,1)} collective-permute-done((bf16[240,768]{1,0:T(8,128)(2,1)S(1)}, bf16[240,768]{1,0:T(8,128)(2,1)}, u32[]{:S(2)}, u32[]{:S(2)}) %collective-permute-start.39) | collective-permute-done | bytes 368672 | tf_op jit(solution)/shard_map/ppermute | solution.py:1253
  200.6 2.7 %last_feed.1 = (f32[96,1536]{1,0:T(8,128)}, f32[96,1536]{1,0:T(8,128)}, f32[96,384]{1,0:T(8,128)}, f32[16,768]{1,0:T(8,128)S(1)}, f32[1,1536]{1,0:T(1,128)S(1)}) custom-call(s32[29]{0:T(128)S(1)} %concatenate.13.place, bf16[240,768]{1,0:T(8,128)(2,1)S(1)} %join.1.own, bf16[240,768]{1,0:T(8,128)(2,1)} %collective-permute-done.39.far), custom_call_target="tpu_custom_call" | custom-call | flops 1 | bytes 1 | tf_op jit(solution)/shard_map/last_feed/pallas_call | solution.py:396
  204.7 5.2 %settle.3 = f32[1024,768]{1,0:T(8,128)} custom-call(s32[29]{0:T(128)S(1)} %concatenate.13.place, bf16[1024,768]{1,0:T(8,128)(2,1)S(1)} %bitcast.55, bf16[1024,768]{1,0:T(8,128)(2,1)S(1)} %bitcast.58, bf16[512,768]{1,0:T(8,128)(2,1)} %add_convert_fusion.mine, bf16[512,768]{1,0:T(8,128)(2,1)} %collective-permute-done.34.theirs), custom_call_target="tpu_custom_call" | custom-call | flops 1 | bytes 1 | tf_op jit(solution)/shard_map/settle/pallas_call | solution.py:396
  210.0 1.6 collective-permute-start.38
  212.1 3.8 %collective-permute-done.38.far = bf16[112,640]{1,0:T(8,128)(2,1)S(1)} collective-permute-done((bf16[112,640]{1,0:T(8,128)(2,1)S(1)}, bf16[112,640]{1,0:T(8,128)(2,1)S(1)}, u32[]{:S(2)}, u32[]{:S(2)}) %collective-permute-start.38) | collective-permute-done | bytes 143392 | tf_op jit(solution)/shard_map/ppermute | solution.py:1253
  215.9 1.4 last_attend.1
  (163 shorter events, 20.0 us)
Async XLA Ops:
  0.7 25.5 %copy-start.35 = (bf16[192]{0:T(256)(128)(2,1)S(1)}, bf16[192]{0:T(256)(128)(2,1)}, u32[]{:S(2)}) copy-start(bf16[192]{0:T(256)(128)(2,1)} %param.25) | copy-start | bytes 1156
  0.7 25.6 %copy-start.6 = (bf16[96,1536]{1,0:T(8,128)(2,1)S(1)}, bf16[96,1536]{1,0:T(8,128)(2,1)}, u32[]{:S(2)}) copy-start(bf16[96,1536]{1,0:T(8,128)(2,1)} %wide.1) | copy-start | bytes 884740
  0.8 25.6 %copy-start.7 = (bf16[1536,96]{0,1:T(8,128)(2,1)S(1)}, bf16[1536,96]{0,1:T(8,128)(2,1)}, u32[]{:S(2)}) copy-start(bf16[1536,96]{0,1:T(8,128)(2,1)} %param.26) | copy-start | bytes 884740
  0.8 25.6 %copy-start.20 = (bf16[96]{0:T(256)(128)(2,1)S(1)}, bf16[96]{0:T(256)(128)(2,1)}, u32[]{:S(2)}) copy-start(bf16[96]{0:T(256)(128)(2,1)} %param.30) | copy-start | bytes 580
  0.8 25.6 %copy-start.21 = (bf16[96]{0:T(256)(128)(2,1)S(1)}, bf16[96]{0:T(256)(128)(2,1)}, u32[]{:S(2)}) copy-start(bf16[96]{0:T(256)(128)(2,1)} %param.31) | copy-start | bytes 580
  0.8 26.2 %copy-start.1 = (bf16[1,1024,768]{2,1,0:T(8,128)(2,1)S(1)}, bf16[1,1024,768]{2,1,0:T(8,128)(2,1)}, u32[]{:S(2)}) copy-start(bf16[1,1024,768]{2,1,0:T(8,128)(2,1)} %param.19) | copy-start | bytes 4718596
  3.1 22.9 %collective-permute-start = (bf16[512,768]{1,0:T(8,128)(2,1)}, bf16[512,768]{1,0:T(8,128)(2,1)}, u32[]{:S(2)}, u32[]{:S(2)}) collective-permute-start(bf16[512,768]{1,0:T(8,128)(2,1)} %dynamic-slice_bitcast_fusion.1), channel_id=1, source_target_pairs={{0,2},{2,0},{1,3},{3,1},{4,6},{6,4},{5,7},{7,5},{8,10},{10,8},{9,1... | collective-permute-start | bytes 2359304 | tf_op jit(solution)/shard_map/ppermute | solution.py:1253
  7.0 5.9 %collective-permute-start.1 = (bf16[112,768]{1,0:T(8,128)(2,1)S(1)}, bf16[112,768]{1,0:T(8,128)(2,1)S(1)}, u32[]{:S(2)}, u32[]{:S(2)}) collective-permute-start(bf16[112,768]{1,0:T(8,128)(2,1)S(1)} %pack_attend.1.refs_0_), channel_id=1, source_target_pairs={{0,8},{8,16},{16,24},{24,28},{28,20},{20,12},{12,4},{4,0},{1,9},{9... | collective-permute-start | bytes 516104 | tf_op jit(solution)/shard_map/ppermute | solution.py:1277
  8.6 5.8 %collective-permute-start.4 = (bf16[112,768]{1,0:T(8,128)(2,1)S(1)}, bf16[112,768]{1,0:T(8,128)(2,1)S(1)}, u32[]{:S(2)}, u32[]{:S(2)}) collective-permute-start(bf16[112,768]{1,0:T(8,128)(2,1)S(1)} %pack_attend.1.refs_0_), channel_id=1, source_target_pairs={{8,0},{16,8},{24,16},{28,24},{20,28},{12,20},{4,12},{0,4},{9,1},{1... | collective-permute-start | bytes 516104 | tf_op jit(solution)/shard_map/ppermute | solution.py:1277
  12.8 5.4 %collective-permute-start.2 = (bf16[112,768]{1,0:T(8,128)(2,1)S(1)}, bf16[112,768]{1,0:T(8,128)(2,1)S(1)}, u32[]{:S(2)}, u32[]{:S(2)}) collective-permute-start(bf16[112,768]{1,0:T(8,128)(2,1)S(1)} %collective-permute-done.1.refs_1_), channel_id=1, source_target_pairs={{0,8},{8,16},{16,24},{24,28},{28,20},{20,12},{12,4},{4,0},{1,9},{9... | collective-permute-start | bytes 516104 | tf_op jit(solution)/shard_map/ppermute | solution.py:1277
  14.4 5.4 %collective-permute-start.5 = (bf16[112,768]{1,0:T(8,128)(2,1)S(1)}, bf16[112,768]{1,0:T(8,128)(2,1)S(1)}, u32[]{:S(2)}, u32[]{:S(2)}) collective-permute-start(bf16[112,768]{1,0:T(8,128)(2,1)S(1)} %collective-permute-done.4.refs_2_), channel_id=1, source_target_pairs={{8,0},{16,8},{24,16},{28,24},{20,28},{12,20},{4,12},{0,4},{9,1},{1... | collective-permute-start | bytes 516104 | tf_op jit(solution)/shard_map/ppermute | solution.py:1277
  18.2 5.5 %collective-permute-start.3 = (bf16[112,768]{1,0:T(8,128)(2,1)S(1)}, bf16[112,768]{1,0:T(8,128)(2,1)}, u32[]{:S(2)}, u32[]{:S(2)}) collective-permute-start(bf16[112,768]{1,0:T(8,128)(2,1)S(1)} %collective-permute-done.2.refs_3_), channel_id=1, source_target_pairs={{0,8},{8,16},{16,24},{24,28},{28,20},{20,12},{12,4},{4,0},{1,9},{9... | collective-permute-start | bytes 516104 | tf_op jit(solution)/shard_map/ppermute | solution.py:1277
  19.8 5.4 %collective-permute-start.6 = (bf16[112,768]{1,0:T(8,128)(2,1)S(1)}, bf16[112,768]{1,0:T(8,128)(2,1)S(1)}, u32[]{:S(2)}, u32[]{:S(2)}) collective-permute-start(bf16[112,768]{1,0:T(8,128)(2,1)S(1)} %collective-permute-done.5.refs_4_), channel_id=1, source_target_pairs={{8,0},{16,8},{24,16},{28,24},{20,28},{12,20},{4,12},{0,4},{9,1},{1... | collective-permute-start | bytes 516104 | tf_op jit(solution)/shard_map/ppermute | solution.py:1277
  25.9 6.2 %collective-permute-start.7 = (bf16[512,768]{1,0:T(8,128)(2,1)}, bf16[512,768]{1,0:T(8,128)(2,1)}, u32[]{:S(2)}, u32[]{:S(2)}) collective-permute-start(bf16[512,768]{1,0:T(8,128)(2,1)} %collective-permute-done), channel_id=1, source_target_pairs={{0,1},{1,0},{2,3},{3,2},{4,5},{5,4},{6,7},{7,6},{8,9},{9,8},{10,11... | collective-permute-start | bytes 2359304 | tf_op jit(solution)/shard_map/ppermute | solution.py:1253
  28.0 10.3 %collective-permute-start.8 = (bf16[208,768]{1,0:T(8,128)(2,1)S(1)}, bf16[208,768]{1,0:T(8,128)(2,1)S(1)}, u32[]{:S(2)}, u32[]{:S(2)}) collective-permute-start(bf16[208,768]{1,0:T(8,128)(2,1)S(1)} %pack_feed.1.refs_0_), channel_id=1, source_target_pairs={{0,8},{8,16},{16,24},{24,28},{28,20},{20,12},{12,4},{4,0},{1,9},{9... | collective-permute-start | bytes 958472 | tf_op jit(solution)/shard_map/ppermute | solution.py:1277
  29.5 9.7 %collective-permute-start.9 = (bf16[208,768]{1,0:T(8,128)(2,1)S(1)}, bf16[208,768]{1,0:T(8,128)(2,1)S(1)}, u32[]{:S(2)}, u32[]{:S(2)}) collective-permute-start(bf16[208,768]{1,0:T(8,128)(2,1)S(1)} %pack_feed.1.refs_0_), channel_id=1, source_target_pairs={{8,0},{16,8},{24,16},{28,24},{20,28},{12,20},{4,12},{0,4},{9,1},{1... | collective-permute-start | bytes 958472 | tf_op jit(solution)/shard_map/ppermute | solution.py:1277
  30.0 11.8 %collective-permute-start.10 = (bf16[112,768]{1,0:T(8,128)(2,1)}, bf16[112,768]{1,0:T(8,128)(2,1)S(1)}, u32[]{:S(2)}, u32[]{:S(2)}) collective-permute-start(bf16[112,768]{1,0:T(8,128)(2,1)} %collective-permute-done.3.refs_5_), channel_id=1, source_target_pairs={{0,8},{8,16},{16,24},{24,28},{28,20},{20,12},{12,4},{4,0},{1,9},{9... | collective-permute-start | bytes 516104 | tf_op jit(solution)/shard_map/ppermute | solution.py:1277
  31.6 19.4 %collective-permute-start.11 = (bf16[512,768]{1,0:T(8,128)(2,1)}, bf16[512,768]{1,0:T(8,128)(2,1)}, u32[]{:S(2)}, u32[]{:S(2)}) collective-permute-start(bf16[512,768]{1,0:T(8,128)(2,1)} %dynamic-slice_bitcast_fusion), channel_id=1, source_target_pairs={{0,2},{2,0},{1,3},{3,1},{4,6},{6,4},{5,7},{7,5},{8,10},{10,8},{9,1... | collective-permute-start | bytes 2359304 | tf_op jit(solution)/shard_map/ppermute | solution.py:1253
  39.2 11.8 %collective-permute-start.12 = (bf16[208,768]{1,0:T(8,128)(2,1)S(1)}, bf16[208,768]{1,0:T(8,128)(2,1)S(1)}, u32[]{:S(2)}, u32[]{:S(2)}) collective-permute-start(bf16[208,768]{1,0:T(8,128)(2,1)S(1)} %collective-permute-done.8.refs_1_), channel_id=1, source_target_pairs={{0,8},{8,16},{16,24},{24,28},{28,20},{20,12},{12,4},{4,0},{1,9},{9... | collective-permute-start | bytes 958472 | tf_op jit(solution)/shard_map/ppermute | solution.py:1277
  40.8 10.2 %collective-permute-start.13 = (bf16[208,768]{1,0:T(8,128)(2,1)S(1)}, bf16[208,768]{1,0:T(8,128)(2,1)S(1)}, u32[]{:S(2)}, u32[]{:S(2)}) collective-permute-start(bf16[208,768]{1,0:T(8,128)(2,1)S(1)} %collective-permute-done.9.refs_2_), channel_id=1, source_target_pairs={{8,0},{16,8},{24,16},{28,24},{20,28},{12,20},{4,12},{0,4},{9,1},{1... | collective-permute-start | bytes 958472 | tf_op jit(solution)/shard_map/ppermute | solution.py:1277
  51.0 14.4 %collective-permute-start.14 = (bf16[512,768]{1,0:T(8,128)(2,1)}, bf16[512,768]{1,0:T(8,128)(2,1)S(1)}, u32[]{:S(2)}, u32[]{:S(2)}) collective-permute-start(bf16[512,768]{1,0:T(8,128)(2,1)} %collective-permute-done.11), channel_id=1, source_target_pairs={{0,1},{1,0},{2,3},{3,2},{4,5},{5,4},{6,7},{7,6},{8,9},{9,8},{10,11... | collective-permute-start | bytes 2359304 | tf_op jit(solution)/shard_map/ppermute | solution.py:1253
  51.2 14.2 %collective-permute-start.15 = (bf16[208,768]{1,0:T(8,128)(2,1)S(1)}, bf16[208,768]{1,0:T(8,128)(2,1)S(1)}, u32[]{:S(2)}, u32[]{:S(2)}) collective-permute-start(bf16[208,768]{1,0:T(8,128)(2,1)S(1)} %collective-permute-done.12.refs_3_), channel_id=1, source_target_pairs={{0,8},{8,16},{16,24},{24,28},{28,20},{20,12},{12,4},{4,0},{1,9},{9... | collective-permute-start | bytes 958472 | tf_op jit(solution)/shard_map/ppermute | solution.py:1277
  52.8 12.5 %collective-permute-start.16 = (bf16[208,768]{1,0:T(8,128)(2,1)S(1)}, bf16[208,768]{1,0:T(8,128)(2,1)S(1)}, u32[]{:S(2)}, u32[]{:S(2)}) collective-permute-start(bf16[208,768]{1,0:T(8,128)(2,1)S(1)} %collective-permute-done.13.refs_4_), channel_id=1, source_target_pairs={{8,0},{16,8},{24,16},{28,24},{20,28},{12,20},{4,12},{0,4},{9,1},{1... | collective-permute-start | bytes 958472 | tf_op jit(solution)/shard_map/ppermute | solution.py:1277
  65.4 20.2 %collective-permute-start.17 = (bf16[208,768]{1,0:T(8,128)(2,1)S(1)}, bf16[208,768]{1,0:T(8,128)(2,1)S(1)}, u32[]{:S(2)}, u32[]{:S(2)}) collective-permute-start(bf16[208,768]{1,0:T(8,128)(2,1)S(1)} %collective-permute-done.15.refs_5_), channel_id=1, source_target_pairs={{0,8},{8,16},{16,24},{24,28},{28,20},{20,12},{12,4},{4,0},{1,9},{9... | collective-permute-start | bytes 958472 | tf_op jit(solution)/shard_map/ppermute | solution.py:1277
  109.8 2.9 %collective-permute-start.18 = (bf16[512,768]{1,0:T(8,128)(2,1)}, bf16[512,768]{1,0:T(8,128)(2,1)S(1)}, u32[]{:S(2)}, u32[]{:S(2)}) collective-permute-start(bf16[512,768]{1,0:T(8,128)(2,1)} %get-tuple-element.122), channel_id=1, source_target_pairs={{0,1},{1,0},{2,3},{3,2},{4,5},{5,4},{6,7},{7,6},{8,9},{9,8},{10,11... | collective-permute-start | bytes 2359304 | tf_op jit(solution)/shard_map/ppermute | solution.py:1253
  109.9 4.7 %collective-permute-start.19 = (bf16[512,768]{1,0:T(8,128)(2,1)S(1)}, bf16[512,768]{1,0:T(8,128)(2,1)S(1)}, u32[]{:S(2)}, u32[]{:S(2)}) collective-permute-start(bf16[512,768]{1,0:T(8,128)(2,1)S(1)} %get-tuple-element.123), channel_id=1, source_target_pairs={{0,1},{1,0},{2,3},{3,2},{4,5},{5,4},{6,7},{7,6},{8,9},{9,8},{10,11... | collective-permute-start | bytes 2359304 | tf_op jit(solution)/shard_map/ppermute | solution.py:1253
  110.4 30.7 %collective-permute-start.20 = (bf16[4,128,768]{2,1,0:T(8,128)(2,1)}, bf16[4,128,768]{2,1,0:T(8,128)(2,1)S(1)}, u32[]{:S(2)}, u32[]{:S(2)}) collective-permute-start(bf16[4,128,768]{2,1,0:T(8,128)(2,1)} %get-tuple-element.127), channel_id=1, source_target_pairs={{0,4},{4,0},{8,12},{12,8},{16,20},{20,16},{24,28},{28,24},{1,5},{5... | collective-permute-start | bytes 2359304 | tf_op jit(solution)/shard_map/ppermute | solution.py:1300
  114.0 27.1 %collective-permute-start.24 = (bf16[512,768]{1,0:T(8,128)(2,1)S(1)}, bf16[512,768]{1,0:T(8,128)(2,1)S(1)}, u32[]{:S(2)}, u32[]{:S(2)}) collective-permute-start(bf16[512,768]{1,0:T(8,128)(2,1)S(1)} %add_convert_fusion.3), channel_id=1, source_target_pairs={{0,2},{2,0},{1,3},{3,1},{4,6},{6,4},{5,7},{7,5},{8,10},{10,8},{9,1... | collective-permute-start | bytes 2359304 | tf_op jit(solution)/shard_map/ppermute | solution.py:1253
  114.6 23.4 %collective-permute-start.21 = (bf16[2,112,768]{2,1,0:T(8,128)(2,1)S(1)}, bf16[2,112,768]{2,1,0:T(8,128)(2,1)S(1)}, u32[]{:S(2)}, u32[]{:S(2)}) collective-permute-start(bf16[2,112,768]{2,1,0:T(8,128)(2,1)S(1)} %get-tuple-element.128), channel_id=1, source_target_pairs={{0,8},{4,12},{8,16},{12,20},{16,24},{20,28},{24,0},{28,4},{1,9},{5... | collective-permute-start | bytes 1032200 | tf_op jit(solution)/shard_map/ppermute | solution.py:1288
  114.6 26.5 %collective-permute-start.22 = (bf16[2,112,768]{2,1,0:T(8,128)(2,1)S(1)}, bf16[2,112,768]{2,1,0:T(8,128)(2,1)S(1)}, u32[]{:S(2)}, u32[]{:S(2)}) collective-permute-start(bf16[2,112,768]{2,1,0:T(8,128)(2,1)S(1)} %get-tuple-element.129), channel_id=1, source_target_pairs={{0,16},{4,20},{8,24},{12,28},{16,0},{20,4},{24,8},{28,12},{1,17},{... | collective-permute-start | bytes 1032200 | tf_op jit(solution)/shard_map/ppermute | solution.py:1288
  114.6 26.5 %collective-permute-start.23 = (bf16[2,112,768]{2,1,0:T(8,128)(2,1)S(1)}, bf16[2,112,768]{2,1,0:T(8,128)(2,1)S(1)}, u32[]{:S(2)}, u32[]{:S(2)}) collective-permute-start(bf16[2,112,768]{2,1,0:T(8,128)(2,1)S(1)} %get-tuple-element.130), channel_id=1, source_target_pairs={{0,24},{4,28},{8,0},{12,4},{16,8},{20,12},{24,16},{28,20},{1,25},{... | collective-permute-start | bytes 1032200 | tf_op jit(solution)/shard_map/ppermute | solution.py:1288
  143.0 24.5 %collective-permute-start.25 = (bf16[128,768]{1,0:T(8,128)(2,1)S(1)}, bf16[128,768]{1,0:T(8,128)(2,1)S(1)}, u32[]{:S(2)}, u32[]{:S(2)}) collective-permute-start(bf16[128,768]{1,0:T(8,128)(2,1)S(1)} %get-tuple-element.139), channel_id=1, source_target_pairs={{0,8},{4,12},{8,16},{12,20},{16,24},{20,28},{24,0},{28,4},{1,9},{5... | collective-permute-start | bytes 589832 | tf_op jit(solution)/shard_map/ppermute | solution.py:1288
  152.8 14.7 %collective-permute-start.26 = (bf16[128,768]{1,0:T(8,128)(2,1)S(1)}, bf16[128,768]{1,0:T(8,128)(2,1)S(1)}, u32[]{:S(2)}, u32[]{:S(2)}) collective-permute-start(bf16[128,768]{1,0:T(8,128)(2,1)S(1)} %get-tuple-element.140), channel_id=1, source_target_pairs={{0,16},{4,20},{8,24},{12,28},{16,0},{20,4},{24,8},{28,12},{1,17},{... | collective-permute-start | bytes 589832 | tf_op jit(solution)/shard_map/ppermute | solution.py:1288
  152.8 14.7 %collective-permute-start.27 = (bf16[128,768]{1,0:T(8,128)(2,1)S(1)}, bf16[128,768]{1,0:T(8,128)(2,1)S(1)}, u32[]{:S(2)}, u32[]{:S(2)}) collective-permute-start(bf16[128,768]{1,0:T(8,128)(2,1)S(1)} %get-tuple-element.141), channel_id=1, source_target_pairs={{0,24},{4,28},{8,0},{12,4},{16,8},{20,12},{24,16},{28,20},{1,25},{... | collective-permute-start | bytes 589832 | tf_op jit(solution)/shard_map/ppermute | solution.py:1288
  155.2 12.3 %collective-permute-start.28 = (bf16[112,768]{1,0:T(8,128)(2,1)S(1)}, bf16[112,768]{1,0:T(8,128)(2,1)S(1)}, u32[]{:S(2)}, u32[]{:S(2)}) collective-permute-start(bf16[112,768]{1,0:T(8,128)(2,1)S(1)} %get-tuple-element.143), channel_id=1, source_target_pairs={{0,4},{4,0},{8,12},{12,8},{16,20},{20,16},{24,28},{28,24},{1,5},{5... | collective-permute-start | bytes 516104 | tf_op jit(solution)/shard_map/ppermute | solution.py:1300
  167.5 2.4 %collective-permute-start.29 = (bf16[512,768]{1,0:T(8,128)(2,1)S(1)}, bf16[512,768]{1,0:T(8,128)(2,1)S(1)}, u32[]{:S(2)}, u32[]{:S(2)}) collective-permute-start(bf16[512,768]{1,0:T(8,128)(2,1)S(1)} %get-tuple-element.153), channel_id=1, source_target_pairs={{0,1},{1,0},{2,3},{3,2},{4,5},{5,4},{6,7},{7,6},{8,9},{9,8},{10,11... | collective-permute-start | bytes 2359304 | tf_op jit(solution)/shard_map/ppermute | solution.py:1253
  170.5 4.5 %collective-permute-start.30 = (bf16[512,768]{1,0:T(8,128)(2,1)S(1)}, bf16[512,768]{1,0:T(8,128)(2,1)S(1)}, u32[]{:S(2)}, u32[]{:S(2)}) collective-permute-start(bf16[512,768]{1,0:T(8,128)(2,1)S(1)} %add_convert_fusion.1.mine), channel_id=1, source_target_pairs={{0,1},{1,0},{2,3},{3,2},{4,5},{5,4},{6,7},{7,6},{8,9},{9,8},{10,11... | collective-permute-start | bytes 2359304 | tf_op jit(solution)/shard_map/ppermute | solution.py:1253
  170.7 19.8 %collective-permute-start.32 = (bf16[512,768]{1,0:T(8,128)(2,1)S(1)}, bf16[512,768]{1,0:T(8,128)(2,1)S(1)}, u32[]{:S(2)}, u32[]{:S(2)}) collective-permute-start(bf16[512,768]{1,0:T(8,128)(2,1)S(1)} %add_convert_fusion.2), channel_id=1, source_target_pairs={{0,2},{2,0},{1,3},{3,1},{4,6},{6,4},{5,7},{7,5},{8,10},{10,8},{9,1... | collective-permute-start | bytes 2359304 | tf_op jit(solution)/shard_map/ppermute | solution.py:1253
  172.2 19.8 %collective-permute-start.31 = (bf16[512,768]{1,0:T(8,128)(2,1)S(1)}, bf16[512,768]{1,0:T(8,128)(2,1)S(1)}, u32[]{:S(2)}, u32[]{:S(2)}) collective-permute-start(bf16[512,768]{1,0:T(8,128)(2,1)S(1)} %get-tuple-element.157), channel_id=1, source_target_pairs={{0,1},{1,0},{2,3},{3,2},{4,5},{5,4},{6,7},{7,6},{8,9},{9,8},{10,11... | collective-permute-start | bytes 2359304 | tf_op jit(solution)/shard_map/ppermute | solution.py:1253
  172.3 15.6 %collective-permute-start.33 = (bf16[4,112,640]{2,1,0:T(8,128)(2,1)S(1)}, bf16[4,112,640]{2,1,0:T(8,128)(2,1)S(1)}, u32[]{:S(2)}, u32[]{:S(2)}) collective-permute-start(bf16[4,112,640]{2,1,0:T(8,128)(2,1)S(1)} %get-tuple-element.159), channel_id=1, source_target_pairs={{0,4},{4,0},{8,12},{12,8},{16,20},{20,16},{24,28},{28,24},{1,5},{5... | collective-permute-start | bytes 1720328 | tf_op jit(solution)/shard_map/ppermute | solution.py:1300
  190.5 10.2 %collective-permute-start.39 = (bf16[240,768]{1,0:T(8,128)(2,1)S(1)}, bf16[240,768]{1,0:T(8,128)(2,1)}, u32[]{:S(2)}, u32[]{:S(2)}) collective-permute-start(bf16[240,768]{1,0:T(8,128)(2,1)S(1)} %join.1.own), channel_id=1, source_target_pairs={{0,2},{2,0},{1,3},{3,1},{4,6},{6,4},{5,7},{7,5},{8,10},{10,8},{9,1... | collective-permute-start | bytes 1105928 | tf_op jit(solution)/shard_map/ppermute | solution.py:1253
  193.3 11.4 %collective-permute-start.34 = (bf16[512,768]{1,0:T(8,128)(2,1)}, bf16[512,768]{1,0:T(8,128)(2,1)}, u32[]{:S(2)}, u32[]{:S(2)}) collective-permute-start(bf16[512,768]{1,0:T(8,128)(2,1)} %add_convert_fusion.mine), channel_id=1, source_target_pairs={{0,1},{1,0},{2,3},{3,2},{4,5},{5,4},{6,7},{7,6},{8,9},{9,8},{10,11... | collective-permute-start | bytes 2359304 | tf_op jit(solution)/shard_map/ppermute | solution.py:1253
  193.3 16.6 %collective-permute-start.35 = (bf16[112,640]{1,0:T(8,128)(2,1)}, bf16[112,640]{1,0:T(8,128)(2,1)S(1)}, u32[]{:S(2)}, u32[]{:S(2)}) collective-permute-start(bf16[112,640]{1,0:T(8,128)(2,1)} %copy-done.28), channel_id=1, source_target_pairs={{0,8},{4,12},{8,16},{12,20},{16,24},{20,28},{24,0},{28,4},{1,9},{5... | collective-permute-start | bytes 430088 | tf_op jit(solution)/shard_map/ppermute | solution.py:1288
  195.0 14.8 %collective-permute-start.36 = (bf16[112,640]{1,0:T(8,128)(2,1)}, bf16[112,640]{1,0:T(8,128)(2,1)S(1)}, u32[]{:S(2)}, u32[]{:S(2)}) collective-permute-start(bf16[112,640]{1,0:T(8,128)(2,1)} %copy-done.27), channel_id=1, source_target_pairs={{0,16},{4,20},{8,24},{12,28},{16,0},{20,4},{24,8},{28,12},{1,17},{... | collective-permute-start | bytes 430088 | tf_op jit(solution)/shard_map/ppermute | solution.py:1288
  198.4 11.4 %collective-permute-start.37 = (bf16[112,640]{1,0:T(8,128)(2,1)}, bf16[112,640]{1,0:T(8,128)(2,1)S(1)}, u32[]{:S(2)}, u32[]{:S(2)}) collective-permute-start(bf16[112,640]{1,0:T(8,128)(2,1)} %copy-done.26), channel_id=1, source_target_pairs={{0,24},{4,28},{8,0},{12,4},{16,8},{20,12},{24,16},{28,20},{1,25},{... | collective-permute-start | bytes 430088 | tf_op jit(solution)/shard_map/ppermute | solution.py:1288
  203.5 1.2 collective-permute-start.40
  210.0 5.9 %collective-permute-start.38 = (bf16[112,640]{1,0:T(8,128)(2,1)S(1)}, bf16[112,640]{1,0:T(8,128)(2,1)S(1)}, u32[]{:S(2)}, u32[]{:S(2)}) collective-permute-start(bf16[112,640]{1,0:T(8,128)(2,1)S(1)} %add_convert_fusion.4.own), channel_id=1, source_target_pairs={{0,2},{2,0},{1,3},{3,1},{4,6},{6,4},{5,7},{7,5},{8,10},{10,8},{9,1... | collective-permute-start | bytes 430088 | tf_op jit(solution)/shard_map/ppermute | solution.py:1253
  217.4 1.1 collective-permute-start.41
  (30 other events, 202.6 us)

commit v5 on v4

--- a/solution.py
+++ b/solution.py
@@ -1451,12 +1451,15 @@
     e_far = after(e_far, attend_cross[0])
     mine = add(near_own, e_got_own, e_far)
     feed_far = swap(after(feed_sum, e_far), "context")
-    tokens_gradient = settle(place, True, own_x, own_g, mine, swap(mine, "tensor"))
-    attend_along = after(attend_along, tokens_gradient)
+    theirs = swap(mine, "tensor")
+    wide_slope, narrow_slope, outgoing_slope, feed_sums, unit_slope = last_feed(place, feed_sum, feed_far, inner)
+    attend_along, theirs = after((attend_along, theirs), wide_slope)
     attend_sum = add_along(attend_cross[0], attend_along)
     attend_far = swap(attend_sum, "context")
-
-    wide_slope, narrow_slope, outgoing_slope, feed_sums, unit_slope = last_feed(place, feed_sum, feed_far, inner)
+    theirs = after(theirs, attend_sum)
+    tokens_gradient = settle(place, True, own_x, own_g, mine, theirs)
+    attend_far = after(attend_far, tokens_gradient)
+
     projection_slope, attend_sums, bias_slope = last_attend(place, attend_sum, attend_far, inner)
 
     def across(rows):

time: 221 us -> 216 us (0.977); the launches traced: 220 us -> 217 us
  Pallas kernels: 97.6 us -> 117 us
  starting transfers between devices: 56.7 us -> 40.2 us
  waiting for transfers between devices: 44.8 us -> 39.2 us
    pallas_call x15, Pallas kernels: 97.6 us -> 117 us  [call(): pl.pallas_call(kernel, grid_spec=pltpu.PrefetchScalarGridSpec(num_scalar_...]
    ppermute x14, starting transfers between devices: 23.8 us -> 14.1 us  [step(): lax.ppermute(end, 'fsdp', way)]
    ppermute x9, starting transfers between devices: 21.3 us -> 13.9 us  [send_along(): got.append(lax.ppermute(piece, 'fsdp', pairs))]
    ppermute x16, waiting for transfers between devices: 14.1 us -> 8.15 us  [swap(): return lax.ppermute(value, axis, PAIR)]
  transfers between devices with their start and end apart: 42 -> 42, of which waited for: 17 -> 17; matrix products, arithmetic and copies ran while one was open for 5% -> 5% of each run, Pallas kernels for 32% -> 42%
where the time goes in v5:
time: 216 us; the launch traced here: 217 us
  Pallas kernels  117 us (54%)
  starting transfers between devices  40.2 us (19%)
  waiting for transfers between devices  39.2 us (18%)
  other arithmetic  10.2 us (5%)
  local copies, waits for them, and re-layouts  9.3 us (4%)
    pallas_call x15, Pallas kernels, call(): pl.pallas_call(kernel, grid_spec=pltpu.PrefetchScalarGridSpec(num_scalar_...  117 us
    ppermute x14, waiting for transfers between devices, step(): lax.ppermute(end, 'fsdp', way)  16.8 us
    ppermute x14, starting transfers between devices, step(): lax.ppermute(end, 'fsdp', way)  14.1 us
    ppermute x9, starting transfers between devices, send_along(): got.append(lax.ppermute(piece, 'fsdp', pairs))  13.9 us
    ppermute x3, waiting for transfers between devices, swap_x(): return lax.ppermute(value, 'fsdp', [(i, i ^ 1) for i in range(8)])  10.9 us
    ppermute x16, starting transfers between devices, swap(): return lax.ppermute(value, axis, PAIR)  8.56 us
    ppermute x16, waiting for transfers between devices, swap(): return lax.ppermute(value, axis, PAIR)  8.15 us
  transfers between devices with their start and end apart: 42, of which 17 were waited for; matrix products, arithmetic and copies ran while one was open for 5% of the time, Pallas kernels for 42%

profile of v5, /device:TPU:0, one launch (start us, length us, event | category | flops | bytes accessed | tf_op | source)
XLA Modules:
  0.0 217.4 jit_solution(3307102072537766660)
XLA Ops:
  0.8 2.3 %dynamic-slice_bitcast_fusion.1 = bf16[512,768]{1,0:T(8,128)(2,1)} fusion(bf16[1,1024,768]{2,1,0:T(8,128)(2,1)} %param.17, s32[]{:T(128)S(6)} %select_n.179), kind=kLoop, calls=%fused_computation.7 | loop fusion | bytes 1572868 | tf_op jit(solution)/shard_map/dynamic_slice | solution.py:1322
  3.1 3.0 %collective-permute-start = (bf16[512,768]{1,0:T(8,128)(2,1)}, bf16[512,768]{1,0:T(8,128)(2,1)}, u32[]{:S(2)}, u32[]{:S(2)}) collective-permute-start(bf16[512,768]{1,0:T(8,128)(2,1)} %dynamic-slice_bitcast_fusion.1), channel_id=1, source_target_pairs={{0,2},{2,0},{1,3},{3,1},{4,6},{6,4},{5,7},{7,5},{8,10},{10,8},{9,1... | collective-permute-start | bytes 2359304 | tf_op jit(solution)/shard_map/ppermute | solution.py:1253
  7.0 1.6 collective-permute-start.1
  9.0 3.8 %collective-permute-done.1.refs_1_ = bf16[112,768]{1,0:T(8,128)(2,1)S(1)} collective-permute-done((bf16[112,768]{1,0:T(8,128)(2,1)S(1)}, bf16[112,768]{1,0:T(8,128)(2,1)S(1)}, u32[]{:S(2)}, u32[]{:S(2)}) %collective-permute-start.1) | collective-permute-done | bytes 172064 | tf_op jit(solution)/shard_map/ppermute | solution.py:1277
  12.8 1.6 collective-permute-start.2
  14.9 3.4 %collective-permute-done.2.refs_3_ = bf16[112,768]{1,0:T(8,128)(2,1)S(1)} collective-permute-done((bf16[112,768]{1,0:T(8,128)(2,1)S(1)}, bf16[112,768]{1,0:T(8,128)(2,1)S(1)}, u32[]{:S(2)}, u32[]{:S(2)}) %collective-permute-start.2) | collective-permute-done | bytes 172064 | tf_op jit(solution)/shard_map/ppermute | solution.py:1277
  18.2 1.6 collective-permute-start.3
  20.4 3.4 %collective-permute-done.3.refs_5_ = bf16[112,768]{1,0:T(8,128)(2,1)} collective-permute-done((bf16[112,768]{1,0:T(8,128)(2,1)S(1)}, bf16[112,768]{1,0:T(8,128)(2,1)}, u32[]{:S(2)}, u32[]{:S(2)}) %collective-permute-start.3) | collective-permute-done | bytes 172064 | tf_op jit(solution)/shard_map/ppermute | solution.py:1277
  23.8 1.5 collective-permute-done.6.refs_6_
  27.0 0.9 dynamic-slice_bitcast_fusion
  28.0 1.6 collective-permute-start.8
  30.0 1.6 collective-permute-start.10
  32.1 1.5 broadcast_select_fusion.3
  33.6 1.2 pad_maximum_fusion.peer_x
  34.9 3.4 %collective-permute-done.8.refs_1_ = bf16[208,768]{1,0:T(8,128)(2,1)S(1)} collective-permute-done((bf16[208,768]{1,0:T(8,128)(2,1)S(1)}, bf16[208,768]{1,0:T(8,128)(2,1)S(1)}, u32[]{:S(2)}, u32[]{:S(2)}) %collective-permute-start.8) | collective-permute-done | bytes 319520 | tf_op jit(solution)/shard_map/ppermute | solution.py:1277
  38.3 0.9 collective-permute-done.9.refs_2_
  39.2 1.6 collective-permute-start.12
  41.8 7.8 %prepare.1 = (bf16[2048,192]{1,0:T(8,128)(2,1)S(1)}, bf16[2048,192]{1,0:T(8,128)(2,1)S(1)}, bf16[2048,192]{1,0:T(8,128)(2,1)S(1)}, bf16[768,768]{1,0:T(8,128)(2,1)S(1)}, f32[16,768]{1,0:T(8,128)S(1)}) custom-call(s32[29]{0:T(128)S(1)} %concatenate.13.place, bf16[1024,768]{1,0:T(8,128)(2,1)} %bitcast.51, bf16[1024,768]{1,0:T(8,128)(2,1)} %pad_maximum_fusion.peer_x, ...), custom_call_target="tpu_custom_call" | custom-call | flops 1 | bytes 1 | tf_op jit(solution)/shard_map/prepare/pallas_call | solution.py:396
  49.7 1.3 collective-permute-done.11
  51.2 1.6 collective-permute-start.15
  53.3 20.2 %forward.1 = (bf16[2048,192]{1,0:T(8,128)(2,1)S(1)}, f32[8,1,768]{2,1,0:T(1,128)S(1)}, f32[192,2048]{1,0:T(8,128)S(1)}) custom-call(s32[32]{0:T(128)S(1)} %pad_add_fusion.first, bf16[2048,192]{1,0:T(8,128)(2,1)S(1)} %get-tuple-element.110.q_ref, bf16[2048,192]{1,0:T(8,128)(2,1)S(1)} %get-tuple-element.111.k_ref, ...), custom_call_target="tpu_custom_call" | custom-call | flops 1 | bytes 1 | tf_op jit(solution)/shard_map/forward/pallas_call | solution.py:396
  73.7 1.2 broadcast_select_fusion.1
  75.0 1.2 pad_maximum_fusion.1.peer_g
  76.2 6.6 %mix.1 = (bf16[2048,192]{1,0:T(8,128)(2,1)S(1)}, bf16[1024,768]{1,0:T(8,128)(2,1)S(1)}, bf16[1024,768]{1,0:T(8,128)(2,1)}, bf16[8,32,768]{2,1,0:T(8,128)(2,1)S(1)}) custom-call(s32[29]{0:T(128)S(1)} %concatenate.13.place, bf16[1024,768]{1,0:T(8,128)(2,1)} %bitcast.56, bf16[1024,768]{1,0:T(8,128)(2,1)} %pad_maximum_fusion.1.peer_g, ...), custom_call_target="tpu_custom_call" | custom-call | flops 1 | bytes 1 | tf_op jit(solution)/shard_map/mix/pallas_call | solution.py:396
  82.8 1.2 copy-done.3
  84.0 24.2 %feed.1 = (bf16[512,768]{1,0:T(8,128)(2,1)S(1)}, bf16[512,768]{1,0:T(8,128)(2,1)S(1)}, bf16[512,768]{1,0:T(8,128)(2,1)}, bf16[512,768]{1,0:T(8,128)(2,1)}, bf16[...) custom-call(s32[29]{0:T(128)S(1)} %concatenate.13.place, ...), custom_call_target="tpu_custom_call" | custom-call | flops 1 | bytes 1 | tf_op jit(solution)/shard_map/feed/pallas_call | solution.py:396
  108.8 2.0 collective-permute-start.20
  111.1 1.3 add_convert_fusion.3
  113.0 3.9 %collective-permute-start.23 = (bf16[2,112,768]{2,1,0:T(8,128)(2,1)S(1)}, bf16[2,112,768]{2,1,0:T(8,128)(2,1)S(1)}, u32[]{:S(2)}, u32[]{:S(2)}) collective-permute-start(bf16[2,112,768]{2,1,0:T(8,128)(2,1)S(1)} %get-tuple-element.133), channel_id=1, source_target_pairs={{0,24},{4,28},{8,0},{12,4},{16,8},{20,12},{24,16},{28,20},{1,25},{... | collective-permute-start | bytes 1032200 | tf_op jit(solution)/shard_map/ppermute | solution.py:1288
  116.9 31.0 %backward.1.slope_ref = bf16[2048,576]{1,0:T(8,128)(2,1)} custom-call(s32[32]{0:T(128)S(1)} %pad_add_fusion.first, bf16[2048,192]{1,0:T(8,128)(2,1)S(1)} %get-tuple-element.110.q_ref, bf16[2048,192]{1,0:T(8,128)(2,1)S(1)} %get-tuple-element.111.k_ref, bf16[2048,192]{1,0:T(8,128)(2,1)S(1)} %get-tuple-element.112.v_ref, ...), custom_call_target="tpu_custom_call" | custom-call | flops 1 | bytes 1 | tf_op jit(solution)/shard_map/backward/pallas_call | solution.py:396
  149.9 3.7 %collective-permute-start.27 = (bf16[128,768]{1,0:T(8,128)(2,1)S(1)}, bf16[128,768]{1,0:T(8,128)(2,1)S(1)}, u32[]{:S(2)}, u32[]{:S(2)}) collective-permute-start(bf16[128,768]{1,0:T(8,128)(2,1)S(1)} %get-tuple-element.144), channel_id=1, source_target_pairs={{0,24},{4,28},{8,0},{12,4},{16,8},{20,12},{24,16},{28,20},{1,25},{... | collective-permute-start | bytes 589832 | tf_op jit(solution)/shard_map/ppermute | solution.py:1288
  153.6 12.2 %finish.1 = (bf16[512,768]{1,0:T(8,128)(2,1)S(1)}, bf16[512,768]{1,0:T(8,128)(2,1)S(1)}, bf16[512,768]{1,0:T(8,128)(2,1)S(1)}, bf16[512,768]{1,0:T(8,128)(2,1)S(...) custom-call(s32[29]{0:T(128)S(1)} %concatenate.13.place, bf16[1024,768]{1,0:T(8,128)(2,1)} %bitcast.53, ...), custom_call_target="tpu_custom_call" | custom-call | flops 1 | bytes 1 | tf_op jit(solution)/shard_map/finish/pallas_call | solution.py:396
  166.3 2.3 %collective-permute-done.29 = bf16[512,768]{1,0:T(8,128)(2,1)S(1)} collective-permute-done((bf16[512,768]{1,0:T(8,128)(2,1)S(1)}, bf16[512,768]{1,0:T(8,128)(2,1)S(1)}, u32[]{:S(2)}, u32[]{:S(2)}) %collective-permute-start.29) | collective-permute-done | bytes 786464 | tf_op jit(solution)/shard_map/ppermute | solution.py:1253
  169.4 1.6 collective-permute-start.32
  171.0 1.7 collective-permute-start.33
  173.4 2.1 settle.2
  175.5 10.8 %collective-permute-done.33.got = bf16[4,112,640]{2,1,0:T(8,128)(2,1)S(1)} collective-permute-done((bf16[4,112,640]{2,1,0:T(8,128)(2,1)S(1)}, bf16[4,112,640]{2,1,0:T(8,128)(2,1)S(1)}, u32[]{:S(2)}, u32[]{:S(2)}) %collective-permute-start.33) | collective-permute-done | bytes 573472 | tf_op jit(solution)/shard_map/ppermute | solution.py:1300
  187.1 2.1 collective-permute-done.32
  189.2 1.5 collective-permute-start.38
  190.8 1.2 add_convert_fusion.mine
  192.0 3.8 %collective-permute-start.34 = (bf16[112,640]{1,0:T(8,128)(2,1)}, bf16[112,640]{1,0:T(8,128)(2,1)S(1)}, u32[]{:S(2)}, u32[]{:S(2)}) collective-permute-start(bf16[112,640]{1,0:T(8,128)(2,1)} %copy-done.27), channel_id=1, source_target_pairs={{0,8},{4,12},{8,16},{12,20},{16,24},{20,28},{24,0},{28,4},{1,9},{5... | collective-permute-start | bytes 430088 | tf_op jit(solution)/shard_map/ppermute | solution.py:1288
  195.8 2.4 %collective-permute-start.36 = (bf16[112,640]{1,0:T(8,128)(2,1)}, bf16[112,640]{1,0:T(8,128)(2,1)S(1)}, u32[]{:S(2)}, u32[]{:S(2)}) collective-permute-start(bf16[112,640]{1,0:T(8,128)(2,1)} %copy-done.25), channel_id=1, source_target_pairs={{0,24},{4,28},{8,0},{12,4},{16,8},{20,12},{24,16},{28,20},{1,25},{... | collective-permute-start | bytes 430088 | tf_op jit(solution)/shard_map/ppermute | solution.py:1288
  198.2 1.2 collective-permute-done.38.far
  199.4 2.7 %last_feed.1 = (f32[96,1536]{1,0:T(8,128)}, f32[96,1536]{1,0:T(8,128)}, f32[96,384]{1,0:T(8,128)}, f32[16,768]{1,0:T(8,128)S(1)}, f32[1,1536]{1,0:T(1,128)S(1)}) custom-call(s32[29]{0:T(128)S(1)} %concatenate.13.place, bf16[240,768]{1,0:T(8,128)(2,1)S(1)} %join.1.own, bf16[240,768]{1,0:T(8,128)(2,1)} %collective-permute-done.38.far), custom_call_target="tpu_custom_call" | custom-call | flops 1 | bytes 1 | tf_op jit(solution)/shard_map/last_feed/pallas_call | solution.py:396
  203.4 3.0 %collective-permute-done.35 = bf16[112,640]{1,0:T(8,128)(2,1)S(1)} collective-permute-done((bf16[112,640]{1,0:T(8,128)(2,1)}, bf16[112,640]{1,0:T(8,128)(2,1)S(1)}, u32[]{:S(2)}, u32[]{:S(2)}) %collective-permute-start.35) | collective-permute-done | bytes 143392 | tf_op jit(solution)/shard_map/ppermute | solution.py:1288
  206.4 1.0 add_convert_fusion.4.own
  208.5 5.1 %settle.3 = f32[1024,768]{1,0:T(8,128)} custom-call(s32[29]{0:T(128)S(1)} %concatenate.13.place, bf16[1024,768]{1,0:T(8,128)(2,1)S(1)} %bitcast.55, bf16[1024,768]{1,0:T(8,128)(2,1)S(1)} %bitcast.58, bf16[512,768]{1,0:T(8,128)(2,1)} %add_convert_fusion.mine, bf16[512,768]{1,0:T(8,128)(2,1)} %collective-permute-done.37.theirs), custom_call_target="tpu_custom_call" | custom-call | flops 1 | bytes 1 | tf_op jit(solution)/shard_map/settle/pallas_call | solution.py:396
  213.7 1.4 last_attend.1
  (161 shorter events, 17.8 us)
Async XLA Ops:
  0.7 25.6 %copy-start.6 = (bf16[96,1536]{1,0:T(8,128)(2,1)S(1)}, bf16[96,1536]{1,0:T(8,128)(2,1)}, u32[]{:S(2)}) copy-start(bf16[96,1536]{1,0:T(8,128)(2,1)} %wide.1) | copy-start | bytes 884740
  0.8 25.6 %copy-start.7 = (bf16[1536,96]{0,1:T(8,128)(2,1)S(1)}, bf16[1536,96]{0,1:T(8,128)(2,1)}, u32[]{:S(2)}) copy-start(bf16[1536,96]{0,1:T(8,128)(2,1)} %param.26) | copy-start | bytes 884740
  0.8 25.6 %copy-start.19 = (bf16[96]{0:T(256)(128)(2,1)S(1)}, bf16[96]{0:T(256)(128)(2,1)}, u32[]{:S(2)}) copy-start(bf16[96]{0:T(256)(128)(2,1)} %param.30) | copy-start | bytes 580
  0.8 25.6 %copy-start.20 = (bf16[96]{0:T(256)(128)(2,1)S(1)}, bf16[96]{0:T(256)(128)(2,1)}, u32[]{:S(2)}) copy-start(bf16[96]{0:T(256)(128)(2,1)} %param.31) | copy-start | bytes 580
  0.8 26.2 %copy-start.1 = (bf16[1,1024,768]{2,1,0:T(8,128)(2,1)S(1)}, bf16[1,1024,768]{2,1,0:T(8,128)(2,1)}, u32[]{:S(2)}) copy-start(bf16[1,1024,768]{2,1,0:T(8,128)(2,1)} %param.19) | copy-start | bytes 4718596
  3.1 22.9 %collective-permute-start = (bf16[512,768]{1,0:T(8,128)(2,1)}, bf16[512,768]{1,0:T(8,128)(2,1)}, u32[]{:S(2)}, u32[]{:S(2)}) collective-permute-start(bf16[512,768]{1,0:T(8,128)(2,1)} %dynamic-slice_bitcast_fusion.1), channel_id=1, source_target_pairs={{0,2},{2,0},{1,3},{3,1},{4,6},{6,4},{5,7},{7,5},{8,10},{10,8},{9,1... | collective-permute-start | bytes 2359304 | tf_op jit(solution)/shard_map/ppermute | solution.py:1253
  7.0 5.9 %collective-permute-start.1 = (bf16[112,768]{1,0:T(8,128)(2,1)S(1)}, bf16[112,768]{1,0:T(8,128)(2,1)S(1)}, u32[]{:S(2)}, u32[]{:S(2)}) collective-permute-start(bf16[112,768]{1,0:T(8,128)(2,1)S(1)} %pack_attend.1.refs_0_), channel_id=1, source_target_pairs={{0,8},{8,16},{16,24},{24,28},{28,20},{20,12},{12,4},{4,0},{1,9},{9... | collective-permute-start | bytes 516104 | tf_op jit(solution)/shard_map/ppermute | solution.py:1277
  8.6 5.8 %collective-permute-start.4 = (bf16[112,768]{1,0:T(8,128)(2,1)S(1)}, bf16[112,768]{1,0:T(8,128)(2,1)S(1)}, u32[]{:S(2)}, u32[]{:S(2)}) collective-permute-start(bf16[112,768]{1,0:T(8,128)(2,1)S(1)} %pack_attend.1.refs_0_), channel_id=1, source_target_pairs={{8,0},{16,8},{24,16},{28,24},{20,28},{12,20},{4,12},{0,4},{9,1},{1... | collective-permute-start | bytes 516104 | tf_op jit(solution)/shard_map/ppermute | solution.py:1277
  12.8 5.4 %collective-permute-start.2 = (bf16[112,768]{1,0:T(8,128)(2,1)S(1)}, bf16[112,768]{1,0:T(8,128)(2,1)S(1)}, u32[]{:S(2)}, u32[]{:S(2)}) collective-permute-start(bf16[112,768]{1,0:T(8,128)(2,1)S(1)} %collective-permute-done.1.refs_1_), channel_id=1, source_target_pairs={{0,8},{8,16},{16,24},{24,28},{28,20},{20,12},{12,4},{4,0},{1,9},{9... | collective-permute-start | bytes 516104 | tf_op jit(solution)/shard_map/ppermute | solution.py:1277
  14.4 5.4 %collective-permute-start.5 = (bf16[112,768]{1,0:T(8,128)(2,1)S(1)}, bf16[112,768]{1,0:T(8,128)(2,1)S(1)}, u32[]{:S(2)}, u32[]{:S(2)}) collective-permute-start(bf16[112,768]{1,0:T(8,128)(2,1)S(1)} %collective-permute-done.4.refs_2_), channel_id=1, source_target_pairs={{8,0},{16,8},{24,16},{28,24},{20,28},{12,20},{4,12},{0,4},{9,1},{1... | collective-permute-start | bytes 516104 | tf_op jit(solution)/shard_map/ppermute | solution.py:1277
  18.2 5.5 %collective-permute-start.3 = (bf16[112,768]{1,0:T(8,128)(2,1)S(1)}, bf16[112,768]{1,0:T(8,128)(2,1)}, u32[]{:S(2)}, u32[]{:S(2)}) collective-permute-start(bf16[112,768]{1,0:T(8,128)(2,1)S(1)} %collective-permute-done.2.refs_3_), channel_id=1, source_target_pairs={{0,8},{8,16},{16,24},{24,28},{28,20},{20,12},{12,4},{4,0},{1,9},{9... | collective-permute-start | bytes 516104 | tf_op jit(solution)/shard_map/ppermute | solution.py:1277
  19.8 5.4 %collective-permute-start.6 = (bf16[112,768]{1,0:T(8,128)(2,1)S(1)}, bf16[112,768]{1,0:T(8,128)(2,1)S(1)}, u32[]{:S(2)}, u32[]{:S(2)}) collective-permute-start(bf16[112,768]{1,0:T(8,128)(2,1)S(1)} %collective-permute-done.5.refs_4_), channel_id=1, source_target_pairs={{8,0},{16,8},{24,16},{28,24},{20,28},{12,20},{4,12},{0,4},{9,1},{1... | collective-permute-start | bytes 516104 | tf_op jit(solution)/shard_map/ppermute | solution.py:1277
  25.9 6.2 %collective-permute-start.7 = (bf16[512,768]{1,0:T(8,128)(2,1)}, bf16[512,768]{1,0:T(8,128)(2,1)}, u32[]{:S(2)}, u32[]{:S(2)}) collective-permute-start(bf16[512,768]{1,0:T(8,128)(2,1)} %collective-permute-done), channel_id=1, source_target_pairs={{0,1},{1,0},{2,3},{3,2},{4,5},{5,4},{6,7},{7,6},{8,9},{9,8},{10,11... | collective-permute-start | bytes 2359304 | tf_op jit(solution)/shard_map/ppermute | solution.py:1253
  28.0 10.3 %collective-permute-start.8 = (bf16[208,768]{1,0:T(8,128)(2,1)S(1)}, bf16[208,768]{1,0:T(8,128)(2,1)S(1)}, u32[]{:S(2)}, u32[]{:S(2)}) collective-permute-start(bf16[208,768]{1,0:T(8,128)(2,1)S(1)} %pack_feed.1.refs_0_), channel_id=1, source_target_pairs={{0,8},{8,16},{16,24},{24,28},{28,20},{20,12},{12,4},{4,0},{1,9},{9... | collective-permute-start | bytes 958472 | tf_op jit(solution)/shard_map/ppermute | solution.py:1277
  29.5 9.7 %collective-permute-start.9 = (bf16[208,768]{1,0:T(8,128)(2,1)S(1)}, bf16[208,768]{1,0:T(8,128)(2,1)S(1)}, u32[]{:S(2)}, u32[]{:S(2)}) collective-permute-start(bf16[208,768]{1,0:T(8,128)(2,1)S(1)} %pack_feed.1.refs_0_), channel_id=1, source_target_pairs={{8,0},{16,8},{24,16},{28,24},{20,28},{12,20},{4,12},{0,4},{9,1},{1... | collective-permute-start | bytes 958472 | tf_op jit(solution)/shard_map/ppermute | solution.py:1277
  30.0 11.8 %collective-permute-start.10 = (bf16[112,768]{1,0:T(8,128)(2,1)}, bf16[112,768]{1,0:T(8,128)(2,1)S(1)}, u32[]{:S(2)}, u32[]{:S(2)}) collective-permute-start(bf16[112,768]{1,0:T(8,128)(2,1)} %collective-permute-done.3.refs_5_), channel_id=1, source_target_pairs={{0,8},{8,16},{16,24},{24,28},{28,20},{20,12},{12,4},{4,0},{1,9},{9... | collective-permute-start | bytes 516104 | tf_op jit(solution)/shard_map/ppermute | solution.py:1277
  31.6 19.4 %collective-permute-start.11 = (bf16[512,768]{1,0:T(8,128)(2,1)}, bf16[512,768]{1,0:T(8,128)(2,1)}, u32[]{:S(2)}, u32[]{:S(2)}) collective-permute-start(bf16[512,768]{1,0:T(8,128)(2,1)} %dynamic-slice_bitcast_fusion), channel_id=1, source_target_pairs={{0,2},{2,0},{1,3},{3,1},{4,6},{6,4},{5,7},{7,5},{8,10},{10,8},{9,1... | collective-permute-start | bytes 2359304 | tf_op jit(solution)/shard_map/ppermute | solution.py:1253
  39.2 11.8 %collective-permute-start.12 = (bf16[208,768]{1,0:T(8,128)(2,1)S(1)}, bf16[208,768]{1,0:T(8,128)(2,1)S(1)}, u32[]{:S(2)}, u32[]{:S(2)}) collective-permute-start(bf16[208,768]{1,0:T(8,128)(2,1)S(1)} %collective-permute-done.8.refs_1_), channel_id=1, source_target_pairs={{0,8},{8,16},{16,24},{24,28},{28,20},{20,12},{12,4},{4,0},{1,9},{9... | collective-permute-start | bytes 958472 | tf_op jit(solution)/shard_map/ppermute | solution.py:1277
  40.8 10.2 %collective-permute-start.13 = (bf16[208,768]{1,0:T(8,128)(2,1)S(1)}, bf16[208,768]{1,0:T(8,128)(2,1)S(1)}, u32[]{:S(2)}, u32[]{:S(2)}) collective-permute-start(bf16[208,768]{1,0:T(8,128)(2,1)S(1)} %collective-permute-done.9.refs_2_), channel_id=1, source_target_pairs={{8,0},{16,8},{24,16},{28,24},{20,28},{12,20},{4,12},{0,4},{9,1},{1... | collective-permute-start | bytes 958472 | tf_op jit(solution)/shard_map/ppermute | solution.py:1277
  51.0 22.5 %collective-permute-start.14 = (bf16[512,768]{1,0:T(8,128)(2,1)}, bf16[512,768]{1,0:T(8,128)(2,1)S(1)}, u32[]{:S(2)}, u32[]{:S(2)}) collective-permute-start(bf16[512,768]{1,0:T(8,128)(2,1)} %collective-permute-done.11), channel_id=1, source_target_pairs={{0,1},{1,0},{2,3},{3,2},{4,5},{5,4},{6,7},{7,6},{8,9},{9,8},{10,11... | collective-permute-start | bytes 2359304 | tf_op jit(solution)/shard_map/ppermute | solution.py:1253
  51.2 22.3 %collective-permute-start.15 = (bf16[208,768]{1,0:T(8,128)(2,1)S(1)}, bf16[208,768]{1,0:T(8,128)(2,1)S(1)}, u32[]{:S(2)}, u32[]{:S(2)}) collective-permute-start(bf16[208,768]{1,0:T(8,128)(2,1)S(1)} %collective-permute-done.12.refs_3_), channel_id=1, source_target_pairs={{0,8},{8,16},{16,24},{24,28},{28,20},{20,12},{12,4},{4,0},{1,9},{9... | collective-permute-start | bytes 958472 | tf_op jit(solution)/shard_map/ppermute | solution.py:1277
  52.8 20.7 %collective-permute-start.16 = (bf16[208,768]{1,0:T(8,128)(2,1)S(1)}, bf16[208,768]{1,0:T(8,128)(2,1)S(1)}, u32[]{:S(2)}, u32[]{:S(2)}) collective-permute-start(bf16[208,768]{1,0:T(8,128)(2,1)S(1)} %collective-permute-done.13.refs_4_), channel_id=1, source_target_pairs={{8,0},{16,8},{24,16},{28,24},{20,28},{12,20},{4,12},{0,4},{9,1},{1... | collective-permute-start | bytes 958472 | tf_op jit(solution)/shard_map/ppermute | solution.py:1277
  73.5 10.5 %collective-permute-start.17 = (bf16[208,768]{1,0:T(8,128)(2,1)S(1)}, bf16[208,768]{1,0:T(8,128)(2,1)S(1)}, u32[]{:S(2)}, u32[]{:S(2)}) collective-permute-start(bf16[208,768]{1,0:T(8,128)(2,1)S(1)} %collective-permute-done.15.refs_5_), channel_id=1, source_target_pairs={{0,8},{8,16},{16,24},{24,28},{28,20},{20,12},{12,4},{4,0},{1,9},{9... | collective-permute-start | bytes 958472 | tf_op jit(solution)/shard_map/ppermute | solution.py:1277
  108.2 2.9 %collective-permute-start.18 = (bf16[512,768]{1,0:T(8,128)(2,1)}, bf16[512,768]{1,0:T(8,128)(2,1)S(1)}, u32[]{:S(2)}, u32[]{:S(2)}) collective-permute-start(bf16[512,768]{1,0:T(8,128)(2,1)} %get-tuple-element.125), channel_id=1, source_target_pairs={{0,1},{1,0},{2,3},{3,2},{4,5},{5,4},{6,7},{7,6},{8,9},{9,8},{10,11... | collective-permute-start | bytes 2359304 | tf_op jit(solution)/shard_map/ppermute | solution.py:1253
  108.3 4.7 %collective-permute-start.19 = (bf16[512,768]{1,0:T(8,128)(2,1)S(1)}, bf16[512,768]{1,0:T(8,128)(2,1)S(1)}, u32[]{:S(2)}, u32[]{:S(2)}) collective-permute-start(bf16[512,768]{1,0:T(8,128)(2,1)S(1)} %get-tuple-element.126), channel_id=1, source_target_pairs={{0,1},{1,0},{2,3},{3,2},{4,5},{5,4},{6,7},{7,6},{8,9},{9,8},{10,11... | collective-permute-start | bytes 2359304 | tf_op jit(solution)/shard_map/ppermute | solution.py:1253
  108.8 39.1 %collective-permute-start.20 = (bf16[4,128,768]{2,1,0:T(8,128)(2,1)}, bf16[4,128,768]{2,1,0:T(8,128)(2,1)S(1)}, u32[]{:S(2)}, u32[]{:S(2)}) collective-permute-start(bf16[4,128,768]{2,1,0:T(8,128)(2,1)} %get-tuple-element.130), channel_id=1, source_target_pairs={{0,4},{4,0},{8,12},{12,8},{16,20},{20,16},{24,28},{28,24},{1,5},{5... | collective-permute-start | bytes 2359304 | tf_op jit(solution)/shard_map/ppermute | solution.py:1300
  112.4 35.5 %collective-permute-start.24 = (bf16[512,768]{1,0:T(8,128)(2,1)S(1)}, bf16[512,768]{1,0:T(8,128)(2,1)S(1)}, u32[]{:S(2)}, u32[]{:S(2)}) collective-permute-start(bf16[512,768]{1,0:T(8,128)(2,1)S(1)} %add_convert_fusion.3), channel_id=1, source_target_pairs={{0,2},{2,0},{1,3},{3,1},{4,6},{6,4},{5,7},{7,5},{8,10},{10,8},{9,1... | collective-permute-start | bytes 2359304 | tf_op jit(solution)/shard_map/ppermute | solution.py:1253
  113.0 34.9 %collective-permute-start.21 = (bf16[2,112,768]{2,1,0:T(8,128)(2,1)S(1)}, bf16[2,112,768]{2,1,0:T(8,128)(2,1)S(1)}, u32[]{:S(2)}, u32[]{:S(2)}) collective-permute-start(bf16[2,112,768]{2,1,0:T(8,128)(2,1)S(1)} %get-tuple-element.131), channel_id=1, source_target_pairs={{0,8},{4,12},{8,16},{12,20},{16,24},{20,28},{24,0},{28,4},{1,9},{5... | collective-permute-start | bytes 1032200 | tf_op jit(solution)/shard_map/ppermute | solution.py:1288
  113.0 34.9 %collective-permute-start.22 = (bf16[2,112,768]{2,1,0:T(8,128)(2,1)S(1)}, bf16[2,112,768]{2,1,0:T(8,128)(2,1)S(1)}, u32[]{:S(2)}, u32[]{:S(2)}) collective-permute-start(bf16[2,112,768]{2,1,0:T(8,128)(2,1)S(1)} %get-tuple-element.132), channel_id=1, source_target_pairs={{0,16},{4,20},{8,24},{12,28},{16,0},{20,4},{24,8},{28,12},{1,17},{... | collective-permute-start | bytes 1032200 | tf_op jit(solution)/shard_map/ppermute | solution.py:1288
  113.0 34.9 %collective-permute-start.23 = (bf16[2,112,768]{2,1,0:T(8,128)(2,1)S(1)}, bf16[2,112,768]{2,1,0:T(8,128)(2,1)S(1)}, u32[]{:S(2)}, u32[]{:S(2)}) collective-permute-start(bf16[2,112,768]{2,1,0:T(8,128)(2,1)S(1)} %get-tuple-element.133), channel_id=1, source_target_pairs={{0,24},{4,28},{8,0},{12,4},{16,8},{20,12},{24,16},{28,20},{1,25},{... | collective-permute-start | bytes 1032200 | tf_op jit(solution)/shard_map/ppermute | solution.py:1288
  116.9 31.9 %copy-start.4 = (bf16[4,128,768]{2,1,0:T(8,128)(2,1)S(1)}, bf16[4,128,768]{2,1,0:T(8,128)(2,1)}, u32[]{:S(2)}) copy-start(bf16[4,128,768]{2,1,0:T(8,128)(2,1)} %get-tuple-element.135.kept) | copy-start | bytes 2359300
  149.7 16.2 %collective-permute-start.25 = (bf16[128,768]{1,0:T(8,128)(2,1)S(1)}, bf16[128,768]{1,0:T(8,128)(2,1)S(1)}, u32[]{:S(2)}, u32[]{:S(2)}) collective-permute-start(bf16[128,768]{1,0:T(8,128)(2,1)S(1)} %get-tuple-element.142), channel_id=1, source_target_pairs={{0,8},{4,12},{8,16},{12,20},{16,24},{20,28},{24,0},{28,4},{1,9},{5... | collective-permute-start | bytes 589832 | tf_op jit(solution)/shard_map/ppermute | solution.py:1288
  149.8 16.5 %collective-permute-start.26 = (bf16[128,768]{1,0:T(8,128)(2,1)S(1)}, bf16[128,768]{1,0:T(8,128)(2,1)S(1)}, u32[]{:S(2)}, u32[]{:S(2)}) collective-permute-start(bf16[128,768]{1,0:T(8,128)(2,1)S(1)} %get-tuple-element.143), channel_id=1, source_target_pairs={{0,16},{4,20},{8,24},{12,28},{16,0},{20,4},{24,8},{28,12},{1,17},{... | collective-permute-start | bytes 589832 | tf_op jit(solution)/shard_map/ppermute | solution.py:1288
  149.9 16.4 %collective-permute-start.27 = (bf16[128,768]{1,0:T(8,128)(2,1)S(1)}, bf16[128,768]{1,0:T(8,128)(2,1)S(1)}, u32[]{:S(2)}, u32[]{:S(2)}) collective-permute-start(bf16[128,768]{1,0:T(8,128)(2,1)S(1)} %get-tuple-element.144), channel_id=1, source_target_pairs={{0,24},{4,28},{8,0},{12,4},{16,8},{20,12},{24,16},{28,20},{1,25},{... | collective-permute-start | bytes 589832 | tf_op jit(solution)/shard_map/ppermute | solution.py:1288
  153.6 12.3 %collective-permute-start.28 = (bf16[112,768]{1,0:T(8,128)(2,1)S(1)}, bf16[112,768]{1,0:T(8,128)(2,1)S(1)}, u32[]{:S(2)}, u32[]{:S(2)}) collective-permute-start(bf16[112,768]{1,0:T(8,128)(2,1)S(1)} %get-tuple-element.146), channel_id=1, source_target_pairs={{0,4},{4,0},{8,12},{12,8},{16,20},{20,16},{24,28},{28,24},{1,5},{5... | collective-permute-start | bytes 516104 | tf_op jit(solution)/shard_map/ppermute | solution.py:1300
  166.3 2.3 %collective-permute-start.29 = (bf16[512,768]{1,0:T(8,128)(2,1)S(1)}, bf16[512,768]{1,0:T(8,128)(2,1)S(1)}, u32[]{:S(2)}, u32[]{:S(2)}) collective-permute-start(bf16[512,768]{1,0:T(8,128)(2,1)S(1)} %get-tuple-element.156), channel_id=1, source_target_pairs={{0,1},{1,0},{2,3},{3,2},{4,5},{5,4},{6,7},{7,6},{8,9},{9,8},{10,11... | collective-permute-start | bytes 2359304 | tf_op jit(solution)/shard_map/ppermute | solution.py:1253
  169.2 4.2 %collective-permute-start.30 = (bf16[512,768]{1,0:T(8,128)(2,1)S(1)}, bf16[512,768]{1,0:T(8,128)(2,1)S(1)}, u32[]{:S(2)}, u32[]{:S(2)}) collective-permute-start(bf16[512,768]{1,0:T(8,128)(2,1)S(1)} %add_convert_fusion.1.mine), channel_id=1, source_target_pairs={{0,1},{1,0},{2,3},{3,2},{4,5},{5,4},{6,7},{7,6},{8,9},{9,8},{10,11... | collective-permute-start | bytes 2359304 | tf_op jit(solution)/shard_map/ppermute | solution.py:1253
  169.4 19.8 %collective-permute-start.32 = (bf16[512,768]{1,0:T(8,128)(2,1)S(1)}, bf16[512,768]{1,0:T(8,128)(2,1)S(1)}, u32[]{:S(2)}, u32[]{:S(2)}) collective-permute-start(bf16[512,768]{1,0:T(8,128)(2,1)S(1)} %add_convert_fusion.2), channel_id=1, source_target_pairs={{0,2},{2,0},{1,3},{3,1},{4,6},{6,4},{5,7},{7,5},{8,10},{10,8},{9,1... | collective-permute-start | bytes 2359304 | tf_op jit(solution)/shard_map/ppermute | solution.py:1253
  170.9 19.8 %collective-permute-start.31 = (bf16[512,768]{1,0:T(8,128)(2,1)S(1)}, bf16[512,768]{1,0:T(8,128)(2,1)S(1)}, u32[]{:S(2)}, u32[]{:S(2)}) collective-permute-start(bf16[512,768]{1,0:T(8,128)(2,1)S(1)} %get-tuple-element.160), channel_id=1, source_target_pairs={{0,1},{1,0},{2,3},{3,2},{4,5},{5,4},{6,7},{7,6},{8,9},{9,8},{10,11... | collective-permute-start | bytes 2359304 | tf_op jit(solution)/shard_map/ppermute | solution.py:1253
  171.0 15.3 %collective-permute-start.33 = (bf16[4,112,640]{2,1,0:T(8,128)(2,1)S(1)}, bf16[4,112,640]{2,1,0:T(8,128)(2,1)S(1)}, u32[]{:S(2)}, u32[]{:S(2)}) collective-permute-start(bf16[4,112,640]{2,1,0:T(8,128)(2,1)S(1)} %get-tuple-element.162), channel_id=1, source_target_pairs={{0,4},{4,0},{8,12},{12,8},{16,20},{20,16},{24,28},{28,24},{1,5},{5... | collective-permute-start | bytes 1720328 | tf_op jit(solution)/shard_map/ppermute | solution.py:1300
  189.2 10.2 %collective-permute-start.38 = (bf16[240,768]{1,0:T(8,128)(2,1)S(1)}, bf16[240,768]{1,0:T(8,128)(2,1)}, u32[]{:S(2)}, u32[]{:S(2)}) collective-permute-start(bf16[240,768]{1,0:T(8,128)(2,1)S(1)} %join.1.own), channel_id=1, source_target_pairs={{0,2},{2,0},{1,3},{3,1},{4,6},{6,4},{5,7},{7,5},{8,10},{10,8},{9,1... | collective-permute-start | bytes 1105928 | tf_op jit(solution)/shard_map/ppermute | solution.py:1253
  192.0 14.4 %collective-permute-start.37 = (bf16[512,768]{1,0:T(8,128)(2,1)}, bf16[512,768]{1,0:T(8,128)(2,1)}, u32[]{:S(2)}, u32[]{:S(2)}) collective-permute-start(bf16[512,768]{1,0:T(8,128)(2,1)} %add_convert_fusion.mine), channel_id=1, source_target_pairs={{0,1},{1,0},{2,3},{3,2},{4,5},{5,4},{6,7},{7,6},{8,9},{9,8},{10,11... | collective-permute-start | bytes 2359304 | tf_op jit(solution)/shard_map/ppermute | solution.py:1253
  192.0 11.4 %collective-permute-start.34 = (bf16[112,640]{1,0:T(8,128)(2,1)}, bf16[112,640]{1,0:T(8,128)(2,1)S(1)}, u32[]{:S(2)}, u32[]{:S(2)}) collective-permute-start(bf16[112,640]{1,0:T(8,128)(2,1)} %copy-done.27), channel_id=1, source_target_pairs={{0,8},{4,12},{8,16},{12,20},{16,24},{20,28},{24,0},{28,4},{1,9},{5... | collective-permute-start | bytes 430088 | tf_op jit(solution)/shard_map/ppermute | solution.py:1288
  195.8 10.6 %collective-permute-start.35 = (bf16[112,640]{1,0:T(8,128)(2,1)}, bf16[112,640]{1,0:T(8,128)(2,1)S(1)}, u32[]{:S(2)}, u32[]{:S(2)}) collective-permute-start(bf16[112,640]{1,0:T(8,128)(2,1)} %copy-done.26), channel_id=1, source_target_pairs={{0,16},{4,20},{8,24},{12,28},{16,0},{20,4},{24,8},{28,12},{1,17},{... | collective-permute-start | bytes 430088 | tf_op jit(solution)/shard_map/ppermute | solution.py:1288
  195.8 10.6 %collective-permute-start.36 = (bf16[112,640]{1,0:T(8,128)(2,1)}, bf16[112,640]{1,0:T(8,128)(2,1)S(1)}, u32[]{:S(2)}, u32[]{:S(2)}) collective-permute-start(bf16[112,640]{1,0:T(8,128)(2,1)} %copy-done.25), channel_id=1, source_target_pairs={{0,24},{4,28},{8,0},{12,4},{16,8},{20,12},{24,16},{28,20},{1,25},{... | collective-permute-start | bytes 430088 | tf_op jit(solution)/shard_map/ppermute | solution.py:1288
  202.2 1.2 collective-permute-start.40
  207.4 6.2 %collective-permute-start.39 = (bf16[112,640]{1,0:T(8,128)(2,1)S(1)}, bf16[112,640]{1,0:T(8,128)(2,1)S(1)}, u32[]{:S(2)}, u32[]{:S(2)}) collective-permute-start(bf16[112,640]{1,0:T(8,128)(2,1)S(1)} %add_convert_fusion.4.own), channel_id=1, source_target_pairs={{0,2},{2,0},{1,3},{3,1},{4,6},{6,4},{5,7},{7,5},{8,10},{10,8},{9,1... | collective-permute-start | bytes 430088 | tf_op jit(solution)/shard_map/ppermute | solution.py:1253
  215.2 1.1 collective-permute-start.41
  (29 other events, 211.5 us)
